TPU v7x, 32 devices: a whole 2x2x4 slice. The times are simulated.
32 devices in a mesh: seq: 8 (over z, x), head: 4 (over y, core).
Axes of the slice: x: 2, y: 2, z: 4, core: 2. Of those that a mesh axis runs over, the one named last changes fastest.
Arguments:
- queries: bfloat16 [2048, 24, 128], P('seq', 'head'), may hold values from -6 to 6
- key_vectors: bfloat16 [2048, 24, 128], P('seq', 'head'), may hold values from -6 to 6
- values: bfloat16 [2048, 24, 128], P('seq', 'head'), may hold values from -6 to 6
- out_grad: bfloat16 [2048, 24, 128], P('seq', 'head'), may hold values from -6 to 6
- ssm_input: bfloat16 [2048, 48, 128], P('seq', 'head'), may hold values from -6 to 6
- ssm_out_grad: bfloat16 [2048, 48, 128], P('seq', 'head'), may hold values from -1.5 to 1.5
- step_sizes: float32 [2048, 48], P('seq', 'head'), may hold values from 0 to 2, as said below
- decay_rates: float32 [48], P('head'), may hold values from -1 to 0, as said below
- skip_gains: float32 [48], P('head'), may hold values from 0.5 to 1.5
- bc_rows: bfloat16 [2048, 128], P('seq'), may hold values from -0.75 to 0.75
- saved_states: float32 [8, 48, 64, 128], P('seq', 'head'), may hold values from -6 to 6
Outputs:
- query_grad: bfloat16 [2048, 24, 128], P('seq', 'head')
- key_grad: bfloat16 [2048, 24, 128], P('seq', 'head')
- value_grad: bfloat16 [2048, 24, 128], P('seq', 'head')
- grad_inputs: bfloat16 [2048, 48, 128], P('seq', 'head')
- grad_steps: float32 [2048, 48], P('seq', 'head')
- grad_bc: float32 [2048, 128], P(('seq', 'head'))
- grad_decay: float32 [48], P('head')
- grad_skip: float32 [48], P('head')
Inputs may be any that keep to these rules, and one draw needn't show every extreme that they name: `step_sizes`: positive. `decay_rates`: negative.
All inputs are finite; a program needn't handle non-finite values.
Results may differ from a plain program's by a relative error of at most 0.0095.
Values may be sent and summed in bfloat16 or wider, within the bound.
No kernel may reach another device: no remote copies, remote signals or barrier semaphores. Data moves between devices by JAX's collectives and lax.ppermute only.
A program may use at most 192 MiB of HBM per device.

v0:
```python
import jax
import jax.numpy as jnp
from jax import lax
from jax.sharding import PartitionSpec as P

NSTATE = 64
WINDOW = 1024
GROUP = 256


TOP_PRECISION = lax.Precision.HIGHEST


def from_behind(value, axis, steps):
    count = lax.axis_size(axis)
    first, last = (max(0, -steps), min(count, count - steps))
    return lax.ppermute(value, axis, [(source, source + steps) for source in range(first, last)])


def carried_in(value, axis, join, neutral):
    count, mine = (lax.axis_size(axis), lax.axis_index(axis))
    pieces = jax.tree.map(lambda part: lax.all_gather(part, axis), value)
    pieces = jax.tree.map(lambda part: part[::-1], pieces)
    mine = count - 1 - mine
    running = jax.tree.map(
        lambda part, zero: jnp.full_like(part, 0) + jnp.asarray(zero, part.dtype), value, neutral
    )

    def step(position, running):
        longer = join(running, jax.tree.map(lambda part: part[position], pieces))
        return jax.tree.map(lambda new, old: jnp.where(position < mine, new, old), longer, running)

    return lax.fori_loop(0, count - 1, step, running)


def triangles(length):
    row_ids = lax.broadcasted_iota(jnp.int32, (length, length), 0)
    col_ids = lax.broadcasted_iota(jnp.int32, (length, length), 1)
    in_lower = col_ids <= row_ids
    return (in_lower, in_lower.astype(jnp.float32), (col_ids < row_ids).astype(jnp.float32))


def group_summary(out_part, steps_part, c_rows, decay_rates, inclusive):
    log_decay = (steps_part * decay_rates[None, :]).T
    cumulative = jnp.dot(log_decay, inclusive.T, precision=TOP_PRECISION)
    weights = jnp.exp(cumulative).T
    scaled = out_part.astype(jnp.float32) * weights[:, :, None]
    carried = jnp.einsum("qhp,qn->hnp", scaled, c_rows.astype(jnp.float32), precision=TOP_PRECISION)
    return (cumulative, jnp.exp(cumulative[:, -1]), carried)


def join_adjoint(upper_side, lower_side):
    return (
        upper_side[0] * lower_side[0],
        lower_side[1] + lower_side[0][:, None, None] * upper_side[1],
    )


def group_grads(
    inputs_part,
    out_part,
    steps_part,
    b_rows,
    c_rows,
    decay_rates,
    skip_gains,
    start_state,
    incoming,
    cumulative,
    tables,
):
    in_lower, inclusive, strict = tables
    last_sum = cumulative[:, -1]
    spread = cumulative[:, :, None] - cumulative[:, None, :]
    lower_decay = jnp.where(in_lower[None], jnp.exp(jnp.where(in_lower[None], spread, 0.0)), 0.0)
    inner_cb = jnp.dot(c_rows, b_rows.T, preferred_element_type=jnp.float32)
    grad_out = out_part.astype(jnp.float32)
    input_float = inputs_part.astype(jnp.float32)
    driven = steps_part[:, :, None] * input_float
    b_float = b_rows.astype(jnp.float32)
    c_float = c_rows.astype(jnp.float32)
    weights = jnp.exp(cumulative).T
    tail_decay = jnp.exp(last_sum[:, None] - cumulative).T
    cross_dy = (
        jnp.einsum("thp,shp->hts", out_part, inputs_part, preferred_element_type=jnp.float32)
        * steps_part.T[:, None, :]
    )
    weighted = lower_decay * cross_dy
    from_start = jnp.einsum("thp,hnp->thn", grad_out, start_state, precision=TOP_PRECISION)
    to_incoming = jnp.einsum("shp,hnp->shn", driven, incoming, precision=TOP_PRECISION)
    grad_c = jnp.sum(weights[:, :, None] * from_start, axis=1) + jnp.einsum(
        "hts,sn->tn", weighted, b_float, precision=TOP_PRECISION
    )
    mixing = lower_decay * inner_cb[None]
    grad_driven = jnp.einsum("hts,thp->shp", mixing, grad_out, precision=TOP_PRECISION)
    grad_driven = grad_driven + tail_decay[:, :, None] * jnp.einsum(
        "sn,hnp->shp", b_float, incoming, precision=TOP_PRECISION
    )
    grad_b = jnp.einsum("hts,tn->sn", weighted, c_float, precision=TOP_PRECISION) + jnp.sum(
        tail_decay[:, :, None] * to_incoming, axis=1
    )
    paired = weighted * inner_cb[None]
    inside = jnp.dot(jnp.sum(paired, axis=1), inclusive.T, precision=TOP_PRECISION) - jnp.dot(
        jnp.sum(paired, axis=2), strict.T, precision=TOP_PRECISION
    )
    early_terms = jnp.sum(from_start * c_float[:, None, :], axis=2) * weights
    after_part = jnp.dot(early_terms.T, inclusive, precision=TOP_PRECISION)
    late_terms = jnp.sum(to_incoming * b_float[:, None, :], axis=2) * tail_decay
    before = jnp.dot(late_terms.T, inclusive.T, precision=TOP_PRECISION)
    whole_term = jnp.exp(last_sum) * jnp.sum(incoming * start_state, axis=(1, 2))
    grad_log = (
        inside + after_part + before + whole_term[:, None] - jnp.sum(driven * grad_driven, axis=2).T
    )
    grad_steps = jnp.sum(input_float * grad_driven, axis=2) + decay_rates[None, :] * grad_log.T
    grad_inputs = (
        steps_part[:, :, None] * grad_driven + skip_gains[None, :, None] * grad_out
    ).astype(jnp.bfloat16)
    grad_decay = jnp.sum(steps_part.T * grad_log, axis=1)
    grad_skip = jnp.sum(grad_out * input_float, axis=(0, 2))
    return (
        grad_inputs,
        grad_steps,
        jnp.concatenate([grad_b, grad_c], axis=1),
        grad_decay,
        grad_skip,
    )


def window_pass(queries, keys_ext, values_ext, out_grad, first_key):
    count = queries.shape[0]
    extent = keys_ext.shape[0]
    scaling_factor = queries.shape[2] ** (-0.5)
    row_ids = lax.broadcasted_iota(jnp.int32, (count, extent), 0)
    col_ids = lax.broadcasted_iota(jnp.int32, (count, extent), 1)
    usable = (col_ids > row_ids) & (col_ids <= WINDOW + row_ids) & (col_ids >= first_key)
    query_parts, total_parts, delta_parts, key_parts, value_parts = ([], [], [], [], [])
    for head_id in range(queries.shape[1]):
        q_head = queries[:, head_id]
        k_head = keys_ext[:, head_id]
        v_head = values_ext[:, head_id]
        g_head = out_grad[:, head_id]
        score_matrix = (
            jnp.einsum("id,ed->ie", q_head, k_head, preferred_element_type=jnp.float32)
            * scaling_factor
        )
        score_matrix = jnp.where(usable, score_matrix, -jnp.inf)
        row_max = jnp.max(score_matrix, axis=1, keepdims=True)
        log_total = row_max[:, 0] + jnp.log(jnp.sum(jnp.exp(score_matrix - row_max), axis=1))
        probs = jnp.exp(score_matrix - log_total[:, None])
        probs_gradient = jnp.einsum("id,ed->ie", g_head, v_head, preferred_element_type=jnp.float32)
        delta_row = jnp.sum(probs * probs_gradient, axis=1)
        scores_gradient = (probs * (probs_gradient - delta_row[:, None]) * scaling_factor).astype(
            jnp.bfloat16
        )
        query_parts.append(jnp.dot(scores_gradient, k_head, preferred_element_type=jnp.float32))
        total_parts.append(log_total)
        delta_parts.append(delta_row)
    query_grad = jnp.stack(query_parts, axis=1).astype(jnp.bfloat16)
    totals = jnp.stack(total_parts, axis=1)
    deltas = jnp.stack(delta_parts, axis=1)
    return (query_grad, totals, deltas, None, None)


def key_pass(query_ext, grad_ext, total_ext, delta_ext, key_vectors, values, last_query):
    extent = query_ext.shape[0]
    count = key_vectors.shape[0]
    scaling_factor = query_ext.shape[2] ** (-0.5)
    row_ids = lax.broadcasted_iota(jnp.int32, (extent, count), 0)
    col_ids = lax.broadcasted_iota(jnp.int32, (extent, count), 1)
    usable = (row_ids >= col_ids) & (row_ids < col_ids + WINDOW) & (row_ids < last_query)
    key_parts, value_parts = ([], [])
    for head_id in range(key_vectors.shape[1]):
        q_head = query_ext[:, head_id]
        g_head = grad_ext[:, head_id]
        score_matrix = (
            jnp.einsum(
                "gd,ed->ge", q_head, key_vectors[:, head_id], preferred_element_type=jnp.float32
            )
            * scaling_factor
        )
        score_matrix = jnp.where(usable, score_matrix, -jnp.inf)
        probs = jnp.exp(score_matrix - total_ext[:, head_id][:, None])
        probs_reduced = probs.astype(jnp.bfloat16)
        probs_gradient = jnp.einsum(
            "gd,ed->ge", g_head, values[:, head_id], preferred_element_type=jnp.float32
        )
        scores_gradient = (
            probs * (probs_gradient - delta_ext[:, head_id][:, None]) * scaling_factor
        ).astype(jnp.bfloat16)
        key_parts.append(
            jnp.einsum("ge,gd->ed", scores_gradient, q_head, preferred_element_type=jnp.float32)
        )
        value_parts.append(
            jnp.einsum("ge,gd->ed", probs_reduced, g_head, preferred_element_type=jnp.float32)
        )
    return (jnp.stack(key_parts, axis=1), jnp.stack(value_parts, axis=1))


def shards(
    queries,
    key_vectors,
    values,
    out_grad,
    ssm_input,
    ssm_out_grad,
    step_sizes,
    decay_rates,
    skip_gains,
    bc_rows,
    saved_states,
):
    count = queries.shape[0]
    reach = WINDOW // count
    shard_id = lax.axis_index("seq")
    shard_total = lax.axis_size("seq")
    first_key = WINDOW - shard_id * count
    own_pair = (key_vectors, values)
    earlier = [
        from_behind((own_pair[0], own_pair[1]), "seq", offset) for offset in range(reach, 0, -1)
    ]
    keys_ext = jnp.concatenate([received[0] for received in earlier] + [key_vectors], axis=0)
    values_ext = jnp.concatenate([received[1] for received in earlier] + [values], axis=0)
    tables = triangles(GROUP)
    pieces = count // GROUP
    block_id = 0
    begin = block_id * GROUP
    summaries = [
        group_summary(
            ssm_out_grad,
            step_sizes,
            bc_rows[begin : begin + GROUP, NSTATE:],
            decay_rates,
            tables[1],
        )
    ]
    combined = (summaries[-1][1], summaries[-1][2])
    heads_here = decay_rates.shape[0]
    identity = (
        jnp.ones((heads_here,), jnp.float32),
        jnp.zeros((heads_here, NSTATE, ssm_input.shape[2]), jnp.float32),
    )
    from_later = carried_in(combined, "seq", join_adjoint, identity)
    incoming = from_later[1]
    input_parts, step_parts, bc_parts = ([None] * pieces, [None] * pieces, [None] * pieces)
    decay_total = jnp.zeros((heads_here,), jnp.float32)
    block_id = 0
    begin = block_id * GROUP
    results = group_grads(
        ssm_input,
        ssm_out_grad,
        step_sizes,
        bc_rows[begin : begin + GROUP, :NSTATE],
        bc_rows[begin : begin + GROUP, NSTATE:],
        decay_rates,
        skip_gains,
        saved_states[block_id],
        incoming,
        summaries[block_id][0],
        tables,
    )
    input_parts[block_id], step_parts[block_id], bc_parts[block_id] = (
        results[0],
        results[1],
        results[2],
    )
    decay_total = decay_total + results[3]
    skip_total = results[4]
    grad_inputs = input_parts[0]
    grad_steps = step_parts[0]
    grad_bc = lax.psum_scatter(
        bc_parts[0].astype(jnp.bfloat16), "head", scatter_dimension=0, tiled=True
    ).astype(jnp.float32)
    grad_decay, grad_skip = lax.psum((decay_total, skip_total), "seq")
    query_grad, totals, deltas, unused_keys, unused_values = window_pass(
        queries, keys_ext, values_ext, out_grad, first_key
    )
    own_rows = (queries, out_grad)
    own_stats = (totals, deltas)
    later_rows = [
        from_behind((own_rows[0], own_rows[1]), "seq", -offset) for offset in range(1, reach + 1)
    ]
    later_stats = [
        from_behind((own_stats[0], own_stats[1]), "seq", -offset) for offset in range(1, reach + 1)
    ]
    query_ext = jnp.concatenate([queries] + [received[0] for received in later_rows], axis=0)
    grad_ext = jnp.concatenate([out_grad] + [received[1] for received in later_rows], axis=0)
    total_ext = jnp.concatenate([totals] + [received[0] for received in later_stats], axis=0)
    delta_ext = jnp.concatenate([deltas] + [received[1] for received in later_stats], axis=0)
    last_query = (shard_total - shard_id) * count
    key_total, value_total = key_pass(
        query_ext, grad_ext, total_ext, delta_ext, key_vectors, values, last_query
    )
    key_grad = key_total.astype(jnp.bfloat16)
    value_grad = value_total.astype(jnp.bfloat16)
    return (
        query_grad,
        key_grad,
        value_grad,
        grad_inputs,
        grad_steps,
        grad_bc,
        grad_decay,
        grad_skip,
    )


def solution(mesh):
    placed = (
        P("seq", "head", None),
        P("seq", "head", None),
        P("seq", "head", None),
        P("seq", "head", None),
        P("seq", "head", None),
        P("seq", "head", None),
        P("seq", "head"),
        P("head"),
        P("head"),
        P("seq", None),
        P("seq", "head", None, None),
    )
    return jax.shard_map(
        shards,
        mesh=mesh,
        in_specs=placed,
        out_specs=(
            P("seq", "head", None),
            P("seq", "head", None),
            P("seq", "head", None),
            P("seq", "head", None),
            P("seq", "head"),
            P(("seq", "head"), None),
            P("head"),
            P("head"),
        ),
        check_vma=False,
    )
```

profile of v0, /device:TPU:0, one launch (start us, length us, event | category | flops | bytes accessed | tf_op | source)
XLA Modules:
  0.0 340.2 jit_solution(2345177765564600045)
XLA Ops:
  7.2 6.7 %collective-permute-start = (bf16[256,6,128]{2,0,1:T(8,128)(2,1)}, bf16[256,6,128]{2,0,1:T(8,128)(2,1)}, u32[]{:S(2)}, u32[]{:S(2)}) collective-permute-start(bf16[256,6,128]{2,0,1:T(8,128)(2,1)} %param.14), channel_id=1, source_target_pairs={{0,16},{4,20},{8,24},{12,28},{1,17},{5,21},{9,25},{13,29},{2,18},{... | collective-permute-start | bytes 1179656 | tf_op jit(solution)/shard_map/ppermute | solution.py:17
  14.0 5.2 %collective-permute-start.1 = (bf16[256,6,128]{2,0,1:T(8,128)(2,1)}, bf16[256,6,128]{2,0,1:T(8,128)(2,1)}, u32[]{:S(2)}, u32[]{:S(2)}) collective-permute-start(bf16[256,6,128]{2,0,1:T(8,128)(2,1)} %param.14), channel_id=1, source_target_pairs={{0,12},{4,16},{8,20},{12,24},{16,28},{1,13},{5,17},{9,21},{13,25},... | collective-permute-start | bytes 1179656 | tf_op jit(solution)/shard_map/ppermute | solution.py:17
  19.1 2.0 collective-permute-start.2
  21.2 3.1 collective-permute-start.3
  24.3 1.3 collective-permute-start.4
  25.6 1.4 copy.42
  27.3 1.8 fusion.76
  29.5 1.8 constant_dynamic-update-slice_fusion.14
  32.2 3.5 %fusion.1 = f32[12,256,128]{1,2,0:T(8,128)} fusion(bf16[256,12,128]{2,0,1:T(8,128)(2,1)S(1)} %copy-done.17, f32[256,256]{1,0:T(8,128)S(1)} %fusion.244, f32[12,256]{1,0:T(8,128)S(1)} %fusion.157, pred[256,256]{1,0:T(8,128)(4,1)S(1)} %iota_compare_fusion.5), kind=kOutput, calls=%fused_computation.4 | convolution fusion | flops 1211105280 | bytes 2699264 | tf_op jit(solution)/shard_map/hts,thp->shp/dot_general | solution.py:95
  35.7 2.4 multiply_reduce_fusion
  44.9 33.9 %all-reduce = f32[96]{0:T(128)S(1)} all-reduce(f32[96]{0:T(128)S(1)} %dynamic-update-slice), channel_id=3, replica_groups=mesh['seq'=8,'head'=4] {'seq'}, use_global_device_ids=true, to_apply=%add | all-reduce | flops 96 | bytes 768
  80.3 54.5 %collective-permute-start.5 = (bf16[256,6,128]{2,0,1:T(8,128)(2,1)}, bf16[256,6,128]{2,0,1:T(8,128)(2,1)S(1)}, u32[]{:S(2)}, u32[]{:S(2)}) collective-permute-start(bf16[256,6,128]{2,0,1:T(8,128)(2,1)} %param.15), channel_id=1, source_target_pairs={{0,12},{4,16},{8,20},{12,24},{16,28},{1,13},{5,17},{9,21},{13,25},... | collective-permute-start | bytes 1179656 | tf_op jit(solution)/shard_map/ppermute | solution.py:17
  135.8 3.5 %collective-permute-start.6 = (bf16[256,6,128]{2,0,1:T(8,128)(2,1)}, bf16[256,6,128]{2,0,1:T(8,128)(2,1)S(1)}, u32[]{:S(2)}, u32[]{:S(2)}) collective-permute-start(bf16[256,6,128]{2,0,1:T(8,128)(2,1)} %param.15), channel_id=1, source_target_pairs={{0,8},{4,12},{8,16},{12,20},{16,24},{20,28},{1,9},{5,13},{9,17},{1... | collective-permute-start | bytes 1179656 | tf_op jit(solution)/shard_map/ppermute | solution.py:17
  140.4 1.7 collective-permute-start.7
  143.2 1.3 collective-permute-start.8
  145.6 1.4 fusion.250
  147.0 1.4 fusion.251
  148.4 1.4 fusion.252
  149.8 1.4 fusion.253
  151.5 1.3 collective-permute-start.9
  152.9 1.3 fusion.254
  154.2 1.3 collective-permute-start.10
  155.6 1.3 collective-permute-start.11
  156.9 1.3 fusion.255
  158.3 1.5 collective-permute-start.16
  161.2 1.5 multiply_reduce_fusion.7
  162.7 1.4 multiply_reduce_fusion.6
  164.4 1.4 multiply_reduce_fusion.5
  166.1 1.4 multiply_reduce_fusion.4
  167.8 1.4 multiply_reduce_fusion.3
  169.5 2.9 multiply_reduce_fusion.2
  172.4 1.4 collective-permute-start.17
  173.9 1.8 constant_dynamic-update-slice_fusion.13
  175.7 1.3 collective-permute-start.18
  177.0 1.8 constant_dynamic-update-slice_fusion.12
  178.8 2.0 fusion.84
  180.8 1.3 collective-permute-start.19
  182.1 2.0 constant_dynamic-update-slice_fusion.11
  184.1 1.6 fusion.86
  185.7 33.9 %collective-permute-done.11 = bf16[256,6,128]{2,0,1:T(8,128)(2,1)} collective-permute-done((bf16[256,6,128]{2,0,1:T(8,128)(2,1)}, bf16[256,6,128]{2,0,1:T(8,128)(2,1)}, u32[]{:S(2)}, u32[]{:S(2)}) %collective-permute-start.11) | collective-permute-done | bytes 393248 | tf_op jit(solution)/shard_map/ppermute | solution.py:17
  219.6 1.3 collective-permute-start.12
  220.9 2.0 constant_dynamic-update-slice_fusion.10
  223.4 1.3 collective-permute-start.13
  226.3 1.3 collective-permute-start.14
  228.3 1.4 collective-permute-start.15
  230.3 19.2 %collective-permute-done.19 = bf16[256,6,128]{2,0,1:T(8,128)(2,1)S(1)} collective-permute-done((bf16[256,6,128]{2,0,1:T(8,128)(2,1)S(1)}, bf16[256,6,128]{2,0,1:T(8,128)(2,1)S(1)}, u32[]{:S(2)}, u32[]{:S(2)}) %collective-permute-start.19) | collective-permute-done | bytes 393248 | tf_op jit(solution)/shard_map/ppermute | solution.py:17
  249.6 1.3 collective-permute-start.20
  250.9 1.3 collective-permute-start.21
  252.3 1.3 collective-permute-start.22
  253.6 1.5 collective-permute-start.23
  255.2 1.3 collective-permute-done.21
  256.5 4.0 %collective-permute-done.22 = f32[256,6]{0,1:T(8,128)S(1)} collective-permute-done((f32[256,6]{0,1:T(8,128)S(1)}, f32[256,6]{0,1:T(8,128)S(1)}, u32[]{:S(2)}, u32[]{:S(2)}) %collective-permute-start.22) | collective-permute-done | bytes 6176 | tf_op jit(solution)/shard_map/ppermute | solution.py:17
  260.5 1.6 collective-permute-done.23
  270.8 2.4 fusion.108
  273.2 2.1 fusion.110
  275.3 2.1 fusion.112
  277.5 2.1 fusion.114
  279.7 2.2 fusion.116
  281.8 2.1 fusion.118
  284.7 2.1 rev.6
  286.8 14.6 %while.14 = (s32[]{:T(128)}, f32[12,64,128]{2,1,0:T(8,128)S(1)}, s32[]{:T(128)}, f32[8,12,64,128]{3,2,1,0:T(8,128)S(1)}, f32[8,12]{1,0:T(8,128)}, /*index=5*/s32[]{:T(128)}, s32[]{:T(128)}) while((s32[]{:T(128)}, f32[12,64,128]{2,1,0:T(8,128)S(1)}, s32[]{:T(128)}, f32[8,12,64,128]{3,2,1,0:T(8,128)S(1)}, f32[8,12]{1,0:T(8,128)}, ...), condition=%wide.region_19.20_spmd.clone, body=%wide.region_18.19_spmd.clone.sunk | while | flops 393220 | bytes 1179905 | solution.py:33
  303.1 2.4 multiply_reduce_fusion.9
  306.6 2.9 fusion.53
  310.6 20.1 %all-reduce.1 = (f32[12]{0:T(128)}, f32[12]{0:T(128)}) all-reduce(f32[12]{0:T(128)S(1)} %fusion.221, f32[12]{0:T(128)S(1)} %get-tuple-element.150), channel_id=1, replica_groups=mesh['seq'=8,'head'=4] {'seq'}, use_global_device_ids=true, to_apply=%region_32.33 | all-reduce | flops 24 | bytes 192 | tf_op jit(solution)/shard_map/psum | solution.py:273
  (233 shorter events, 49.5 us)
Async XLA Ops:
  7.2 19.8 %copy-start.40 = (f32[256,12]{0,1:T(8,128)S(1)}, f32[256,12]{0,1:T(8,128)}, u32[]{:S(2)}) copy-start(f32[256,12]{0,1:T(8,128)} %param.19) | copy-start | bytes 36868
  7.2 19.8 %copy-start.45 = (f32[12]{0:T(128)S(1)}, f32[12]{0:T(128)}, u32[]{:S(2)}) copy-start(f32[12]{0:T(128)} %param.20) | copy-start | bytes 148
  7.2 20.1 %copy-start.13 = (bf16[256,128]{1,0:T(8,128)(2,1)S(1)}, bf16[256,128]{1,0:T(8,128)(2,1)}, u32[]{:S(2)}) copy-start(bf16[256,128]{1,0:T(8,128)(2,1)} %param.22) | copy-start | bytes 196612
  7.2 276.8 %all-gather.4.cloned.1.call-start = ((), (), s32[]{:S(2)}) async-start(), calls=%async_computation.1 | async-start | bytes 3538944 | tf_op jit(solution)/shard_map/all_gather | solution.py:22
  7.2 73.0 %collective-permute-start = (bf16[256,6,128]{2,0,1:T(8,128)(2,1)}, bf16[256,6,128]{2,0,1:T(8,128)(2,1)}, u32[]{:S(2)}, u32[]{:S(2)}) collective-permute-start(bf16[256,6,128]{2,0,1:T(8,128)(2,1)} %param.14), channel_id=1, source_target_pairs={{0,16},{4,20},{8,24},{12,28},{1,17},{5,21},{9,25},{13,29},{2,18},{... | collective-permute-start | bytes 1179656 | tf_op jit(solution)/shard_map/ppermute | solution.py:17
  14.0 121.9 %collective-permute-start.1 = (bf16[256,6,128]{2,0,1:T(8,128)(2,1)}, bf16[256,6,128]{2,0,1:T(8,128)(2,1)}, u32[]{:S(2)}, u32[]{:S(2)}) collective-permute-start(bf16[256,6,128]{2,0,1:T(8,128)(2,1)} %param.14), channel_id=1, source_target_pairs={{0,12},{4,16},{8,20},{12,24},{16,28},{1,13},{5,17},{9,21},{13,25},... | collective-permute-start | bytes 1179656 | tf_op jit(solution)/shard_map/ppermute | solution.py:17
  19.1 121.3 %collective-permute-start.2 = (bf16[256,6,128]{2,0,1:T(8,128)(2,1)}, bf16[256,6,128]{2,0,1:T(8,128)(2,1)}, u32[]{:S(2)}, u32[]{:S(2)}) collective-permute-start(bf16[256,6,128]{2,0,1:T(8,128)(2,1)} %param.14), channel_id=1, source_target_pairs={{0,8},{4,12},{8,16},{12,20},{16,24},{20,28},{1,9},{5,13},{9,17},{1... | collective-permute-start | bytes 1179656 | tf_op jit(solution)/shard_map/ppermute | solution.py:17
  21.2 122.0 %collective-permute-start.3 = (bf16[256,6,128]{2,0,1:T(8,128)(2,1)}, bf16[256,6,128]{2,0,1:T(8,128)(2,1)}, u32[]{:S(2)}, u32[]{:S(2)}) collective-permute-start(bf16[256,6,128]{2,0,1:T(8,128)(2,1)} %param.14), channel_id=1, source_target_pairs={{0,4},{4,8},{8,12},{12,16},{16,20},{20,24},{24,28},{1,5},{5,9},{9,... | collective-permute-start | bytes 1179656 | tf_op jit(solution)/shard_map/ppermute | solution.py:17
  24.3 127.3 %collective-permute-start.4 = (bf16[256,6,128]{2,0,1:T(8,128)(2,1)}, bf16[256,6,128]{2,0,1:T(8,128)(2,1)S(1)}, u32[]{:S(2)}, u32[]{:S(2)}) collective-permute-start(bf16[256,6,128]{2,0,1:T(8,128)(2,1)} %param.15), channel_id=1, source_target_pairs={{0,16},{4,20},{8,24},{12,28},{1,17},{5,21},{9,25},{13,29},{2,18},{... | collective-permute-start | bytes 1179656 | tf_op jit(solution)/shard_map/ppermute | solution.py:17
  27.0 4.4 %copy-start.15 = (bf16[256,12,128]{0,2,1:T(8,128)(2,1)}, bf16[256,12,128]{0,2,1:T(8,128)(2,1)S(1)}, u32[]{:S(2)}) copy-start(bf16[256,12,128]{0,2,1:T(8,128)(2,1)S(1)} %copy.42) | copy-start | bytes 2359300
  27.3 4.1 %copy-start.24 = (bf16[256,6,128]{2,0,1:T(8,128)(2,1)S(1)}, bf16[256,6,128]{2,0,1:T(8,128)(2,1)}, u32[]{:S(2)}) copy-start(bf16[256,6,128]{2,0,1:T(8,128)(2,1)} %param.16) | copy-start | bytes 1179652
  29.1 3.1 copy-start.17
  29.1 302.7 %reduce-scatter.4.cloned.1.call-start = ((), (), s32[]{:S(2)}) async-start(), calls=%async_computation.2 | async-start | bytes 81920
  32.2 3.5 %copy-start.34 = (bf16[256,12,128]{2,0,1:T(8,128)(2,1)S(1)}, bf16[256,12,128]{2,0,1:T(8,128)(2,1)}, u32[]{:S(2)}) copy-start(bf16[256,12,128]{2,0,1:T(8,128)(2,1)} %param.17) | copy-start | bytes 2359300
  35.7 3.7 %copy-start.25 = (f32[1,12,64,128]{3,2,1,0:T(8,128)S(1)}, f32[1,12,64,128]{3,2,1,0:T(8,128)}, u32[]{:S(2)}) copy-start(f32[1,12,64,128]{3,2,1,0:T(8,128)} %param.23) | copy-start | bytes 1179652
  38.0 5.4 %copy-start.32 = (f32[256,256]{1,0:T(8,128)}, f32[256,256]{1,0:T(8,128)S(1)}, u32[]{:S(2)}) copy-start(f32[256,256]{1,0:T(8,128)S(1)} %get-tuple-element.147) | copy-start | bytes 786436
  40.3 3.1 copy-start.48
  80.3 73.9 %collective-permute-start.5 = (bf16[256,6,128]{2,0,1:T(8,128)(2,1)}, bf16[256,6,128]{2,0,1:T(8,128)(2,1)S(1)}, u32[]{:S(2)}, u32[]{:S(2)}) collective-permute-start(bf16[256,6,128]{2,0,1:T(8,128)(2,1)} %param.15), channel_id=1, source_target_pairs={{0,12},{4,16},{8,20},{12,24},{16,28},{1,13},{5,17},{9,21},{13,25},... | collective-permute-start | bytes 1179656 | tf_op jit(solution)/shard_map/ppermute | solution.py:17
  135.8 9.7 %copy-start.36 = (bf16[256,6,128]{2,0,1:T(8,128)(2,1)S(1)}, bf16[256,6,128]{2,0,1:T(8,128)(2,1)}, u32[]{:S(2)}) copy-start(bf16[256,6,128]{2,0,1:T(8,128)(2,1)} %param.14) | copy-start | bytes 1179652
  135.8 19.7 %collective-permute-start.6 = (bf16[256,6,128]{2,0,1:T(8,128)(2,1)}, bf16[256,6,128]{2,0,1:T(8,128)(2,1)S(1)}, u32[]{:S(2)}, u32[]{:S(2)}) collective-permute-start(bf16[256,6,128]{2,0,1:T(8,128)(2,1)} %param.15), channel_id=1, source_target_pairs={{0,8},{4,12},{8,16},{12,20},{16,24},{20,28},{1,9},{5,13},{9,17},{1... | collective-permute-start | bytes 1179656 | tf_op jit(solution)/shard_map/ppermute | solution.py:17
  140.4 17.9 %collective-permute-start.7 = (bf16[256,6,128]{2,0,1:T(8,128)(2,1)}, bf16[256,6,128]{2,0,1:T(8,128)(2,1)S(1)}, u32[]{:S(2)}, u32[]{:S(2)}) collective-permute-start(bf16[256,6,128]{2,0,1:T(8,128)(2,1)} %param.15), channel_id=1, source_target_pairs={{0,4},{4,8},{8,12},{12,16},{16,20},{20,24},{24,28},{1,5},{5,9},{9,... | collective-permute-start | bytes 1179656 | tf_op jit(solution)/shard_map/ppermute | solution.py:17
  143.2 29.3 %collective-permute-start.8 = (bf16[256,6,128]{2,0,1:T(8,128)(2,1)}, bf16[256,6,128]{2,0,1:T(8,128)(2,1)}, u32[]{:S(2)}, u32[]{:S(2)}) collective-permute-start(bf16[256,6,128]{2,0,1:T(8,128)(2,1)} %param.13), channel_id=1, source_target_pairs={{4,0},{8,4},{12,8},{16,12},{20,16},{24,20},{28,24},{5,1},{9,5},{13... | collective-permute-start | bytes 1179656 | tf_op jit(solution)/shard_map/ppermute | solution.py:17
  145.6 11.3 %copy-start.19 = (bf16[1280,6,128]{2,0,1:T(8,128)(2,1)}, bf16[1280,6,128]{2,0,1:T(8,128)(2,1)S(1)}, u32[]{:S(2)}) copy-start(bf16[1280,6,128]{2,0,1:T(8,128)(2,1)S(1)} %constant_dynamic-update-slice_fusion) | copy-start | bytes 5898244
  147.0 14.2 %copy-start.6 = (f32[256,1280]{0,1:T(8,128)}, f32[256,1280]{0,1:T(8,128)S(1)}, u32[]{:S(2)}) copy-start(f32[256,1280]{0,1:T(8,128)S(1)} %get-tuple-element.185) | copy-start | bytes 3932164
  148.4 14.3 %copy-start.4 = (f32[256,1280]{0,1:T(8,128)}, f32[256,1280]{0,1:T(8,128)S(1)}, u32[]{:S(2)}) copy-start(f32[256,1280]{0,1:T(8,128)S(1)} %get-tuple-element.189) | copy-start | bytes 3932164
  149.8 14.6 %copy-start.2 = (f32[256,1280]{0,1:T(8,128)}, f32[256,1280]{0,1:T(8,128)S(1)}, u32[]{:S(2)}) copy-start(f32[256,1280]{0,1:T(8,128)S(1)} %get-tuple-element.193) | copy-start | bytes 3932164
  151.5 24.2 %collective-permute-start.9 = (bf16[256,6,128]{2,0,1:T(8,128)(2,1)}, bf16[256,6,128]{2,0,1:T(8,128)(2,1)}, u32[]{:S(2)}, u32[]{:S(2)}) collective-permute-start(bf16[256,6,128]{2,0,1:T(8,128)(2,1)} %param.13), channel_id=1, source_target_pairs={{8,0},{12,4},{16,8},{20,12},{24,16},{28,20},{9,1},{13,5},{17,9},{2... | collective-permute-start | bytes 1179656 | tf_op jit(solution)/shard_map/ppermute | solution.py:17
  154.2 26.6 %collective-permute-start.10 = (bf16[256,6,128]{2,0,1:T(8,128)(2,1)}, bf16[256,6,128]{2,0,1:T(8,128)(2,1)}, u32[]{:S(2)}, u32[]{:S(2)}) collective-permute-start(bf16[256,6,128]{2,0,1:T(8,128)(2,1)} %param.13), channel_id=1, source_target_pairs={{12,0},{16,4},{20,8},{24,12},{28,16},{13,1},{17,5},{21,9},{25,13},... | collective-permute-start | bytes 1179656 | tf_op jit(solution)/shard_map/ppermute | solution.py:17
  155.6 64.1 %collective-permute-start.11 = (bf16[256,6,128]{2,0,1:T(8,128)(2,1)}, bf16[256,6,128]{2,0,1:T(8,128)(2,1)}, u32[]{:S(2)}, u32[]{:S(2)}) collective-permute-start(bf16[256,6,128]{2,0,1:T(8,128)(2,1)} %param.13), channel_id=1, source_target_pairs={{16,0},{20,4},{24,8},{28,12},{17,1},{21,5},{25,9},{29,13},{18,2},{... | collective-permute-start | bytes 1179656 | tf_op jit(solution)/shard_map/ppermute | solution.py:17
  158.3 11.0 %copy-start = (f32[256,1280]{0,1:T(8,128)}, f32[256,1280]{0,1:T(8,128)S(1)}, u32[]{:S(2)}) copy-start(f32[256,1280]{0,1:T(8,128)S(1)} %get-tuple-element.205) | copy-start | bytes 3932164
  158.3 65.1 %collective-permute-start.16 = (bf16[256,6,128]{2,0,1:T(8,128)(2,1)S(1)}, bf16[256,6,128]{2,0,1:T(8,128)(2,1)}, u32[]{:S(2)}, u32[]{:S(2)}) collective-permute-start(bf16[256,6,128]{2,0,1:T(8,128)(2,1)S(1)} %copy-done.24), channel_id=1, source_target_pairs={{4,0},{8,4},{12,8},{16,12},{20,16},{24,20},{28,24},{5,1},{9,5},{13... | collective-permute-start | bytes 1179656 | tf_op jit(solution)/shard_map/ppermute | solution.py:17
  160.9 6.9 %copy-start.18 = (bf16[1280,6,128]{2,0,1:T(8,128)(2,1)}, bf16[1280,6,128]{2,0,1:T(8,128)(2,1)S(1)}, u32[]{:S(2)}) copy-start(bf16[1280,6,128]{2,0,1:T(8,128)(2,1)S(1)} %constant_dynamic-update-slice_fusion.5) | copy-start | bytes 5898244
  172.4 6.4 %copy-start.7 = (f32[256,1280]{0,1:T(8,128)S(1)}, f32[256,1280]{0,1:T(8,128)}, u32[]{:S(2)}) copy-start(f32[256,1280]{0,1:T(8,128)} %copy-done.6) | copy-start | bytes 3932164
  172.4 53.9 %collective-permute-start.17 = (bf16[256,6,128]{2,0,1:T(8,128)(2,1)S(1)}, bf16[256,6,128]{2,0,1:T(8,128)(2,1)S(1)}, u32[]{:S(2)}, u32[]{:S(2)}) collective-permute-start(bf16[256,6,128]{2,0,1:T(8,128)(2,1)S(1)} %copy-done.24), channel_id=1, source_target_pairs={{8,0},{12,4},{16,8},{20,12},{24,16},{28,20},{9,1},{13,5},{17,9},{2... | collective-permute-start | bytes 1179656 | tf_op jit(solution)/shard_map/ppermute | solution.py:17
  175.7 52.5 %collective-permute-start.18 = (bf16[256,6,128]{2,0,1:T(8,128)(2,1)S(1)}, bf16[256,6,128]{2,0,1:T(8,128)(2,1)S(1)}, u32[]{:S(2)}, u32[]{:S(2)}) collective-permute-start(bf16[256,6,128]{2,0,1:T(8,128)(2,1)S(1)} %copy-done.24), channel_id=1, source_target_pairs={{12,0},{16,4},{20,8},{24,12},{28,16},{13,1},{17,5},{21,9},{25,13},... | collective-permute-start | bytes 1179656 | tf_op jit(solution)/shard_map/ppermute | solution.py:17
  178.8 5.3 %copy-start.5 = (f32[256,1280]{0,1:T(8,128)S(1)}, f32[256,1280]{0,1:T(8,128)}, u32[]{:S(2)}) copy-start(f32[256,1280]{0,1:T(8,128)} %copy-done.4) | copy-start | bytes 3932164
  178.8 5.3 %copy-start.12 = (f32[256,1280]{0,1:T(8,128)S(1)}, f32[256,1280]{0,1:T(8,128)}, u32[]{:S(2)}) copy-start(f32[256,1280]{0,1:T(8,128)} %get-tuple-element.191) | copy-start | bytes 3932164
  180.8 68.7 %collective-permute-start.19 = (bf16[256,6,128]{2,0,1:T(8,128)(2,1)S(1)}, bf16[256,6,128]{2,0,1:T(8,128)(2,1)S(1)}, u32[]{:S(2)}, u32[]{:S(2)}) collective-permute-start(bf16[256,6,128]{2,0,1:T(8,128)(2,1)S(1)} %copy-done.24), channel_id=1, source_target_pairs={{16,0},{20,4},{24,8},{28,12},{17,1},{21,5},{25,9},{29,13},{18,2},{... | collective-permute-start | bytes 1179656 | tf_op jit(solution)/shard_map/ppermute | solution.py:17
  182.1 40.8 %copy-start.20 = (bf16[1280,6,128]{2,0,1:T(8,128)(2,1)S(1)}, bf16[1280,6,128]{2,0,1:T(8,128)(2,1)}, u32[]{:S(2)}) copy-start(bf16[1280,6,128]{2,0,1:T(8,128)(2,1)} %copy-done.19) | copy-start | bytes 5898244
  184.1 38.8 %copy-start.3 = (f32[256,1280]{0,1:T(8,128)S(1)}, f32[256,1280]{0,1:T(8,128)}, u32[]{:S(2)}) copy-start(f32[256,1280]{0,1:T(8,128)} %copy-done.2) | copy-start | bytes 3932164
  184.1 38.8 %copy-start.11 = (f32[256,1280]{0,1:T(8,128)S(1)}, f32[256,1280]{0,1:T(8,128)}, u32[]{:S(2)}) copy-start(f32[256,1280]{0,1:T(8,128)} %get-tuple-element.195) | copy-start | bytes 3932164
  219.6 31.3 %collective-permute-start.12 = (f32[256,6]{0,1:T(8,128)S(1)}, f32[256,6]{0,1:T(8,128)S(1)}, u32[]{:S(2)}, u32[]{:S(2)}) collective-permute-start(f32[256,6]{0,1:T(8,128)S(1)} %stack.109), channel_id=1, source_target_pairs={{4,0},{8,4},{12,8},{16,12},{20,16},{24,20},{28,24},{5,1},{9,5},{13... | collective-permute-start | bytes 18440 | tf_op jit(solution)/shard_map/ppermute | solution.py:17
  220.9 3.8 %copy-start.21 = (bf16[1280,6,128]{2,0,1:T(8,128)(2,1)S(1)}, bf16[1280,6,128]{2,0,1:T(8,128)(2,1)}, u32[]{:S(2)}) copy-start(bf16[1280,6,128]{2,0,1:T(8,128)(2,1)} %constant_dynamic-update-slice_fusion.24) | copy-start | bytes 5898244
  222.9 2.9 copy-start.10
  223.4 28.8 %collective-permute-start.13 = (f32[256,6]{0,1:T(8,128)S(1)}, f32[256,6]{0,1:T(8,128)S(1)}, u32[]{:S(2)}, u32[]{:S(2)}) collective-permute-start(f32[256,6]{0,1:T(8,128)S(1)} %stack.109), channel_id=1, source_target_pairs={{8,0},{12,4},{16,8},{20,12},{24,16},{28,20},{9,1},{13,5},{17,9},{2... | collective-permute-start | bytes 18440 | tf_op jit(solution)/shard_map/ppermute | solution.py:17
  226.3 27.2 %collective-permute-start.14 = (f32[256,6]{0,1:T(8,128)S(1)}, f32[256,6]{0,1:T(8,128)S(1)}, u32[]{:S(2)}, u32[]{:S(2)}) collective-permute-start(f32[256,6]{0,1:T(8,128)S(1)} %stack.109), channel_id=1, source_target_pairs={{12,0},{16,4},{20,8},{24,12},{28,16},{13,1},{17,5},{21,9},{25,13},... | collective-permute-start | bytes 18440 | tf_op jit(solution)/shard_map/ppermute | solution.py:17
  228.3 26.9 %collective-permute-start.15 = (f32[256,6]{0,1:T(8,128)S(1)}, f32[256,6]{0,1:T(8,128)S(1)}, u32[]{:S(2)}, u32[]{:S(2)}) collective-permute-start(f32[256,6]{0,1:T(8,128)S(1)} %stack.109), channel_id=1, source_target_pairs={{16,0},{20,4},{24,8},{28,12},{17,1},{21,5},{25,9},{29,13},{18,2},{... | collective-permute-start | bytes 18440 | tf_op jit(solution)/shard_map/ppermute | solution.py:17
  229.8 32.5 %copy-start.37 = (bf16[256,6,128]{2,0,1:T(8,128)(2,1)S(1)}, bf16[256,6,128]{2,0,1:T(8,128)(2,1)}, u32[]{:S(2)}) copy-start(bf16[256,6,128]{2,0,1:T(8,128)(2,1)} %param.14) | copy-start | bytes 1179652
  229.8 32.5 %copy-start.39 = (bf16[1280,6,128]{2,0,1:T(8,128)(2,1)S(1)}, bf16[1280,6,128]{2,0,1:T(8,128)(2,1)}, u32[]{:S(2)}) copy-start(bf16[1280,6,128]{2,0,1:T(8,128)(2,1)} %constant_dynamic-update-slice_fusion.10) | copy-start | bytes 5898244
  230.3 32.6 %copy-start.42 = (bf16[256,6,128]{2,0,1:T(8,128)(2,1)}, bf16[256,6,128]{2,0,1:T(8,128)(2,1)S(1)}, u32[]{:S(2)}) copy-start(bf16[256,6,128]{2,0,1:T(8,128)(2,1)S(1)} %fusion.94) | copy-start | bytes 1179652
  249.6 5.6 %collective-permute-start.20 = (f32[256,6]{0,1:T(8,128)S(1)}, f32[256,6]{0,1:T(8,128)S(1)}, u32[]{:S(2)}, u32[]{:S(2)}) collective-permute-start(f32[256,6]{0,1:T(8,128)S(1)} %stack.110), channel_id=1, source_target_pairs={{4,0},{8,4},{12,8},{16,12},{20,16},{24,20},{28,24},{5,1},{9,5},{13... | collective-permute-start | bytes 18440 | tf_op jit(solution)/shard_map/ppermute | solution.py:17
  250.9 18.1 %copy-start.22 = (bf16[1280,6,128]{2,0,1:T(8,128)(2,1)}, bf16[1280,6,128]{2,0,1:T(8,128)(2,1)S(1)}, u32[]{:S(2)}) copy-start(bf16[1280,6,128]{2,0,1:T(8,128)(2,1)S(1)} %constant_dynamic-update-slice_fusion.20) | copy-start | bytes 5898244
  250.9 5.5 %collective-permute-start.21 = (f32[256,6]{0,1:T(8,128)S(1)}, f32[256,6]{0,1:T(8,128)S(1)}, u32[]{:S(2)}, u32[]{:S(2)}) collective-permute-start(f32[256,6]{0,1:T(8,128)S(1)} %stack.110), channel_id=1, source_target_pairs={{8,0},{12,4},{16,8},{20,12},{24,16},{28,20},{9,1},{13,5},{17,9},{2... | collective-permute-start | bytes 18440 | tf_op jit(solution)/shard_map/ppermute | solution.py:17
  252.3 8.3 %collective-permute-start.22 = (f32[256,6]{0,1:T(8,128)S(1)}, f32[256,6]{0,1:T(8,128)S(1)}, u32[]{:S(2)}, u32[]{:S(2)}) collective-permute-start(f32[256,6]{0,1:T(8,128)S(1)} %stack.110), channel_id=1, source_target_pairs={{12,0},{16,4},{20,8},{24,12},{28,16},{13,1},{17,5},{21,9},{25,13},... | collective-permute-start | bytes 18440 | tf_op jit(solution)/shard_map/ppermute | solution.py:17
  253.6 8.5 %collective-permute-start.23 = (f32[256,6]{0,1:T(8,128)S(1)}, f32[256,6]{0,1:T(8,128)S(1)}, u32[]{:S(2)}, u32[]{:S(2)}) collective-permute-start(f32[256,6]{0,1:T(8,128)S(1)} %stack.110), channel_id=1, source_target_pairs={{16,0},{20,4},{24,8},{28,12},{17,1},{21,5},{25,9},{29,13},{18,2},{... | collective-permute-start | bytes 18440 | tf_op jit(solution)/shard_map/ppermute | solution.py:17
  301.4 4.1 %copy-start.14 = (bf16[256,128]{1,0:T(8,128)(2,1)S(1)}, bf16[256,128]{1,0:T(8,128)(2,1)}, u32[]{:S(2)}) copy-start(bf16[256,128]{1,0:T(8,128)(2,1)} %param.22) | copy-start | bytes 196612
  301.4 4.1 %copy-start.33 = (f32[256,256]{1,0:T(8,128)S(1)}, f32[256,256]{1,0:T(8,128)}, u32[]{:S(2)}) copy-start(f32[256,256]{1,0:T(8,128)} %copy-done.32) | copy-start | bytes 786436
  301.4 4.4 %copy-start.38 = (bf16[256,64]{0,1:T(8,128)(2,1)S(1)}, bf16[256,64]{0,1:T(8,128)(2,1)}, u32[]{:S(2)}) copy-start(bf16[256,64]{0,1:T(8,128)(2,1)} %fusion.120) | copy-start | bytes 98308
  302.7 3.9 %copy-start.16 = (bf16[256,12,128]{0,2,1:T(8,128)(2,1)S(1)}, bf16[256,12,128]{0,2,1:T(8,128)(2,1)}, u32[]{:S(2)}) copy-start(bf16[256,12,128]{0,2,1:T(8,128)(2,1)} %copy-done.15) | copy-start | bytes 2359300
  302.7 3.9 %copy-start.35 = (bf16[256,12,128]{0,2,1:T(8,128)(2,1)S(1)}, bf16[256,12,128]{0,2,1:T(8,128)(2,1)}, u32[]{:S(2)}) copy-start(bf16[256,12,128]{0,2,1:T(8,128)(2,1)} %copy.44) | copy-start | bytes 2359300
  302.7 3.9 %copy-start.41 = (f32[256,12]{0,1:T(8,128)S(1)}, f32[256,12]{0,1:T(8,128)}, u32[]{:S(2)}) copy-start(f32[256,12]{0,1:T(8,128)} %param.19) | copy-start | bytes 36868
  302.7 3.9 %copy-start.44 = (f32[12]{0:T(128)S(1)}, f32[12]{0:T(128)}, u32[]{:S(2)}) copy-start(f32[12]{0:T(128)} %param.21) | copy-start | bytes 148
  306.6 3.0 copy-start.46
  306.6 3.0 copy-start.49
  (12 other events, 16.4 us)
Sparse Core Ops, SparseCore 0:
  29.3 71.4 all-gather.3
  306.7 19.4 reduce-scatter.3
where the time goes:
time: 342 us; the launch traced here: 340 us
  starting transfers between devices  99.4 us (29%)
  matrix products  61.4 us (18%)
  waiting for transfers between devices  60.2 us (18%)
  blocking collectives  54 us (16%)
  local copies, waits for them, and re-layouts  39.7 us (12%)
  between operations  15.9 us (5%)
  other arithmetic  9.3 us (3%)
    ppermute x24, starting transfers between devices, from_behind(): lax.ppermute(value, axis, [(source, source + steps) for source in range(f...  99.3 us
    ppermute x24, waiting for transfers between devices, from_behind(): lax.ppermute(value, axis, [(source, source + steps) for source in range(f...  60.1 us
    unnamed x1, blocking collectives  33.9 us
    unnamed x136, local copies, waits for them, and re-layouts  24.4 us
    psum x1, blocking collectives, shards(): grad_decay, grad_skip = lax.psum((decay_total, skip_total), 'seq')  20.1 us
    dot_general x6, matrix products, key_pass(): jnp.einsum('ge,gd->ed', scores_gradient, q_head, preferred_element_type=j...  13.1 us
    dot_general x6, matrix products, window_pass(): jnp.einsum('id,ed->ie', g_head, v_head, preferred_element_type=jnp.float32)  10.1 us
    mul x7, local copies, waits for them, and re-layouts, join_adjoint(): lower_side[0][:, None, None] * upper_side[1]  8.79 us
  transfers between devices with their start and end apart: 26, of which 5 were waited for; matrix products, arithmetic and copies ran while one was open for 25% of the time, Pallas kernels for 0%

commit v1 on v0

v1 whole, which is shorter than its diff:
```python
import functools
import math

import jax
import jax.numpy as jnp
from jax import lax
from jax.experimental import pallas as pl
from jax.experimental.pallas import tpu as pltpu
from jax.sharding import PartitionSpec as P

NSTATE = 64
WINDOW = 1024
LOG2E = math.log2(math.e)
NEVER = -1e30
EXACT = lax.Precision.HIGHEST
F32 = jnp.float32
BF16 = jnp.bfloat16
VMEM_BYTES = 48 * 1024 * 1024


def dot(left, right, contract, precision=None):
    return lax.dot_general(
        left, right, (contract, ((), ())), precision=precision, preferred_element_type=F32
    )


NT = ((1,), (1,))
NN = ((1,), (0,))
TN = ((0,), (0,))


def moved(value, steps):
    count = lax.axis_size("seq")
    pairs = [(at, at + steps) for at in range(count) if 0 <= at + steps < count]
    return lax.ppermute(value, "seq", pairs)


def swapped(value):
    count = lax.axis_size("seq")
    return lax.ppermute(value, "seq", [(at, at ^ 1) for at in range(count)])


def vmem(count):
    return [pl.BlockSpec(memory_space=pltpu.VMEM)] * count


def call(body, outs, ins, flops, scratch=(), smem=0, name=None):
    whole = sum(math.prod(v.shape) * v.dtype.itemsize for v in (*ins, *outs))
    specs = [pl.BlockSpec(memory_space=pltpu.SMEM)] * smem + vmem(len(ins) - smem)
    return pl.pallas_call(
        body,
        out_shape=outs,
        in_specs=specs,
        out_specs=vmem(len(outs)),
        scratch_shapes=list(scratch),
        compiler_params=pltpu.CompilerParams(vmem_limit_bytes=VMEM_BYTES),
        cost_estimate=pl.CostEstimate(flops=flops, bytes_accessed=whole, transcendentals=0),
        name=name,
    )(*ins)


def shape(dims, dtype):
    return jax.ShapeDtypeStruct(dims, dtype)


def block_mask(distance, reach, tokens):
    keys = lax.broadcasted_iota(jnp.int32, (tokens, tokens), 0)
    rows = lax.broadcasted_iota(jnp.int32, (tokens, tokens), 1)
    if distance == 0:
        return keys <= rows
    if distance == reach:
        return keys > rows
    return None


def scores(key_block, query_block, mask, factor, bias=None):
    value = dot(key_block, query_block, NT) * factor
    if bias is not None:
        value = value + bias
    if mask is not None:
        value = jnp.where(mask, value, NEVER)
    return value


def place_pairs(place, mine, theirs, target, first):
    for step in range(len(mine)):
        target[first + 2 * step + place] = mine[step][...]
        target[first + 2 * step + 1 - place] = theirs[step][...]


def stats_body(reach, *refs):
    where_ref = refs[0]
    hops = reach // 2
    keys = refs[1 : 1 + 2 * (hops + 1)]
    qg_mine, qg_theirs, stats_ref, kv, qg = refs[1 + 2 * (hops + 1) :]
    place, pair = where_ref[0], where_ref[1]
    place_pairs(place, keys[0::2], keys[1::2], kv, 0)
    place_pairs(place, [qg_mine], [qg_theirs], qg, 0)
    heads, tokens, width = kv.shape[2:]
    factor = width ** (-0.5) * LOG2E
    masks = {0: block_mask(0, reach, tokens), reach: block_mask(reach, reach, tokens)}
    biases = [jnp.where(pair >= hops - hop, 0.0, NEVER) for hop in range(hops)] + [None]
    for head in range(heads):
        for a in range(2):
            q, g = qg[a, 0, head], qg[a, 1, head]
            top = total = delta = None
            for j in range(a + reach, a - 1, -1):
                s = scores(kv[j, 0, head], q, masks.get(a + reach - j), factor, biases[j // 2])
                dp = dot(kv[j, 1, head], g, NT)
                best = jnp.max(s, axis=0, keepdims=True)
                if top is not None:
                    best = jnp.maximum(top, best)
                p = jnp.exp2(s - best)
                own_total = jnp.sum(p, axis=0, keepdims=True)
                own_delta = jnp.sum(p * dp, axis=0, keepdims=True)
                if top is None:
                    total, delta = own_total, own_delta
                else:
                    fade = jnp.exp2(top - best)
                    total, delta = total * fade + own_total, delta * fade + own_delta
                top = best
            at = 2 * head + a
            stats_ref[0, at : at + 1, :] = top + jnp.log2(total)
            stats_ref[1, at : at + 1, :] = delta / total


def score_grads(key_block, value_block, q, g, lse, delta, mask, factor, scale, bias=None):
    p = jnp.exp2(scores(key_block, q, mask, factor, bias) - lse)
    dp = dot(value_block, g, NT)
    return p, (p * (dp - delta) * scale).astype(BF16)


def query_body(reach, *refs):
    where_ref = refs[0]
    hops = reach // 2
    keys = refs[1 : 1 + 2 * (hops + 1)]
    qg_mine, qg_theirs, stats_ref, dq_mine, dq_theirs, part, kv, qg, dq = refs[1 + 2 * (hops + 1) :]
    place, pair = where_ref[0], where_ref[1]
    place_pairs(place, keys[0::2], keys[1::2], kv, 0)
    place_pairs(place, [qg_mine], [qg_theirs], qg, 0)
    heads, tokens, width = kv.shape[2:]
    scale = width ** (-0.5)
    factor = scale * LOG2E
    masks = {0: block_mask(0, reach, tokens), reach: block_mask(reach, reach, tokens)}
    biases = [jnp.where(pair >= hops - hop, 0.0, NEVER) for hop in range(hops)] + [None]
    for head in range(heads):
        for a in range(2):
            q, g = qg[a, 0, head], qg[a, 1, head]
            at = 2 * head + a
            lse, delta = stats_ref[0, at : at + 1, :], stats_ref[1, at : at + 1, :]
            grad = None
            for j in range(a, a + reach + 1):
                key_block = kv[j, 0, head]
                p, ds = score_grads(
                    key_block, kv[j, 1, head], q, g, lse, delta,
                    masks.get(a + reach - j), factor, scale, biases[j // 2],
                )
                term = dot(ds, key_block, TN)
                grad = term if grad is None else grad + term
                own = j - reach
                if own >= 0:
                    dk, dv = dot(ds, q, NN), dot(p.astype(BF16), g, NN)
                    if a == own:
                        part[own, 0, head], part[own, 1, head] = dk, dv
                    if a > own:
                        part[own, 0, head] += dk
                        part[own, 1, head] += dv
            dq[a, head] = grad.astype(BF16)
    dq_mine[...] = dq[place]
    dq_theirs[...] = dq[1 - place]


def later_body(reach, *refs):
    where_ref = refs[0]
    hops = reach // 2
    own_mine, own_theirs = refs[1:3]
    rows = refs[3 : 3 + 2 * hops]
    stats = refs[3 + 2 * hops : 3 + 3 * hops]
    part, mine, theirs, kv, qg, out = refs[3 + 3 * hops :]
    place = where_ref[0]
    place_pairs(place, [own_mine], [own_theirs], kv, 0)
    place_pairs(place, rows[0::2], rows[1::2], qg, 0)
    heads, tokens, width = kv.shape[2:]
    scale = width ** (-0.5)
    factor = scale * LOG2E
    far = block_mask(reach, reach, tokens)
    for head in range(heads):
        for b in range(2):
            dk, dv = part[b, 0, head], part[b, 1, head]
            for a in range(2, b + reach + 1):
                q, g = qg[a - 2, 0, head], qg[a - 2, 1, head]
                source = stats[(a - 2) // 2]
                at = 2 * head + a % 2
                p, ds = score_grads(
                    kv[b, 0, head], kv[b, 1, head], q, g,
                    source[0, at : at + 1, :], source[1, at : at + 1, :],
                    far if a - b == reach else None, factor, scale,
                )
                dk = dk + dot(ds, q, NN)
                dv = dv + dot(p.astype(BF16), g, NN)
            out[b, 0, head], out[b, 1, head] = dk.astype(BF16), dv.astype(BF16)
    mine[...] = out[place]
    theirs[...] = out[1 - place]


def lane_scalars(values, count):
    lanes = lax.broadcasted_iota(jnp.int32, (1, 128), 1)
    row = jnp.zeros((1, 128), F32)
    for at in range(count):
        row = jnp.where(lanes == at, values[at], row)
    return row


def triangle(length):
    rows = lax.broadcasted_iota(jnp.int32, (length, length), 0)
    cols = lax.broadcasted_iota(jnp.int32, (length, length), 1)
    return rows, cols


def split_decay(rows):
    high = rows.astype(BF16).astype(F32)
    lanes = lax.broadcasted_iota(jnp.int32, rows.shape, 1)
    return jnp.where(lanes < 64, high, rows - high).astype(BF16)


def joined_decay(rows):
    rows = rows.astype(F32)
    return rows + pltpu.roll(rows, 64, 1)


def summary_body(rates_ref, dy_ref, dt_ref, bc_ref, base_ref, sent_ref, cum_ref, cumt_ref, wide):
    heads, tokens, width = dy_ref.shape
    wide[...] = jnp.zeros_like(wide)
    wide[:, :heads] = dt_ref[...]
    log_decay = wide[...] * lane_scalars(rates_ref, heads)
    rows, cols = triangle(tokens)
    cum = dot((cols <= rows).astype(F32), log_decay, NN, EXACT)
    cum_ref[...] = cum
    cumt = cum.T
    cumt_ref[...] = cumt[: cumt_ref.shape[0]]
    weights = jnp.exp(cum)
    last = jnp.exp(cumt[: cumt_ref.shape[0], tokens - 1 : tokens])
    bc = bc_ref[...].astype(F32)
    for head in range(heads):
        weighted = (bc * weights[:, head : head + 1]).astype(BF16)
        state = dot(weighted, dy_ref[head], TN)[NSTATE:]
        base_ref[head * NSTATE : (head + 1) * NSTATE] = state
        sent_ref[head * NSTATE : (head + 1) * NSTATE] = state.astype(BF16)
    decay = jnp.broadcast_to(last, (last.shape[0], width))
    base_ref[heads * NSTATE :] = decay
    sent_ref[heads * NSTATE :] = split_decay(decay)


def join_body(heads, first, base_ref, *refs):
    if first:
        got_ref, far_ref, sent_ref = refs
    else:
        far_old, got_ref, far_ref, sent_ref = refs
    tail = heads * NSTATE
    got_decay = joined_decay(got_ref[tail:])
    own = base_ref[tail:]
    if first:
        far_decay = got_decay
    else:
        old_decay = far_old[tail:]
        far_decay = old_decay * got_decay
    far_ref[tail:] = far_decay
    sent_ref[tail:] = split_decay(own * far_decay)
    for head in range(heads):
        rows = slice(head * NSTATE, (head + 1) * NSTATE)
        value = got_ref[rows].astype(F32)
        if not first:
            value = far_old[rows] + old_decay[head : head + 1] * value
        far_ref[rows] = value
        sent_ref[rows] = (base_ref[rows] + own[head : head + 1] * value).astype(BF16)


def scan_body(
    rates_ref, skips_ref, u_ref, dy_ref, dt_ref, bc_ref, start_ref, far_ref, cum_ref, cumt_ref,
    du_ref, steps_ref, gbc_ref, sums_ref, wide, columns, rows_one, rows_two,
):
    heads, tokens, width = u_ref.shape
    rates = lane_scalars(rates_ref, heads)
    wide[...] = jnp.zeros_like(wide)
    wide[:, :heads] = dt_ref[...]
    dt = wide[...]
    dtt = dt.T
    columns[...] = jnp.zeros_like(columns)
    rows_one[...] = jnp.zeros_like(rows_one)
    rows_two[...] = jnp.zeros_like(rows_two)
    cum, cumt = cum_ref[...], cumt_ref[...]
    bc = bc_ref[...]
    bct = bc.astype(F32).T
    bt, ct = bct[:NSTATE], bct[NSTATE:]
    c_only = bc[:, NSTATE:]
    b_only = bc[:, :NSTATE]
    inner = dot(b_only, c_only, NT)
    s_at, t_at = triangle(tokens)
    seen = s_at <= t_at
    inner = jnp.where(seen, inner, 0.0)
    last = cum[tokens - 1 : tokens]
    tail_all = jnp.exp(last - cum)
    weights_t = jnp.exp(cumt)
    tail_t = jnp.exp(cumt[:, tokens - 1 : tokens] - cumt)
    lanes = lax.broadcasted_iota(jnp.int32, (1, 128), 1)
    whole = jnp.zeros((1, 128), F32)
    skip_sum = jnp.zeros((1, 128), F32)
    pair_sum = None
    gb_t = jnp.zeros((NSTATE, tokens), F32)
    gc_t = jnp.zeros((NSTATE, tokens), F32)
    for head in range(heads):
        u, dy = u_ref[head], dy_ref[head]
        start = start_ref[head]
        far = far_ref[head * NSTATE : (head + 1) * NSTATE]
        far_low = far.astype(BF16)
        dt_col, dt_row = dt[:, head : head + 1], dtt[head : head + 1]
        spread = cumt[head : head + 1] - cum[:, head : head + 1]
        decay = jnp.where(seen, jnp.exp(jnp.where(seen, spread, 0.0)), 0.0)
        cross = dot(u, dy, NT)
        mixing = decay * inner
        product = mixing * cross
        weighted = decay * cross * dt_col
        pair_sum = weighted if pair_sum is None else pair_sum + weighted
        columns[:, head : head + 1] = jnp.sum(product, axis=1, keepdims=True)
        from_pairs = jnp.sum(product * dt_col, axis=0, keepdims=True)
        from_start = dot(start.astype(BF16), dy, NT) * weights_t[head : head + 1]
        gc_t = gc_t + from_start
        to_far = dot(far_low, u, NT) * tail_t[head : head + 1]
        gb_t = gb_t + to_far * dt_row
        rows_one[head : head + 1] = from_pairs + jnp.sum(from_start * ct, axis=0, keepdims=True)
        rows_two[head : head + 1] = jnp.sum(to_far * bt, axis=0, keepdims=True)
        driven = dot(mixing.astype(BF16), dy, NN)
        driven = driven + tail_all[:, head : head + 1] * dot(b_only, far_low, NN)
        dy_float = dy.astype(F32)
        du_ref[head] = (dt_col * driven + skips_ref[head] * dy_float).astype(BF16)
        own_whole = jnp.sum(jnp.sum(far * start, axis=0, keepdims=True), axis=1, keepdims=True)
        whole = jnp.where(lanes == head, own_whole, whole)
        own_skip = jnp.sum(
            jnp.sum(dy_float * u.astype(F32), axis=0, keepdims=True), axis=1, keepdims=True
        )
        skip_sum = jnp.where(lanes == head, own_skip, skip_sum)
    pair_low = pair_sum.astype(BF16)
    grad_b = dot(pair_low, c_only, NN) + gb_t.T
    grad_c = dot(pair_low, b_only, TN) + gc_t.T
    gbc_ref[:, :NSTATE] = grad_b.astype(BF16)
    gbc_ref[:, NSTATE:] = grad_c.astype(BF16)
    late = rows_two[...].T
    direct = columns[...] + late
    gathered = rows_one[...].T - dt * direct
    beyond = jnp.sum(dt * late, axis=0, keepdims=True) + jnp.exp(last) * whole
    grad_log = dot(seen.astype(F32), gathered, NN, EXACT) + beyond
    steps_ref[...] = (direct + rates * grad_log)[:, :heads]
    sums_ref[...] = jnp.zeros_like(sums_ref)
    sums_ref[0:1] = jnp.sum(dt * grad_log, axis=0, keepdims=True)
    sums_ref[1:2] = skip_sum


def shards(
    queries, key_vectors, values, out_grad, ssm_input, ssm_out_grad,
    step_sizes, decay_rates, skip_gains, bc_rows, saved_states,
):
    tokens, heads, width = queries.shape
    half = heads // 2
    reach = WINDOW // tokens
    hops = reach // 2
    at = lax.axis_index("seq")
    members = lax.axis_size("seq")
    place, pair = at % 2, at // 2
    where = jnp.stack([place, pair]).astype(jnp.int32)
    block = 2 * tokens * tokens * width

    sets = ssm_input.shape[1]
    held = -(-sets // 16) * 16
    u = jnp.transpose(ssm_input, (1, 0, 2))
    dy = jnp.transpose(ssm_out_grad, (1, 0, 2))
    packed = sets * NSTATE + held
    base, sent, cum, cumt = call(
        summary_body,
        [
            shape((packed, width), F32), shape((packed, width), BF16),
            shape((tokens, 128), F32), shape((held, tokens), F32),
        ],
        [decay_rates, dy, step_sizes, bc_rows],
        sets * block // 2, [pltpu.VMEM((tokens, 128), F32)], smem=1, name="summary",
    )

    def by_head(one, two):
        both = jnp.transpose(jnp.stack([one, two]), (0, 2, 1, 3))
        keep = lax.dynamic_slice_in_dim(both, place * half, half, 1)
        give = lax.dynamic_slice_in_dim(both, (1 - place) * half, half, 1)
        return keep, give

    kv_mine, kv_give = by_head(key_vectors, values)
    qg_mine, qg_give = by_head(queries, out_grad)
    kv_theirs = swapped(kv_give)
    qg_theirs = swapped(qg_give)
    keys = [(kv_mine, kv_theirs)]
    rows = [(qg_mine, qg_theirs)]
    for _ in range(hops):
        keys.insert(0, tuple(moved(v, 2) for v in keys[0]))
        rows.append(tuple(moved(v, -2) for v in rows[-1]))

    far = None
    step = 1
    while step < members:
        got = moved(sent, -step)
        ins = [base, got] if far is None else [base, far, got]
        far, sent = call(
            functools.partial(join_body, sets, far is None),
            [shape((packed, width), F32), shape((packed, width), BF16)],
            ins, packed * width * 4, name="join",
        )
        step *= 2
    du, grad_steps, gbc, sums = call(
        scan_body,
        [
            shape((sets, tokens, width), BF16), shape((tokens, sets), F32),
            shape((tokens, 2 * NSTATE), BF16), shape((8, 128), F32),
        ],
        [
            decay_rates, skip_gains, u, dy, step_sizes, bc_rows,
            saved_states.reshape(saved_states.shape[1:]), far, cum, cumt,
        ],
        sets * block * 4,
        [
            pltpu.VMEM((tokens, 128), F32), pltpu.VMEM((tokens, 128), F32),
            pltpu.VMEM((128, tokens), F32), pltpu.VMEM((128, tokens), F32),
        ],
        smem=2, name="scan",
    )
    grad_inputs = jnp.transpose(du, (1, 0, 2))
    gbc = lax.all_to_all(gbc, "head", 0, 0, tiled=True)
    grad_bc = jnp.sum(
        gbc.reshape(lax.axis_size("head"), -1, 2 * NSTATE).astype(F32), axis=0
    )
    spread = jnp.broadcast_to(sums[None], (members, *sums.shape))
    summed = jnp.sum(lax.all_to_all(spread, "seq", 0, 0, tiled=True), axis=0)
    grad_decay, grad_skip = summed[0, :sets], summed[1, :sets]

    flat = [v for both in keys for v in both]
    kv_space = pltpu.VMEM((2 * (hops + 1), 2, half, tokens, width), BF16)
    qg_space = pltpu.VMEM((2, 2, half, tokens, width), BF16)
    (stats,) = call(
        functools.partial(stats_body, reach),
        [shape((2, 2 * half, tokens), F32)],
        [where, *flat, qg_mine, qg_theirs],
        4 * (reach + 1) * half * block, [kv_space, qg_space], smem=1, name="stats",
    )
    later_stats = [moved(stats, -2 * (hop + 1)) for hop in range(hops)]
    dq_mine, dq_give, part = call(
        functools.partial(query_body, reach),
        [
            shape((half, tokens, width), BF16), shape((half, tokens, width), BF16),
            shape((2, 2, half, tokens, width), F32),
        ],
        [where, *flat, qg_mine, qg_theirs, stats],
        6 * (reach + 1) * half * block,
        [kv_space, qg_space, pltpu.VMEM((2, half, tokens, width), BF16)],
        smem=1, name="query",
    )
    dq_theirs = swapped(dq_give)
    later = [v for both in rows[1:] for v in both]
    dkv_mine, dkv_give = call(
        functools.partial(later_body, reach),
        [shape((2, half, tokens, width), BF16)] * 2,
        [where, kv_mine, kv_theirs, *later, *later_stats, part],
        8 * reach * half * block,
        [qg_space, pltpu.VMEM((2 * hops, 2, half, tokens, width), BF16), qg_space],
        smem=1, name="later",
    )
    dkv_theirs = swapped(dkv_give)

    def by_token(mine, theirs):
        first = jnp.where(place == 0, mine, theirs)
        second = jnp.where(place == 0, theirs, mine)
        return jnp.transpose(jnp.concatenate([first, second], axis=0), (1, 0, 2))

    query_grad = by_token(dq_mine, dq_theirs)
    key_grad = by_token(dkv_mine[0], dkv_theirs[0])
    value_grad = by_token(dkv_mine[1], dkv_theirs[1])
    return (
        query_grad, key_grad, value_grad, grad_inputs, grad_steps, grad_bc, grad_decay, grad_skip,
    )


def solution(mesh):
    wide = P("seq", "head", None)
    return jax.shard_map(
        shards,
        mesh=mesh,
        in_specs=(
            wide, wide, wide, wide, wide, wide, P("seq", "head"), P("head"), P("head"),
            P("seq", None), P("seq", "head", None, None),
        ),
        out_specs=(
            wide, wide, wide, wide, P("seq", "head"), P(("seq", "head"), None), P("head"), P("head"),
        ),
        check_vma=False,
    )
```

time: 342 us -> 127 us (0.37)
  matrix products: 61.4 us -> 0 us
  starting transfers between devices: 99.4 us -> 43.2 us
  blocking collectives: 54 us -> 0 us
  local copies, waits for them, and re-layouts: 39.7 us -> 3.11 us
  Pallas kernels: 0 us -> 29.9 us
  waiting for transfers between devices: 60.2 us -> 43.6 us
  between operations: 15.9 us -> 0.93 us
  other arithmetic: 9.3 us -> 5.48 us
    ppermute x24 -> x17, starting transfers between devices: 99.3 us -> 36.6 us  [the longest x13 31.5 us: moved(): return lax.ppermute(value, 'seq', pairs)]
    dot_general x50 -> x0, matrix products: 61.4 us -> none  [the longest x6 13.1 us: key_pass(): jnp.einsum('ge,gd->ed', scores_gradient, q_head, preferred_element_type=j...]
    unnamed x1 -> x0, blocking collectives: 33.9 us -> none
    pallas_call x0 -> x8, Pallas kernels: none -> 29.9 us  [call(): pl.pallas_call(body, out_shape=outs, in_specs=specs, out_specs=vmem(len(o...]
    ppermute x24 -> x17, waiting for transfers between devices: 60.1 us -> 35.6 us  [the longest x13 24.9 us: moved(): return lax.ppermute(value, 'seq', pairs)]
    unnamed x136 -> x20, local copies, waits for them, and re-layouts: 24.4 us -> 1.97 us
    psum x1 -> x0, blocking collectives: 20.1 us -> none  [shards(): grad_decay, grad_skip = lax.psum((decay_total, skip_total), 'seq')]
    mul x7 -> x0, local copies, waits for them, and re-layouts: 8.79 us -> none  [join_adjoint(): lower_side[0][:, None, None] * upper_side[1]]
  transfers between devices with their start and end apart: 26 -> 19, of which waited for: 5 -> 7; matrix products, arithmetic and copies ran while one was open for 25% -> 3% of each run, Pallas kernels for 0% -> 24%
where the time goes in v1:
time: 127 us; the launch traced here: 126 us
  waiting for transfers between devices  43.6 us (34%)
  starting transfers between devices  43.2 us (34%)
  Pallas kernels  29.9 us (24%)
  other arithmetic  5.48 us (4%)
  local copies, waits for them, and re-layouts  3.11 us (2%)
    ppermute x13, starting transfers between devices, moved(): return lax.ppermute(value, 'seq', pairs)  31.5 us
    pallas_call x8, Pallas kernels, call(): pl.pallas_call(body, out_shape=outs, in_specs=specs, out_specs=vmem(len(o...  29.9 us
    ppermute x13, waiting for transfers between devices, moved(): return lax.ppermute(value, 'seq', pairs)  24.9 us
    ppermute x4, waiting for transfers between devices, swapped(): return lax.ppermute(value, 'seq', [(at, at ^ 1) for at in range(count)])  10.7 us
    all_to_all x1, waiting for transfers between devices, shards(): summed = jnp.sum(lax.all_to_all(spread, 'seq', 0, 0, tiled=True), axis=0)  6 us
    ppermute x4, starting transfers between devices, swapped(): return lax.ppermute(value, 'seq', [(at, at ^ 1) for at in range(count)])  5.11 us
    all_to_all x1, starting transfers between devices, shards(): summed = jnp.sum(lax.all_to_all(spread, 'seq', 0, 0, tiled=True), axis=0)  3.34 us
    all_to_all x1, starting transfers between devices, shards(): gbc = lax.all_to_all(gbc, 'head', 0, 0, tiled=True)  3.28 us
  transfers between devices with their start and end apart: 19, of which 7 were waited for; matrix products, arithmetic and copies ran while one was open for 3% of the time, Pallas kernels for 24%

profile of v1, /device:TPU:0, one launch (start us, length us, event | category | flops | bytes accessed | tf_op | source)
XLA Modules:
  0.0 126.3 jit_solution(16391084438255628422)
XLA Ops:
  0.6 0.0 copy-start.6
  0.6 0.0 copy-start.7
  0.7 2.1 %fusion.5 = (bf16[2,3,256,128]{3,2,1,0:T(8,128)(2,1)}, bf16[2,3,256,128]{3,2,1,0:T(8,128)(2,1)S(1)}) fusion(s32[]{:T(128)S(6)} %select_n.65, bf16[1,256,6,128]{3,1,2,0:T(8,128)(2,1)} %bitcast.41, bf16[1,256,6,128]{3,1,2,0:T(8,128)(2,1)} %bitcast.42, s32[]{:T(128)S(6)} %select_n.64), kind=kLoop, calls=%fused_computation.13 | loop fusion | flops 393216 | bytes 1572872 | tf_op jit(solution)/shard_map/dynamic_slice | solution.py:390
  2.9 2.9 %collective-permute-start.2 = (bf16[2,3,256,128]{3,2,1,0:T(8,128)(2,1)}, bf16[2,3,256,128]{3,2,1,0:T(8,128)(2,1)}, u32[]{:S(2)}, u32[]{:S(2)}) collective-permute-start(bf16[2,3,256,128]{3,2,1,0:T(8,128)(2,1)} %get-tuple-element.66), channel_id=1, source_target_pairs={{0,4},{4,0},{8,12},{12,8},{16,20},{20,16},{24,28},{28,24},{1,5},{5... | collective-permute-start | bytes 1179656 | tf_op jit(solution)/shard_map/ppermute | solution.py:40
  5.8 0.0 copy-done.6
  5.8 0.8 fusion.1
  6.6 0.0 collective-permute-start.5
  6.6 0.1 copy.23.dt_ref
  6.8 0.0 copy-done.1
  6.8 0.0 copy-start.4
  6.8 0.0 copy-start.5
  6.8 2.2 %summary.1 = (f32[784,128]{1,0:T(8,128)S(1)}, bf16[784,128]{1,0:T(8,128)(2,1)S(1)}, f32[256,128]{1,0:T(8,128)S(1)}, f32[16,256]{1,0:T(8,128)S(1)}) custom-call(f32[12]{0:T(128)S(1)} %copy-done.2, bf16[12,256,128]{2,1,0:T(8,128)(2,1)S(1)} %bitcast.37, f32[256,12]{1,0:T(8,128)S(1)} %copy.23.dt_ref, bf16[256,128]{1,0:T(8,128)(2,1)S(1)} %copy-done.1), custom_call_target="tpu_custom_call" | custom-call | flops 100663296 | bytes 1613872 | tf_op jit(solution)/shard_map/summary/pallas_call | solution.py:50
  9.0 1.3 %collective-permute-start.14 = (bf16[784,128]{1,0:T(8,128)(2,1)S(1)}, bf16[784,128]{1,0:T(8,128)(2,1)S(1)}, u32[]{:S(2)}, u32[]{:S(2)}) collective-permute-start(bf16[784,128]{1,0:T(8,128)(2,1)S(1)} %get-tuple-element.32), channel_id=1, source_target_pairs={{4,0},{8,4},{12,8},{16,12},{20,16},{24,20},{28,24},{5,1},{9,5},{13... | collective-permute-start | bytes 602120 | tf_op jit(solution)/shard_map/ppermute | solution.py:35
  10.3 6.7 %collective-permute-start = (bf16[2,3,256,128]{3,2,1,0:T(8,128)(2,1)S(1)}, bf16[2,3,256,128]{3,2,1,0:T(8,128)(2,1)}, u32[]{:S(2)}, u32[]{:S(2)}) collective-permute-start(bf16[2,3,256,128]{3,2,1,0:T(8,128)(2,1)S(1)} %get-tuple-element.67.refs_5_.refs_1_), channel_id=1, source_target_pairs={{0,8},{4,12},{8,16},{12,20},{16,24},{20,28},{1,9},{5,13},{9,17},{1... | collective-permute-start | bytes 1179656 | tf_op jit(solution)/shard_map/ppermute | solution.py:35
  17.0 2.9 %collective-permute-done.2.refs_6_.refs_2_ = bf16[2,3,256,128]{3,2,1,0:T(8,128)(2,1)} collective-permute-done((bf16[2,3,256,128]{3,2,1,0:T(8,128)(2,1)}, bf16[2,3,256,128]{3,2,1,0:T(8,128)(2,1)}, u32[]{:S(2)}, u32[]{:S(2)}) %collective-permute-start.2) | collective-permute-done | bytes 393248 | tf_op jit(solution)/shard_map/ppermute | solution.py:40
  19.9 4.2 %collective-permute-start.3 = (bf16[2,3,256,128]{3,2,1,0:T(8,128)(2,1)}, bf16[2,3,256,128]{3,2,1,0:T(8,128)(2,1)}, u32[]{:S(2)}, u32[]{:S(2)}) collective-permute-start(bf16[2,3,256,128]{3,2,1,0:T(8,128)(2,1)} %collective-permute-done.2.refs_6_.refs_2_), channel_id=1, source_target_pairs={{0,8},{4,12},{8,16},{12,20},{16,24},{20,28},{1,9},{5,13},{9,17},{1... | collective-permute-start | bytes 1179656 | tf_op jit(solution)/shard_map/ppermute | solution.py:35
  24.2 3.7 %collective-permute-done.14.refs_0_ = bf16[784,128]{1,0:T(8,128)(2,1)S(1)} collective-permute-done((bf16[784,128]{1,0:T(8,128)(2,1)S(1)}, bf16[784,128]{1,0:T(8,128)(2,1)S(1)}, u32[]{:S(2)}, u32[]{:S(2)}) %collective-permute-start.14) | collective-permute-done | bytes 200736 | tf_op jit(solution)/shard_map/ppermute | solution.py:35
  27.8 0.1 join.3
  27.9 1.3 %collective-permute-start.15 = (bf16[784,128]{1,0:T(8,128)(2,1)S(1)}, bf16[784,128]{1,0:T(8,128)(2,1)S(1)}, u32[]{:S(2)}, u32[]{:S(2)}) collective-permute-start(bf16[784,128]{1,0:T(8,128)(2,1)S(1)} %get-tuple-element.34), channel_id=1, source_target_pairs={{8,0},{12,4},{16,8},{20,12},{24,16},{28,20},{9,1},{13,5},{17,9},{2... | collective-permute-start | bytes 602120 | tf_op jit(solution)/shard_map/ppermute | solution.py:35
  29.2 1.3 %collective-permute-start.7 = (bf16[2,3,256,128]{3,2,1,0:T(8,128)(2,1)S(1)}, bf16[2,3,256,128]{3,2,1,0:T(8,128)(2,1)}, u32[]{:S(2)}, u32[]{:S(2)}) collective-permute-start(bf16[2,3,256,128]{3,2,1,0:T(8,128)(2,1)S(1)} %get-tuple-element.65.refs_7_), channel_id=1, source_target_pairs={{8,0},{12,4},{16,8},{20,12},{24,16},{28,20},{9,1},{13,5},{17,9},{2... | collective-permute-start | bytes 1179656 | tf_op jit(solution)/shard_map/ppermute | solution.py:35
  30.5 0.0 collective-permute-done.5.refs_8_
  30.5 1.3 %collective-permute-start.8 = (bf16[2,3,256,128]{3,2,1,0:T(8,128)(2,1)}, bf16[2,3,256,128]{3,2,1,0:T(8,128)(2,1)}, u32[]{:S(2)}, u32[]{:S(2)}) collective-permute-start(bf16[2,3,256,128]{3,2,1,0:T(8,128)(2,1)} %collective-permute-done.5.refs_8_), channel_id=1, source_target_pairs={{8,0},{12,4},{16,8},{20,12},{24,16},{28,20},{9,1},{13,5},{17,9},{2... | collective-permute-start | bytes 1179656 | tf_op jit(solution)/shard_map/ppermute | solution.py:35
  31.8 5.9 %collective-permute-done.15.refs_1_ = bf16[784,128]{1,0:T(8,128)(2,1)S(1)} collective-permute-done((bf16[784,128]{1,0:T(8,128)(2,1)S(1)}, bf16[784,128]{1,0:T(8,128)(2,1)S(1)}, u32[]{:S(2)}, u32[]{:S(2)}) %collective-permute-start.15) | collective-permute-done | bytes 200736 | tf_op jit(solution)/shard_map/ppermute | solution.py:35
  37.7 0.1 join.4
  37.8 1.3 %collective-permute-start.16 = (bf16[784,128]{1,0:T(8,128)(2,1)S(1)}, bf16[784,128]{1,0:T(8,128)(2,1)S(1)}, u32[]{:S(2)}, u32[]{:S(2)}) collective-permute-start(bf16[784,128]{1,0:T(8,128)(2,1)S(1)} %get-tuple-element.36), channel_id=1, source_target_pairs={{16,0},{20,4},{24,8},{28,12},{17,1},{21,5},{25,9},{29,13},{18,2},{... | collective-permute-start | bytes 602120 | tf_op jit(solution)/shard_map/ppermute | solution.py:35
  39.1 0.0 collective-permute-done.refs_3_
  39.1 4.5 %collective-permute-start.1 = (bf16[2,3,256,128]{3,2,1,0:T(8,128)(2,1)}, bf16[2,3,256,128]{3,2,1,0:T(8,128)(2,1)}, u32[]{:S(2)}, u32[]{:S(2)}) collective-permute-start(bf16[2,3,256,128]{3,2,1,0:T(8,128)(2,1)} %collective-permute-done.refs_3_), channel_id=1, source_target_pairs={{0,8},{4,12},{8,16},{12,20},{16,24},{20,28},{1,9},{5,13},{9,17},{1... | collective-permute-start | bytes 1179656 | tf_op jit(solution)/shard_map/ppermute | solution.py:35
  43.6 0.0 collective-permute-done.3.refs_4_
  43.7 4.2 %collective-permute-start.4 = (bf16[2,3,256,128]{3,2,1,0:T(8,128)(2,1)}, bf16[2,3,256,128]{3,2,1,0:T(8,128)(2,1)}, u32[]{:S(2)}, u32[]{:S(2)}) collective-permute-start(bf16[2,3,256,128]{3,2,1,0:T(8,128)(2,1)} %collective-permute-done.3.refs_4_), channel_id=1, source_target_pairs={{0,8},{4,12},{8,16},{12,20},{16,24},{20,28},{1,9},{5,13},{9,17},{1... | collective-permute-start | bytes 1179656 | tf_op jit(solution)/shard_map/ppermute | solution.py:35
  47.9 0.0 collective-permute-done.7.refs_3_
  47.9 1.3 %collective-permute-start.9 = (bf16[2,3,256,128]{3,2,1,0:T(8,128)(2,1)}, bf16[2,3,256,128]{3,2,1,0:T(8,128)(2,1)}, u32[]{:S(2)}, u32[]{:S(2)}) collective-permute-start(bf16[2,3,256,128]{3,2,1,0:T(8,128)(2,1)} %collective-permute-done.7.refs_3_), channel_id=1, source_target_pairs={{8,0},{12,4},{16,8},{20,12},{24,16},{28,20},{9,1},{13,5},{17,9},{2... | collective-permute-start | bytes 1179656 | tf_op jit(solution)/shard_map/ppermute | solution.py:35
  49.2 15.3 %collective-permute-done.16.refs_1_ = bf16[784,128]{1,0:T(8,128)(2,1)S(1)} collective-permute-done((bf16[784,128]{1,0:T(8,128)(2,1)S(1)}, bf16[784,128]{1,0:T(8,128)(2,1)S(1)}, u32[]{:S(2)}, u32[]{:S(2)}) %collective-permute-start.16) | collective-permute-done | bytes 200736 | tf_op jit(solution)/shard_map/ppermute | solution.py:35
  64.5 0.8 join.5
  65.2 1.1 copy-done.3
  66.4 5.6 %scan.1 = (bf16[12,256,128]{2,1,0:T(8,128)(2,1)}, f32[256,12]{1,0:T(8,128)S(1)}, bf16[256,128]{1,0:T(8,128)(2,1)}, f32[8,128]{1,0:T(8,128)S(1)}) custom-call(f32[12]{0:T(128)S(1)} %copy-done.2, f32[12]{0:T(128)S(1)} %copy-done.5, bf16[12,256,128]{2,1,0:T(8,128)(2,1)S(1)} %bitcast.39, bf16[12,256,128]{2,1,0:T(8,128)(2,1)S(1)} %bitcast.38, ...), custom_call_target="tpu_custom_call" | custom-call | flops 805306368 | bytes 3461216 | tf_op jit(solution)/shard_map/scan/pallas_call | solution.py:50
  72.0 3.3 %all-to-all-start = ((bf16[4,64,128]{2,1,0:T(8,128)(2,1)}), bf16[4,64,128]{2,1,0:T(8,128)(2,1)S(1)}, u32[]{:S(2)}, u32[]{:S(2)}) async-start(bf16[4,64,128]{2,1,0:T(8,128)(2,1)} %bitcast.21), calls=%async_computation | async-start | bytes 131072 | tf_op jit(solution)/shard_map/all_to_all | solution.py:432
  75.3 0.0 collective-permute-done.8.refs_4_
  75.3 1.3 %collective-permute-start.10 = (bf16[2,3,256,128]{3,2,1,0:T(8,128)(2,1)}, bf16[2,3,256,128]{3,2,1,0:T(8,128)(2,1)S(1)}, u32[]{:S(2)}, u32[]{:S(2)}) collective-permute-start(bf16[2,3,256,128]{3,2,1,0:T(8,128)(2,1)} %collective-permute-done.8.refs_4_), channel_id=1, source_target_pairs={{8,0},{12,4},{16,8},{20,12},{24,16},{28,20},{9,1},{13,5},{17,9},{2... | collective-permute-start | bytes 1179656 | tf_op jit(solution)/shard_map/ppermute | solution.py:35
  76.6 0.1 pad_add_fusion.refs_0_
  76.7 0.7 copy.24
  77.4 2.0 %all-to-all-done = bf16[4,64,128]{2,1,0:T(8,128)(2,1)S(1)} async-done(((bf16[4,64,128]{2,1,0:T(8,128)(2,1)}), bf16[4,64,128]{2,1,0:T(8,128)(2,1)S(1)}, u32[]{:S(2)}, u32[]{:S(2)}) %all-to-all-start) | async-done | bytes 65568 | tf_op jit(solution)/shard_map/all_to_all | solution.py:432
  79.4 0.6 broadcast_in_dim.2
  80.0 3.3 %all-to-all-start.1 = ((f32[8,8,128]{2,1,0:T(8,128)}), f32[8,8,128]{2,1,0:T(8,128)S(1)}, u32[]{:S(2)}, u32[]{:S(2)}) async-start(f32[8,8,128]{2,1,0:T(8,128)} %broadcast_in_dim.2), calls=%async_computation.1 | async-start | bytes 65536 | tf_op jit(solution)/shard_map/all_to_all | solution.py:437
  83.3 0.6 convert_reduce_fusion
  84.0 6.0 %all-to-all-done.1 = f32[8,8,128]{2,1,0:T(8,128)S(1)} async-done(((f32[8,8,128]{2,1,0:T(8,128)}), f32[8,8,128]{2,1,0:T(8,128)S(1)}, u32[]{:S(2)}, u32[]{:S(2)}) %all-to-all-start.1) | async-done | bytes 32800 | tf_op jit(solution)/shard_map/all_to_all | solution.py:437
  90.0 0.0 collective-permute-done.1.refs_1_
  90.0 0.0 collective-permute-done.4.refs_2_
  90.0 4.6 %stats.1.refs_9_ = f32[2,6,256]{2,1,0:T(8,128)S(1)} custom-call(s32[2]{0:T(128)S(1)} %pad_add_fusion.refs_0_, bf16[2,3,256,128]{3,2,1,0:T(8,128)(2,1)} %collective-permute-done.1.refs_1_, bf16[2,3,256,128]{3,2,1,0:T(8,128)(2,1)} %collective-permute-done.4.refs_2_, bf16[2,3,256,128]{3,2,1,0:T(8,128)(2,1)} %collective-permute-done.refs_3_, ...), custom_call_target="tpu_custom_call" | custom-call | flops 1006632960 | bytes 3158024 | tf_op jit(solution)/shard_map/stats/pallas_call | solution.py:50
  94.6 1.3 %collective-permute-start.11 = (f32[2,6,256]{2,1,0:T(8,128)S(1)}, f32[2,6,256]{2,1,0:T(8,128)S(1)}, u32[]{:S(2)}, u32[]{:S(2)}) collective-permute-start(f32[2,6,256]{2,1,0:T(8,128)S(1)} %stats.1.refs_9_), channel_id=1, source_target_pairs={{8,0},{12,4},{16,8},{20,12},{24,16},{28,20},{9,1},{13,5},{17,9},{2... | collective-permute-start | bytes 36872 | tf_op jit(solution)/shard_map/ppermute | solution.py:35
  95.9 1.5 %collective-permute-start.12 = (f32[2,6,256]{2,1,0:T(8,128)S(1)}, f32[2,6,256]{2,1,0:T(8,128)S(1)}, u32[]{:S(2)}, u32[]{:S(2)}) collective-permute-start(f32[2,6,256]{2,1,0:T(8,128)S(1)} %stats.1.refs_9_), channel_id=1, source_target_pairs={{16,0},{20,4},{24,8},{28,12},{17,1},{21,5},{25,9},{29,13},{18,2},{... | collective-permute-start | bytes 36872 | tf_op jit(solution)/shard_map/ppermute | solution.py:35
  97.3 10.2 %query.1 = (bf16[3,256,128]{2,1,0:T(8,128)(2,1)S(1)}, bf16[3,256,128]{2,1,0:T(8,128)(2,1)S(1)}, f32[2,2,3,256,128]{4,3,2,1,0:T(8,128)S(1)}) custom-call(s32[2]{0:T(128)S(1)} %pad_add_fusion.refs_0_, bf16[2,3,256,128]{3,2,1,0:T(8,128)(2,1)} %collective-permute-done.1.refs_1_, bf16[2,3,256,128]{3,2,1,0:T(8,128)(2,1)} %collective-permute-done.4.refs_2_, ...), custom_call_target="tpu_custom_call" | custom-call | flops 1509949440 | bytes 5124104 | tf_op jit(solution)/shard_map/query/pallas_call | solution.py:50
  107.6 0.9 collective-permute-start.6
  108.5 0.0 collective-permute-done.9.refs_5_
  108.5 0.0 collective-permute-done.10.refs_6_
  108.5 0.0 collective-permute-done.11.refs_7_
  108.5 0.0 collective-permute-done.12.refs_8_
  108.5 6.4 %later.1 = (bf16[2,3,256,128]{3,2,1,0:T(8,128)(2,1)S(1)}, bf16[2,3,256,128]{3,2,1,0:T(8,128)(2,1)S(1)}) custom-call(s32[2]{0:T(128)S(1)} %pad_add_fusion.refs_0_, bf16[2,3,256,128]{3,2,1,0:T(8,128)(2,1)S(1)} %get-tuple-element.67.refs_5_.refs_1_, bf16[2,3,256,128]{3,2,1,0:T(8,128)(2,1)} %collective-permute-done.2.refs_6_.refs_2_, ...), custom_call_target="tpu_custom_call" | custom-call | flops 1610612736 | bytes 4743176 | tf_op jit(solution)/shard_map/later/pallas_call | solution.py:50
  114.9 1.2 collective-permute-start.13
  116.1 0.5 slice_bitcast_fusion
  116.7 0.0 collective-permute-done.6
  116.7 0.8 maximum_bitcast_fusion
  117.5 7.8 %collective-permute-done.13 = bf16[2,3,256,128]{3,2,1,0:T(8,128)(2,1)S(1)} collective-permute-done((bf16[2,3,256,128]{3,2,1,0:T(8,128)(2,1)S(1)}, bf16[2,3,256,128]{3,2,1,0:T(8,128)(2,1)S(1)}, u32[]{:S(2)}, u32[]{:S(2)}) %collective-permute-start.13) | collective-permute-done | bytes 393248 | tf_op jit(solution)/shard_map/ppermute | solution.py:40
  125.3 0.1 select_bitcast_fusion.1
  125.3 0.9 maximum_bitcast_fusion.1
  (13 shorter events, 0.1 us)
Async XLA Ops:
  0.6 5.2 %copy-start.6 = (bf16[256,6,128]{2,0,1:T(8,128)(2,1)S(1)}, bf16[256,6,128]{2,0,1:T(8,128)(2,1)}, u32[]{:S(2)}) copy-start(bf16[256,6,128]{2,0,1:T(8,128)(2,1)} %param.11) | copy-start | bytes 1179652
  0.6 5.2 %copy-start.7 = (bf16[256,6,128]{2,0,1:T(8,128)(2,1)S(1)}, bf16[256,6,128]{2,0,1:T(8,128)(2,1)}, u32[]{:S(2)}) copy-start(bf16[256,6,128]{2,0,1:T(8,128)(2,1)} %param.14) | copy-start | bytes 1179652
  0.7 6.0 %copy-start.8 = (f32[256,12]{0,1:T(8,128)S(1)}, f32[256,12]{0,1:T(8,128)}, u32[]{:S(2)}) copy-start(f32[256,12]{0,1:T(8,128)} %param.17) | copy-start | bytes 36868
  0.7 6.1 %copy-start = (bf16[256,12,128]{2,0,1:T(8,128)(2,1)S(1)}, bf16[256,12,128]{2,0,1:T(8,128)(2,1)}, u32[]{:S(2)}) copy-start(bf16[256,12,128]{2,0,1:T(8,128)(2,1)} %param.16) | copy-start | bytes 2359300
  0.7 6.1 %copy-start.1 = (bf16[256,128]{1,0:T(8,128)(2,1)S(1)}, bf16[256,128]{1,0:T(8,128)(2,1)}, u32[]{:S(2)}) copy-start(bf16[256,128]{1,0:T(8,128)(2,1)} %bc_ref.3) | copy-start | bytes 196612
  0.7 6.1 %copy-start.2 = (f32[12]{0:T(128)S(1)}, f32[12]{0:T(128)}, u32[]{:S(2)}) copy-start(f32[12]{0:T(128)} %rates_ref.3) | copy-start | bytes 148
  2.9 17.1 %collective-permute-start.2 = (bf16[2,3,256,128]{3,2,1,0:T(8,128)(2,1)}, bf16[2,3,256,128]{3,2,1,0:T(8,128)(2,1)}, u32[]{:S(2)}, u32[]{:S(2)}) collective-permute-start(bf16[2,3,256,128]{3,2,1,0:T(8,128)(2,1)} %get-tuple-element.66), channel_id=1, source_target_pairs={{0,4},{4,0},{8,12},{12,8},{16,20},{20,16},{24,28},{28,24},{1,5},{5... | collective-permute-start | bytes 1179656 | tf_op jit(solution)/shard_map/ppermute | solution.py:40
  6.6 23.9 %collective-permute-start.5 = (bf16[2,3,256,128]{3,2,1,0:T(8,128)(2,1)}, bf16[2,3,256,128]{3,2,1,0:T(8,128)(2,1)}, u32[]{:S(2)}, u32[]{:S(2)}) collective-permute-start(bf16[2,3,256,128]{3,2,1,0:T(8,128)(2,1)} %get-tuple-element.64), channel_id=1, source_target_pairs={{0,4},{4,0},{8,12},{12,8},{16,20},{20,16},{24,28},{28,24},{1,5},{5... | collective-permute-start | bytes 1179656 | tf_op jit(solution)/shard_map/ppermute | solution.py:40
  6.8 58.5 %copy-start.4 = (f32[1,12,64,128]{3,2,1,0:T(8,128)S(1)}, f32[1,12,64,128]{3,2,1,0:T(8,128)}, u32[]{:S(2)}) copy-start(f32[1,12,64,128]{3,2,1,0:T(8,128)} %param.21) | copy-start | bytes 1179652
  6.8 58.4 %copy-start.5 = (f32[12]{0:T(128)S(1)}, f32[12]{0:T(128)}, u32[]{:S(2)}) copy-start(f32[12]{0:T(128)} %skips_ref.1) | copy-start | bytes 148
  9.0 18.8 %collective-permute-start.14 = (bf16[784,128]{1,0:T(8,128)(2,1)S(1)}, bf16[784,128]{1,0:T(8,128)(2,1)S(1)}, u32[]{:S(2)}, u32[]{:S(2)}) collective-permute-start(bf16[784,128]{1,0:T(8,128)(2,1)S(1)} %get-tuple-element.32), channel_id=1, source_target_pairs={{4,0},{8,4},{12,8},{16,12},{20,16},{24,20},{28,24},{5,1},{9,5},{13... | collective-permute-start | bytes 602120 | tf_op jit(solution)/shard_map/ppermute | solution.py:35
  10.3 28.8 %collective-permute-start = (bf16[2,3,256,128]{3,2,1,0:T(8,128)(2,1)S(1)}, bf16[2,3,256,128]{3,2,1,0:T(8,128)(2,1)}, u32[]{:S(2)}, u32[]{:S(2)}) collective-permute-start(bf16[2,3,256,128]{3,2,1,0:T(8,128)(2,1)S(1)} %get-tuple-element.67.refs_5_.refs_1_), channel_id=1, source_target_pairs={{0,8},{4,12},{8,16},{12,20},{16,24},{20,28},{1,9},{5,13},{9,17},{1... | collective-permute-start | bytes 1179656 | tf_op jit(solution)/shard_map/ppermute | solution.py:35
  19.9 23.7 %collective-permute-start.3 = (bf16[2,3,256,128]{3,2,1,0:T(8,128)(2,1)}, bf16[2,3,256,128]{3,2,1,0:T(8,128)(2,1)}, u32[]{:S(2)}, u32[]{:S(2)}) collective-permute-start(bf16[2,3,256,128]{3,2,1,0:T(8,128)(2,1)} %collective-permute-done.2.refs_6_.refs_2_), channel_id=1, source_target_pairs={{0,8},{4,12},{8,16},{12,20},{16,24},{20,28},{1,9},{5,13},{9,17},{1... | collective-permute-start | bytes 1179656 | tf_op jit(solution)/shard_map/ppermute | solution.py:35
  27.9 9.8 %collective-permute-start.15 = (bf16[784,128]{1,0:T(8,128)(2,1)S(1)}, bf16[784,128]{1,0:T(8,128)(2,1)S(1)}, u32[]{:S(2)}, u32[]{:S(2)}) collective-permute-start(bf16[784,128]{1,0:T(8,128)(2,1)S(1)} %get-tuple-element.34), channel_id=1, source_target_pairs={{8,0},{12,4},{16,8},{20,12},{24,16},{28,20},{9,1},{13,5},{17,9},{2... | collective-permute-start | bytes 602120 | tf_op jit(solution)/shard_map/ppermute | solution.py:35
  29.2 18.6 %collective-permute-start.7 = (bf16[2,3,256,128]{3,2,1,0:T(8,128)(2,1)S(1)}, bf16[2,3,256,128]{3,2,1,0:T(8,128)(2,1)}, u32[]{:S(2)}, u32[]{:S(2)}) collective-permute-start(bf16[2,3,256,128]{3,2,1,0:T(8,128)(2,1)S(1)} %get-tuple-element.65.refs_7_), channel_id=1, source_target_pairs={{8,0},{12,4},{16,8},{20,12},{24,16},{28,20},{9,1},{13,5},{17,9},{2... | collective-permute-start | bytes 1179656 | tf_op jit(solution)/shard_map/ppermute | solution.py:35
  30.5 44.7 %collective-permute-start.8 = (bf16[2,3,256,128]{3,2,1,0:T(8,128)(2,1)}, bf16[2,3,256,128]{3,2,1,0:T(8,128)(2,1)}, u32[]{:S(2)}, u32[]{:S(2)}) collective-permute-start(bf16[2,3,256,128]{3,2,1,0:T(8,128)(2,1)} %collective-permute-done.5.refs_8_), channel_id=1, source_target_pairs={{8,0},{12,4},{16,8},{20,12},{24,16},{28,20},{9,1},{13,5},{17,9},{2... | collective-permute-start | bytes 1179656 | tf_op jit(solution)/shard_map/ppermute | solution.py:35
  37.8 26.6 %collective-permute-start.16 = (bf16[784,128]{1,0:T(8,128)(2,1)S(1)}, bf16[784,128]{1,0:T(8,128)(2,1)S(1)}, u32[]{:S(2)}, u32[]{:S(2)}) collective-permute-start(bf16[784,128]{1,0:T(8,128)(2,1)S(1)} %get-tuple-element.36), channel_id=1, source_target_pairs={{16,0},{20,4},{24,8},{28,12},{17,1},{21,5},{25,9},{29,13},{18,2},{... | collective-permute-start | bytes 602120 | tf_op jit(solution)/shard_map/ppermute | solution.py:35
  39.1 50.8 %collective-permute-start.1 = (bf16[2,3,256,128]{3,2,1,0:T(8,128)(2,1)}, bf16[2,3,256,128]{3,2,1,0:T(8,128)(2,1)}, u32[]{:S(2)}, u32[]{:S(2)}) collective-permute-start(bf16[2,3,256,128]{3,2,1,0:T(8,128)(2,1)} %collective-permute-done.refs_3_), channel_id=1, source_target_pairs={{0,8},{4,12},{8,16},{12,20},{16,24},{20,28},{1,9},{5,13},{9,17},{1... | collective-permute-start | bytes 1179656 | tf_op jit(solution)/shard_map/ppermute | solution.py:35
  43.7 46.3 %collective-permute-start.4 = (bf16[2,3,256,128]{3,2,1,0:T(8,128)(2,1)}, bf16[2,3,256,128]{3,2,1,0:T(8,128)(2,1)}, u32[]{:S(2)}, u32[]{:S(2)}) collective-permute-start(bf16[2,3,256,128]{3,2,1,0:T(8,128)(2,1)} %collective-permute-done.3.refs_4_), channel_id=1, source_target_pairs={{0,8},{4,12},{8,16},{12,20},{16,24},{20,28},{1,9},{5,13},{9,17},{1... | collective-permute-start | bytes 1179656 | tf_op jit(solution)/shard_map/ppermute | solution.py:35
  47.9 60.6 %collective-permute-start.9 = (bf16[2,3,256,128]{3,2,1,0:T(8,128)(2,1)}, bf16[2,3,256,128]{3,2,1,0:T(8,128)(2,1)}, u32[]{:S(2)}, u32[]{:S(2)}) collective-permute-start(bf16[2,3,256,128]{3,2,1,0:T(8,128)(2,1)} %collective-permute-done.7.refs_3_), channel_id=1, source_target_pairs={{8,0},{12,4},{16,8},{20,12},{24,16},{28,20},{9,1},{13,5},{17,9},{2... | collective-permute-start | bytes 1179656 | tf_op jit(solution)/shard_map/ppermute | solution.py:35
  65.2 1.1 copy-start.3
  72.0 7.4 %all-to-all-start = ((bf16[4,64,128]{2,1,0:T(8,128)(2,1)}), bf16[4,64,128]{2,1,0:T(8,128)(2,1)S(1)}, u32[]{:S(2)}, u32[]{:S(2)}) async-start(bf16[4,64,128]{2,1,0:T(8,128)(2,1)} %bitcast.21), calls=%async_computation | async-start | bytes 131072 | tf_op jit(solution)/shard_map/all_to_all | solution.py:432
  75.3 33.2 %collective-permute-start.10 = (bf16[2,3,256,128]{3,2,1,0:T(8,128)(2,1)}, bf16[2,3,256,128]{3,2,1,0:T(8,128)(2,1)S(1)}, u32[]{:S(2)}, u32[]{:S(2)}) collective-permute-start(bf16[2,3,256,128]{3,2,1,0:T(8,128)(2,1)} %collective-permute-done.8.refs_4_), channel_id=1, source_target_pairs={{8,0},{12,4},{16,8},{20,12},{24,16},{28,20},{9,1},{13,5},{17,9},{2... | collective-permute-start | bytes 1179656 | tf_op jit(solution)/shard_map/ppermute | solution.py:35
  80.0 10.0 %all-to-all-start.1 = ((f32[8,8,128]{2,1,0:T(8,128)}), f32[8,8,128]{2,1,0:T(8,128)S(1)}, u32[]{:S(2)}, u32[]{:S(2)}) async-start(f32[8,8,128]{2,1,0:T(8,128)} %broadcast_in_dim.2), calls=%async_computation.1 | async-start | bytes 65536 | tf_op jit(solution)/shard_map/all_to_all | solution.py:437
  94.6 13.9 %collective-permute-start.11 = (f32[2,6,256]{2,1,0:T(8,128)S(1)}, f32[2,6,256]{2,1,0:T(8,128)S(1)}, u32[]{:S(2)}, u32[]{:S(2)}) collective-permute-start(f32[2,6,256]{2,1,0:T(8,128)S(1)} %stats.1.refs_9_), channel_id=1, source_target_pairs={{8,0},{12,4},{16,8},{20,12},{24,16},{28,20},{9,1},{13,5},{17,9},{2... | collective-permute-start | bytes 36872 | tf_op jit(solution)/shard_map/ppermute | solution.py:35
  95.9 12.7 %collective-permute-start.12 = (f32[2,6,256]{2,1,0:T(8,128)S(1)}, f32[2,6,256]{2,1,0:T(8,128)S(1)}, u32[]{:S(2)}, u32[]{:S(2)}) collective-permute-start(f32[2,6,256]{2,1,0:T(8,128)S(1)} %stats.1.refs_9_), channel_id=1, source_target_pairs={{16,0},{20,4},{24,8},{28,12},{17,1},{21,5},{25,9},{29,13},{18,2},{... | collective-permute-start | bytes 36872 | tf_op jit(solution)/shard_map/ppermute | solution.py:35
  107.6 9.1 %collective-permute-start.6 = (bf16[3,256,128]{2,1,0:T(8,128)(2,1)S(1)}, bf16[3,256,128]{2,1,0:T(8,128)(2,1)S(1)}, u32[]{:S(2)}, u32[]{:S(2)}) collective-permute-start(bf16[3,256,128]{2,1,0:T(8,128)(2,1)S(1)} %get-tuple-element.27), channel_id=1, source_target_pairs={{0,4},{4,0},{8,12},{12,8},{16,20},{20,16},{24,28},{28,24},{1,5},{5... | collective-permute-start | bytes 589832 | tf_op jit(solution)/shard_map/ppermute | solution.py:40
  114.9 10.4 %collective-permute-start.13 = (bf16[2,3,256,128]{3,2,1,0:T(8,128)(2,1)S(1)}, bf16[2,3,256,128]{3,2,1,0:T(8,128)(2,1)S(1)}, u32[]{:S(2)}, u32[]{:S(2)}) collective-permute-start(bf16[2,3,256,128]{3,2,1,0:T(8,128)(2,1)S(1)} %get-tuple-element.30), channel_id=1, source_target_pairs={{0,4},{4,0},{8,12},{12,8},{16,20},{20,16},{24,28},{28,24},{1,5},{5... | collective-permute-start | bytes 1179656 | tf_op jit(solution)/shard_map/ppermute | solution.py:40

commit v2 on v1

--- a/solution.py
+++ b/solution.py
@@ -38,6 +38,10 @@
 def swapped(value):
     count = lax.axis_size("seq")
     return lax.ppermute(value, "seq", [(at, at ^ 1) for at in range(count)])
+
+
+def after(value, *others):
+    return lax.optimization_barrier((value, *others))[0]
 
 
 def vmem(count):
@@ -73,13 +77,24 @@
     return None
 
 
-def scores(key_block, query_block, mask, factor, bias=None):
-    value = dot(key_block, query_block, NT) * factor
-    if bias is not None:
-        value = value + bias
-    if mask is not None:
-        value = jnp.where(mask, value, NEVER)
-    return value
+def dressed(value, factor, axis, masks, biases):
+    count = len(masks)
+    length = value.shape[axis] // count
+    pieces = []
+    for at in range(count):
+        cut = slice(at * length, (at + 1) * length)
+        piece = (value[cut] if axis == 0 else value[:, cut]) * factor
+        if biases[at] is not None:
+            piece = piece + biases[at]
+        if masks[at] is not None:
+            piece = jnp.where(masks[at], piece, NEVER)
+        pieces.append(piece)
+    return jnp.concatenate(pieces, axis=axis)
+
+
+def band(ref, first, count, kind, head):
+    rows = ref[first : first + count, kind, head]
+    return rows.reshape(count * rows.shape[1], rows.shape[2])
 
 
 def place_pairs(place, mine, theirs, target, first):
@@ -88,84 +103,128 @@
         target[first + 2 * step + 1 - place] = theirs[step][...]
 
 
-def stats_body(reach, *refs):
+def online(kv, q, g, head, a, blocks, reach, factor, masks, biases, state):
+    for j in blocks:
+        s = dressed(
+            dot(kv[j % 2 if kv.shape[0] == 2 else j, 0, head], q, NT), factor, 0,
+            [masks[j - a]], [biases[j // 2]],
+        )
+        dp = dot(kv[j % 2 if kv.shape[0] == 2 else j, 1, head], g, NT)
+        best = jnp.max(s, axis=0, keepdims=True)
+        if state is not None:
+            best = jnp.maximum(state[0], best)
+        p = jnp.exp2(s - best)
+        total = jnp.sum(p, axis=0, keepdims=True)
+        delta = jnp.sum(p * dp, axis=0, keepdims=True)
+        if state is not None:
+            fade = jnp.exp2(state[0] - best)
+            total, delta = state[1] * fade + total, state[2] * fade + delta
+        state = (best, total, delta)
+    return state
+
+
+def early_body(reach, *refs):
     where_ref = refs[0]
     hops = reach // 2
-    keys = refs[1 : 1 + 2 * (hops + 1)]
-    qg_mine, qg_theirs, stats_ref, kv, qg = refs[1 + 2 * (hops + 1) :]
+    keys = refs[1 : 1 + 2 * hops]
+    qg_mine, qg_theirs, out_ref, kv, qg = refs[1 + 2 * hops :]
     place, pair = where_ref[0], where_ref[1]
-    place_pairs(place, keys[0::2], keys[1::2], kv, 0)
+    place_pairs(place, keys[0::2], keys[1::2], kv, 2)
     place_pairs(place, [qg_mine], [qg_theirs], qg, 0)
     heads, tokens, width = kv.shape[2:]
     factor = width ** (-0.5) * LOG2E
-    masks = {0: block_mask(0, reach, tokens), reach: block_mask(reach, reach, tokens)}
+    masks = [block_mask(reach - at, reach, tokens) for at in range(reach + 1)]
     biases = [jnp.where(pair >= hops - hop, 0.0, NEVER) for hop in range(hops)] + [None]
     for head in range(heads):
         for a in range(2):
-            q, g = qg[a, 0, head], qg[a, 1, head]
-            top = total = delta = None
-            for j in range(a + reach, a - 1, -1):
-                s = scores(kv[j, 0, head], q, masks.get(a + reach - j), factor, biases[j // 2])
-                dp = dot(kv[j, 1, head], g, NT)
-                best = jnp.max(s, axis=0, keepdims=True)
-                if top is not None:
-                    best = jnp.maximum(top, best)
-                p = jnp.exp2(s - best)
-                own_total = jnp.sum(p, axis=0, keepdims=True)
-                own_delta = jnp.sum(p * dp, axis=0, keepdims=True)
-                if top is None:
-                    total, delta = own_total, own_delta
-                else:
-                    fade = jnp.exp2(top - best)
-                    total, delta = total * fade + own_total, delta * fade + own_delta
-                top = best
+            state = online(
+                kv, qg[a, 0, head], qg[a, 1, head], head, a,
+                range(a + reach, max(a, 2) - 1, -1), reach, factor, masks, biases, None,
+            )
             at = 2 * head + a
+            for kind in range(3):
+                out_ref[kind, at : at + 1, :] = state[kind]
+
+
+def late_body(reach, *refs):
+    where_ref, far_mine, far_theirs, qg_mine, qg_theirs, early_ref, stats_ref, kv, qg = refs
+    hops = reach // 2
+    place, pair = where_ref[0], where_ref[1]
+    place_pairs(place, [far_mine], [far_theirs], kv, 0)
+    place_pairs(place, [qg_mine], [qg_theirs], qg, 0)
+    heads, tokens, width = kv.shape[2:]
+    factor = width ** (-0.5) * LOG2E
+    masks = [block_mask(reach - at, reach, tokens) for at in range(reach + 1)]
+    biases = [jnp.where(pair >= hops, 0.0, NEVER)]
+    for head in range(heads):
+        for a in range(2):
+            at = 2 * head + a
+            top, total, delta = online(
+                kv, qg[a, 0, head], qg[a, 1, head], head, a, range(1, a - 1, -1), reach, factor,
+                masks, biases, tuple(early_ref[kind, at : at + 1, :] for kind in range(3)),
+            )
             stats_ref[0, at : at + 1, :] = top + jnp.log2(total)
             stats_ref[1, at : at + 1, :] = delta / total
 
 
-def score_grads(key_block, value_block, q, g, lse, delta, mask, factor, scale, bias=None):
-    p = jnp.exp2(scores(key_block, q, mask, factor, bias) - lse)
+def key_grads(key_block, value_block, q, g, lse, delta, masks, factor, scale):
+    s = dressed(dot(key_block, q, NT), factor, 1, masks, [None] * len(masks))
+    p = jnp.exp2(s - lse)
     dp = dot(value_block, g, NT)
-    return p, (p * (dp - delta) * scale).astype(BF16)
+    ds = (p * (dp - delta) * scale).astype(BF16)
+    return dot(ds, q, NN), dot(p.astype(BF16), g, NN)
+
+
+def stat_row(sources, kind, head, first, count):
+    rows = [
+        sources[a // 2][kind, 2 * head + a % 2 : 2 * head + a % 2 + 1, :]
+        for a in range(first, first + count)
+    ]
+    return jnp.concatenate(rows, axis=1) if count > 1 else rows[0]
 
 
 def query_body(reach, *refs):
     where_ref = refs[0]
     hops = reach // 2
     keys = refs[1 : 1 + 2 * (hops + 1)]
-    qg_mine, qg_theirs, stats_ref, dq_mine, dq_theirs, part, kv, qg, dq = refs[1 + 2 * (hops + 1) :]
+    qg_mine, qg_theirs, stats_ref, dq_mine, dq_theirs, part, kv, qg, dq, tall = refs[
+        1 + 2 * (hops + 1) :
+    ]
     place, pair = where_ref[0], where_ref[1]
     place_pairs(place, keys[0::2], keys[1::2], kv, 0)
     place_pairs(place, [qg_mine], [qg_theirs], qg, 0)
     heads, tokens, width = kv.shape[2:]
     scale = width ** (-0.5)
     factor = scale * LOG2E
-    masks = {0: block_mask(0, reach, tokens), reach: block_mask(reach, reach, tokens)}
+    count = 2 * heads
+    tall[...] = jnp.zeros_like(tall)
+    tall[0:count] = stats_ref[0]
+    tall[8 : 8 + count] = stats_ref[1]
+    columns = tall[...].T
+    rows = lax.broadcasted_iota(jnp.int32, (tokens, tokens), 0)
+    cols = lax.broadcasted_iota(jnp.int32, (tokens, tokens), 1)
+    flat = [cols > rows] + [None] * (reach - 1) + [cols <= rows]
     biases = [jnp.where(pair >= hops - hop, 0.0, NEVER) for hop in range(hops)] + [None]
     for head in range(heads):
         for a in range(2):
+            at = 2 * head + a
             q, g = qg[a, 0, head], qg[a, 1, head]
-            at = 2 * head + a
-            lse, delta = stats_ref[0, at : at + 1, :], stats_ref[1, at : at + 1, :]
-            grad = None
-            for j in range(a, a + reach + 1):
-                key_block = kv[j, 0, head]
-                p, ds = score_grads(
-                    key_block, kv[j, 1, head], q, g, lse, delta,
-                    masks.get(a + reach - j), factor, scale, biases[j // 2],
-                )
-                term = dot(ds, key_block, TN)
-                grad = term if grad is None else grad + term
-                own = j - reach
-                if own >= 0:
-                    dk, dv = dot(ds, q, NN), dot(p.astype(BF16), g, NN)
-                    if a == own:
-                        part[own, 0, head], part[own, 1, head] = dk, dv
-                    if a > own:
-                        part[own, 0, head] += dk
-                        part[own, 1, head] += dv
-            dq[a, head] = grad.astype(BF16)
+            key_band = band(kv, a, reach + 1, 0, head)
+            s = dressed(
+                dot(q, key_band, NT), factor, 1, flat,
+                [biases[j // 2] for j in range(a, a + reach + 1)],
+            )
+            p = jnp.exp2(s - columns[:, at : at + 1])
+            dp = dot(g, band(kv, a, reach + 1, 1, head), NT)
+            ds = (p * (dp - columns[:, 8 + at : 9 + at]) * scale).astype(BF16)
+            dq[a, head] = dot(ds, key_band, NN).astype(BF16)
+        for b in range(2):
+            part[b, 0, head], part[b, 1, head] = key_grads(
+                kv[b + reach, 0, head], kv[b + reach, 1, head],
+                band(qg, b, 2 - b, 0, head), band(qg, b, 2 - b, 1, head),
+                stat_row([stats_ref], 0, head, b, 2 - b), stat_row([stats_ref], 1, head, b, 2 - b),
+                [block_mask(a - b, reach, tokens) for a in range(b, 2)], factor, scale,
+            )
     dq_mine[...] = dq[place]
     dq_theirs[...] = dq[1 - place]
 
@@ -183,22 +242,17 @@
     heads, tokens, width = kv.shape[2:]
     scale = width ** (-0.5)
     factor = scale * LOG2E
-    far = block_mask(reach, reach, tokens)
     for head in range(heads):
         for b in range(2):
-            dk, dv = part[b, 0, head], part[b, 1, head]
-            for a in range(2, b + reach + 1):
-                q, g = qg[a - 2, 0, head], qg[a - 2, 1, head]
-                source = stats[(a - 2) // 2]
-                at = 2 * head + a % 2
-                p, ds = score_grads(
-                    kv[b, 0, head], kv[b, 1, head], q, g,
-                    source[0, at : at + 1, :], source[1, at : at + 1, :],
-                    far if a - b == reach else None, factor, scale,
-                )
-                dk = dk + dot(ds, q, NN)
-                dv = dv + dot(p.astype(BF16), g, NN)
-            out[b, 0, head], out[b, 1, head] = dk.astype(BF16), dv.astype(BF16)
+            count = b + reach - 1
+            dk, dv = key_grads(
+                kv[b, 0, head], kv[b, 1, head],
+                band(qg, 0, count, 0, head), band(qg, 0, count, 1, head),
+                stat_row(stats, 0, head, 0, count), stat_row(stats, 1, head, 0, count),
+                [block_mask(2 + at - b, reach, tokens) for at in range(count)], factor, scale,
+            )
+            out[b, 0, head] = (part[b, 0, head] + dk).astype(BF16)
+            out[b, 1, head] = (part[b, 1, head] + dv).astype(BF16)
     mine[...] = out[place]
     theirs[...] = out[1 - place]
 
@@ -395,15 +449,19 @@
     kv_theirs = swapped(kv_give)
     qg_theirs = swapped(qg_give)
     keys = [(kv_mine, kv_theirs)]
-    rows = [(qg_mine, qg_theirs)]
     for _ in range(hops):
         keys.insert(0, tuple(moved(v, 2) for v in keys[0]))
-        rows.append(tuple(moved(v, -2) for v in rows[-1]))
-
+
+    gots = []
     far = None
     step = 1
     while step < members:
         got = moved(sent, -step)
+        gots.append(got)
+        if step == 2:
+            base = after(base, keys[-2][1])
+        if far is None:
+            base = after(base, keys[-2][0])
         ins = [base, got] if far is None else [base, far, got]
         far, sent = call(
             functools.partial(join_body, sets, far is None),
@@ -411,6 +469,28 @@
             ins, packed * width * 4, name="join",
         )
         step *= 2
+    rows = [(qg_mine, qg_theirs)]
+    source = (after(qg_mine, gots[0]), after(qg_theirs, gots[min(1, len(gots) - 1)]))
+    for _ in range(hops):
+        source = tuple(moved(v, -2) for v in source)
+        rows.append(source)
+    flat = [v for both in keys for v in both]
+    kv_space = pltpu.VMEM((2 * (hops + 1), 2, half, tokens, width), BF16)
+    qg_space = pltpu.VMEM((2, 2, half, tokens, width), BF16)
+    (early,) = call(
+        functools.partial(early_body, reach),
+        [shape((3, 2 * half, tokens), F32)],
+        [where, *flat[2:], qg_mine, qg_theirs],
+        4 * (reach - 1) * half * block, [kv_space, qg_space], smem=1, name="early",
+    )
+    (stats,) = call(
+        functools.partial(late_body, reach),
+        [shape((2, 2 * half, tokens), F32)],
+        [where, *flat[:2], qg_mine, qg_theirs, early],
+        6 * half * block, [qg_space, qg_space], smem=1, name="late",
+    )
+    later_stats = [moved(stats, -2 * (hop + 1)) for hop in range(hops)]
+    far = after(far, stats)
     du, grad_steps, gbc, sums = call(
         scan_body,
         [
@@ -433,20 +513,7 @@
     grad_bc = jnp.sum(
         gbc.reshape(lax.axis_size("head"), -1, 2 * NSTATE).astype(F32), axis=0
     )
-    spread = jnp.broadcast_to(sums[None], (members, *sums.shape))
-    summed = jnp.sum(lax.all_to_all(spread, "seq", 0, 0, tiled=True), axis=0)
-    grad_decay, grad_skip = summed[0, :sets], summed[1, :sets]
-
-    flat = [v for both in keys for v in both]
-    kv_space = pltpu.VMEM((2 * (hops + 1), 2, half, tokens, width), BF16)
-    qg_space = pltpu.VMEM((2, 2, half, tokens, width), BF16)
-    (stats,) = call(
-        functools.partial(stats_body, reach),
-        [shape((2, 2 * half, tokens), F32)],
-        [where, *flat, qg_mine, qg_theirs],
-        4 * (reach + 1) * half * block, [kv_space, qg_space], smem=1, name="stats",
-    )
-    later_stats = [moved(stats, -2 * (hop + 1)) for hop in range(hops)]
+
     dq_mine, dq_give, part = call(
         functools.partial(query_body, reach),
         [
@@ -455,7 +522,10 @@
         ],
         [where, *flat, qg_mine, qg_theirs, stats],
         6 * (reach + 1) * half * block,
-        [kv_space, qg_space, pltpu.VMEM((2, half, tokens, width), BF16)],
+        [
+            kv_space, qg_space, pltpu.VMEM((2, half, tokens, width), BF16),
+            pltpu.VMEM((16, tokens), F32),
+        ],
         smem=1, name="query",
     )
     dq_theirs = swapped(dq_give)
@@ -469,6 +539,11 @@
         smem=1, name="later",
     )
     dkv_theirs = swapped(dkv_give)
+
+    sums = after(sums, dkv_give)
+    spread = jnp.broadcast_to(sums[None], (members, *sums.shape))
+    summed = jnp.sum(lax.all_to_all(spread, "seq", 0, 0, tiled=True), axis=0)
+    grad_decay, grad_skip = summed[0, :sets], summed[1, :sets]
 
     def by_token(mine, theirs):
         first = jnp.where(place == 0, mine, theirs)

time: 127 us -> 106 us (0.83)
  waiting for transfers between devices: 43.6 us -> 21.7 us
  Pallas kernels: 29.9 us -> 26 us
  local copies, waits for them, and re-layouts: 3.11 us -> 5.57 us
  starting transfers between devices: 43.2 us -> 45.5 us
    ppermute x13, waiting for transfers between devices: 24.9 us -> 11.8 us  [moved(): return lax.ppermute(value, 'seq', pairs)]
    ppermute x4, waiting for transfers between devices: 10.7 us -> 3.99 us  [swapped(): return lax.ppermute(value, 'seq', [(at, at ^ 1) for at in range(count)])]
    ppermute x13, starting transfers between devices: 31.5 us -> 27.4 us  [moved(): return lax.ppermute(value, 'seq', pairs)]
    pallas_call x8 -> x9, Pallas kernels: 29.9 us -> 26 us  [call(): pl.pallas_call(body, out_shape=outs, in_specs=specs, out_specs=vmem(len(o...]
    all_to_all x1, starting transfers between devices: 3.34 us -> 6.89 us  [shards(): summed = jnp.sum(lax.all_to_all(spread, 'seq', 0, 0, tiled=True), axis=0)]
    ppermute x4, starting transfers between devices: 5.11 us -> 7.73 us  [swapped(): return lax.ppermute(value, 'seq', [(at, at ^ 1) for at in range(count)])]
    unnamed x20 -> x34, local copies, waits for them, and re-layouts: 1.97 us -> 4.43 us
    all_to_all x1, waiting for transfers between devices: 2.01 us -> 0.01 us  [shards(): gbc = lax.all_to_all(gbc, 'head', 0, 0, tiled=True)]
  transfers between devices with their start and end apart: 19 -> 19, of which waited for: 7 -> 6; matrix products, arithmetic and copies ran while one was open for 3% -> 4% of each run, Pallas kernels for 24% -> 25%
where the time goes in v2:
time: 106 us
  starting transfers between devices  45.5 us (43%)
  Pallas kernels  26 us (25%)
  waiting for transfers between devices  21.7 us (20%)
  other arithmetic  5.77 us (5%)
  local copies, waits for them, and re-layouts  5.57 us (5%)
    ppermute x13, starting transfers between devices, moved(): return lax.ppermute(value, 'seq', pairs)  27.4 us
    pallas_call x9, Pallas kernels, call(): pl.pallas_call(body, out_shape=outs, in_specs=specs, out_specs=vmem(len(o...  26 us
    ppermute x13, waiting for transfers between devices, moved(): return lax.ppermute(value, 'seq', pairs)  11.8 us
    ppermute x4, starting transfers between devices, swapped(): return lax.ppermute(value, 'seq', [(at, at ^ 1) for at in range(count)])  7.73 us
    all_to_all x1, starting transfers between devices, shards(): summed = jnp.sum(lax.all_to_all(spread, 'seq', 0, 0, tiled=True), axis=0)  6.89 us
    all_to_all x1, waiting for transfers between devices, shards(): summed = jnp.sum(lax.all_to_all(spread, 'seq', 0, 0, tiled=True), axis=0)  5.9 us
    unnamed x34, local copies, waits for them, and re-layouts  4.43 us
    ppermute x4, waiting for transfers between devices, swapped(): return lax.ppermute(value, 'seq', [(at, at ^ 1) for at in range(count)])  3.99 us
  transfers between devices with their start and end apart: 19, of which 6 were waited for; matrix products, arithmetic and copies ran while one was open for 4% of the time, Pallas kernels for 25%

profile of v2, /device:TPU:0, one launch (start us, length us, event | category | flops | bytes accessed | tf_op | source)
XLA Modules:
  0.0 105.7 jit_solution(13392242287548372848)
XLA Ops:
  0.7 0.0 copy-start.4
  0.7 2.1 %fusion.5 = (bf16[2,3,256,128]{3,2,1,0:T(8,128)(2,1)}, bf16[2,3,256,128]{3,2,1,0:T(8,128)(2,1)S(1)}) fusion(s32[]{:T(128)S(6)} %select_n.65, bf16[1,256,6,128]{3,1,2,0:T(8,128)(2,1)} %bitcast.41, bf16[1,256,6,128]{3,1,2,0:T(8,128)(2,1)} %bitcast.42, s32[]{:T(128)S(6)} %select_n.64), kind=kLoop, calls=%fused_computation.13 | loop fusion | flops 393216 | bytes 1572872 | tf_op jit(solution)/shard_map/dynamic_slice | solution.py:444
  2.8 2.9 %collective-permute-start.2 = (bf16[2,3,256,128]{3,2,1,0:T(8,128)(2,1)}, bf16[2,3,256,128]{3,2,1,0:T(8,128)(2,1)S(1)}, u32[]{:S(2)}, u32[]{:S(2)}) collective-permute-start(bf16[2,3,256,128]{3,2,1,0:T(8,128)(2,1)} %get-tuple-element.78), channel_id=1, source_target_pairs={{0,4},{4,0},{8,12},{12,8},{16,20},{20,16},{24,28},{28,24},{1,5},{5... | collective-permute-start | bytes 1179656 | tf_op jit(solution)/shard_map/ppermute | solution.py:40
  5.8 4.2 %collective-permute-start = (bf16[2,3,256,128]{3,2,1,0:T(8,128)(2,1)S(1)}, bf16[2,3,256,128]{3,2,1,0:T(8,128)(2,1)}, u32[]{:S(2)}, u32[]{:S(2)}) collective-permute-start(bf16[2,3,256,128]{3,2,1,0:T(8,128)(2,1)S(1)} %get-tuple-element.79.refs_3_.refs_5_.refs_1_), channel_id=1, source_target_pairs={{0,8},{4,12},{8,16},{12,20},{16,24},{20,28},{1,9},{5,13},{9,17},{1... | collective-permute-start | bytes 1179656 | tf_op jit(solution)/shard_map/ppermute | solution.py:35
  10.0 0.1 copy.22.dt_ref
  10.1 2.2 %summary.1 = (f32[784,128]{1,0:T(8,128)S(1)}, bf16[784,128]{1,0:T(8,128)(2,1)S(1)}, f32[256,128]{1,0:T(8,128)S(1)}, f32[16,256]{1,0:T(8,128)S(1)}) custom-call(f32[12]{0:T(128)S(1)} %copy-done.6, bf16[12,256,128]{2,1,0:T(8,128)(2,1)S(1)} %bitcast.37, f32[256,12]{1,0:T(8,128)S(1)} %copy.22.dt_ref, bf16[256,128]{1,0:T(8,128)(2,1)S(1)} %copy-done.4), custom_call_target="tpu_custom_call" | custom-call | flops 100663296 | bytes 1613872 | tf_op jit(solution)/shard_map/summary/pallas_call | solution.py:54
  12.3 0.0 copy-start.9
  12.4 1.3 %collective-permute-start.7 = (bf16[784,128]{1,0:T(8,128)(2,1)S(1)}, bf16[784,128]{1,0:T(8,128)(2,1)S(1)}, u32[]{:S(2)}, u32[]{:S(2)}) collective-permute-start(bf16[784,128]{1,0:T(8,128)(2,1)S(1)} %get-tuple-element.34), channel_id=1, source_target_pairs={{4,0},{8,4},{12,8},{16,12},{20,16},{24,20},{28,24},{5,1},{9,5},{13... | collective-permute-start | bytes 602120 | tf_op jit(solution)/shard_map/ppermute | solution.py:35
  13.7 1.1 %fusion.1 = (bf16[2,3,256,128]{3,2,1,0:T(8,128)(2,1)S(1)}, bf16[2,3,256,128]{3,2,1,0:T(8,128)(2,1)S(1)}) fusion(s32[]{:T(128)S(6)} %select_n.65, bf16[1,256,6,128]{3,1,2,0:T(8,128)(2,1)S(1)} %bitcast.43, bf16[1,256,6,128]{3,1,2,0:T(8,128)(2,1)} %bitcast.44, s32[]{:T(128)S(6)} %select_n.64), kind=kLoop, calls=%fused_computation.9 | loop fusion | flops 393216 | bytes 1572872 | tf_op jit(solution)/shard_map/dynamic_slice | solution.py:444
  14.8 2.7 %collective-permute-start.5 = (bf16[2,3,256,128]{3,2,1,0:T(8,128)(2,1)S(1)}, bf16[2,3,256,128]{3,2,1,0:T(8,128)(2,1)S(1)}, u32[]{:S(2)}, u32[]{:S(2)}) collective-permute-start(bf16[2,3,256,128]{3,2,1,0:T(8,128)(2,1)S(1)} %get-tuple-element.76), channel_id=1, source_target_pairs={{0,4},{4,0},{8,12},{12,8},{16,20},{20,16},{24,28},{28,24},{1,5},{5... | collective-permute-start | bytes 1179656 | tf_op jit(solution)/shard_map/ppermute | solution.py:40
  17.5 0.0 collective-permute-done.2.refs_4_.refs_6_.refs_2_
  17.5 3.5 %collective-permute-start.3 = (bf16[2,3,256,128]{3,2,1,0:T(8,128)(2,1)S(1)}, bf16[2,3,256,128]{3,2,1,0:T(8,128)(2,1)}, u32[]{:S(2)}, u32[]{:S(2)}) collective-permute-start(bf16[2,3,256,128]{3,2,1,0:T(8,128)(2,1)S(1)} %collective-permute-done.2.refs_4_.refs_6_.refs_2_), channel_id=1, source_target_pairs={{0,8},{4,12},{8,16},{12,20},{16,24},{20,28},{1,9},{5,13},{9,17},{1... | collective-permute-start | bytes 1179656 | tf_op jit(solution)/shard_map/ppermute | solution.py:35
  21.0 0.0 collective-permute-done.refs_1_.refs_3_
  21.0 1.2 %collective-permute-done.7.refs_0_ = bf16[784,128]{1,0:T(8,128)(2,1)S(1)} collective-permute-done((bf16[784,128]{1,0:T(8,128)(2,1)S(1)}, bf16[784,128]{1,0:T(8,128)(2,1)S(1)}, u32[]{:S(2)}, u32[]{:S(2)}) %collective-permute-start.7) | collective-permute-done | bytes 200736 | tf_op jit(solution)/shard_map/ppermute | solution.py:35
  22.2 0.1 join.3
  22.3 1.3 %collective-permute-start.9 = (bf16[784,128]{1,0:T(8,128)(2,1)S(1)}, bf16[784,128]{1,0:T(8,128)(2,1)S(1)}, u32[]{:S(2)}, u32[]{:S(2)}) collective-permute-start(bf16[784,128]{1,0:T(8,128)(2,1)S(1)} %get-tuple-element.38), channel_id=1, source_target_pairs={{8,0},{12,4},{16,8},{20,12},{24,16},{28,20},{9,1},{13,5},{17,9},{2... | collective-permute-start | bytes 602120 | tf_op jit(solution)/shard_map/ppermute | solution.py:35
  23.6 1.3 %collective-permute-start.8 = (bf16[2,3,256,128]{3,2,1,0:T(8,128)(2,1)S(1)}, bf16[2,3,256,128]{3,2,1,0:T(8,128)(2,1)}, u32[]{:S(2)}, u32[]{:S(2)}) collective-permute-start(bf16[2,3,256,128]{3,2,1,0:T(8,128)(2,1)S(1)} %get-tuple-element.35.refs_5_.refs_3_.refs_7_), channel_id=1, source_target_pairs={{8,0},{12,4},{16,8},{20,12},{24,16},{28,20},{9,1},{13,5},{17,9},{2... | collective-permute-start | bytes 1179656 | tf_op jit(solution)/shard_map/ppermute | solution.py:35
  24.9 4.0 %collective-permute-done.5.refs_6_.refs_4_.refs_8_ = bf16[2,3,256,128]{3,2,1,0:T(8,128)(2,1)S(1)} collective-permute-done((bf16[2,3,256,128]{3,2,1,0:T(8,128)(2,1)S(1)}, bf16[2,3,256,128]{3,2,1,0:T(8,128)(2,1)S(1)}, u32[]{:S(2)}, u32[]{:S(2)}) %collective-permute-start.5) | collective-permute-done | bytes 393248 | tf_op jit(solution)/shard_map/ppermute | solution.py:40
  28.8 3.2 %collective-permute-done.9.refs_1_ = bf16[784,128]{1,0:T(8,128)(2,1)S(1)} collective-permute-done((bf16[784,128]{1,0:T(8,128)(2,1)S(1)}, bf16[784,128]{1,0:T(8,128)(2,1)S(1)}, u32[]{:S(2)}, u32[]{:S(2)}) %collective-permute-start.9) | collective-permute-done | bytes 200736 | tf_op jit(solution)/shard_map/ppermute | solution.py:35
  32.1 1.3 %collective-permute-start.10 = (bf16[2,3,256,128]{3,2,1,0:T(8,128)(2,1)S(1)}, bf16[2,3,256,128]{3,2,1,0:T(8,128)(2,1)}, u32[]{:S(2)}, u32[]{:S(2)}) collective-permute-start(bf16[2,3,256,128]{3,2,1,0:T(8,128)(2,1)S(1)} %collective-permute-done.5.refs_6_.refs_4_.refs_8_), channel_id=1, source_target_pairs={{8,0},{12,4},{16,8},{20,12},{24,16},{28,20},{9,1},{13,5},{17,9},{2... | collective-permute-start | bytes 1179656 | tf_op jit(solution)/shard_map/ppermute | solution.py:35
  33.4 4.6 %collective-permute-start.1 = (bf16[2,3,256,128]{3,2,1,0:T(8,128)(2,1)}, bf16[2,3,256,128]{3,2,1,0:T(8,128)(2,1)S(1)}, u32[]{:S(2)}, u32[]{:S(2)}) collective-permute-start(bf16[2,3,256,128]{3,2,1,0:T(8,128)(2,1)} %collective-permute-done.refs_1_.refs_3_), channel_id=1, source_target_pairs={{0,8},{4,12},{8,16},{12,20},{16,24},{20,28},{1,9},{5,13},{9,17},{1... | collective-permute-start | bytes 1179656 | tf_op jit(solution)/shard_map/ppermute | solution.py:35
  38.0 0.0 collective-permute-done.3.refs_2_.refs_4_
  38.0 3.4 %collective-permute-start.4 = (bf16[2,3,256,128]{3,2,1,0:T(8,128)(2,1)}, bf16[2,3,256,128]{3,2,1,0:T(8,128)(2,1)}, u32[]{:S(2)}, u32[]{:S(2)}) collective-permute-start(bf16[2,3,256,128]{3,2,1,0:T(8,128)(2,1)} %collective-permute-done.3.refs_2_.refs_4_), channel_id=1, source_target_pairs={{0,8},{4,12},{8,16},{12,20},{16,24},{20,28},{1,9},{5,13},{9,17},{1... | collective-permute-start | bytes 1179656 | tf_op jit(solution)/shard_map/ppermute | solution.py:35
  41.4 0.8 join.4
  42.1 1.3 %collective-permute-start.16 = (bf16[784,128]{1,0:T(8,128)(2,1)}, bf16[784,128]{1,0:T(8,128)(2,1)S(1)}, u32[]{:S(2)}, u32[]{:S(2)}) collective-permute-start(bf16[784,128]{1,0:T(8,128)(2,1)} %get-tuple-element.46), channel_id=1, source_target_pairs={{16,0},{20,4},{24,8},{28,12},{17,1},{21,5},{25,9},{29,13},{18,2},{... | collective-permute-start | bytes 602120 | tf_op jit(solution)/shard_map/ppermute | solution.py:35
  43.4 0.1 pad_add_fusion.refs_0_
  43.5 1.3 %collective-permute-start.11 = (bf16[2,3,256,128]{3,2,1,0:T(8,128)(2,1)}, bf16[2,3,256,128]{3,2,1,0:T(8,128)(2,1)}, u32[]{:S(2)}, u32[]{:S(2)}) collective-permute-start(bf16[2,3,256,128]{3,2,1,0:T(8,128)(2,1)} %collective-permute-done.8.refs_3_), channel_id=1, source_target_pairs={{8,0},{12,4},{16,8},{20,12},{24,16},{28,20},{9,1},{13,5},{17,9},{2... | collective-permute-start | bytes 1179656 | tf_op jit(solution)/shard_map/ppermute | solution.py:35
  44.8 4.3 %collective-permute-done.10.refs_4_ = bf16[2,3,256,128]{3,2,1,0:T(8,128)(2,1)} collective-permute-done((bf16[2,3,256,128]{3,2,1,0:T(8,128)(2,1)S(1)}, bf16[2,3,256,128]{3,2,1,0:T(8,128)(2,1)}, u32[]{:S(2)}, u32[]{:S(2)}) %collective-permute-start.10) | collective-permute-done | bytes 393248 | tf_op jit(solution)/shard_map/ppermute | solution.py:35
  49.1 1.3 %collective-permute-start.12 = (bf16[2,3,256,128]{3,2,1,0:T(8,128)(2,1)}, bf16[2,3,256,128]{3,2,1,0:T(8,128)(2,1)}, u32[]{:S(2)}, u32[]{:S(2)}) collective-permute-start(bf16[2,3,256,128]{3,2,1,0:T(8,128)(2,1)} %collective-permute-done.10.refs_4_), channel_id=1, source_target_pairs={{8,0},{12,4},{16,8},{20,12},{24,16},{28,20},{9,1},{13,5},{17,9},{2... | collective-permute-start | bytes 1179656 | tf_op jit(solution)/shard_map/ppermute | solution.py:35
  50.4 0.0 copy-start.2
  50.4 1.0 copy-done.2
  51.4 3.2 %early.1.refs_5_ = f32[3,6,256]{2,1,0:T(8,128)S(1)} custom-call(s32[2]{0:T(128)S(1)} %pad_add_fusion.refs_0_, bf16[2,3,256,128]{3,2,1,0:T(8,128)(2,1)} %collective-permute-done.refs_1_.refs_3_, bf16[2,3,256,128]{3,2,1,0:T(8,128)(2,1)} %collective-permute-done.3.refs_2_.refs_4_, bf16[2,3,256,128]{3,2,1,0:T(8,128)(2,1)S(1)} %get-tuple-element.79.refs_3_.refs_5_.refs_1_, ...), custom_call_target="tpu_custom_call" | custom-call | flops 603979776 | bytes 2377736 | tf_op jit(solution)/shard_map/early/pallas_call | solution.py:54
  54.6 0.0 copy-start.5
  54.6 0.0 copy-start.7
  54.6 0.0 copy-start.8
  54.6 0.0 copy-start.10
  54.6 0.0 copy-start.11
  54.6 3.1 %collective-permute-done.16.refs_1_ = bf16[784,128]{1,0:T(8,128)(2,1)S(1)} collective-permute-done((bf16[784,128]{1,0:T(8,128)(2,1)}, bf16[784,128]{1,0:T(8,128)(2,1)S(1)}, u32[]{:S(2)}, u32[]{:S(2)}) %collective-permute-start.16) | collective-permute-done | bytes 200736 | tf_op jit(solution)/shard_map/ppermute | solution.py:35
  57.7 0.8 join.5
  58.5 0.0 collective-permute-done.1.refs_1_
  58.5 2.1 %late.1.refs_9_ = f32[2,6,256]{2,1,0:T(8,128)S(1)} custom-call(s32[2]{0:T(128)S(1)} %pad_add_fusion.refs_0_, bf16[2,3,256,128]{3,2,1,0:T(8,128)(2,1)S(1)} %collective-permute-done.1.refs_1_, bf16[2,3,256,128]{3,2,1,0:T(8,128)(2,1)} %collective-permute-done.4.refs_2_, bf16[2,3,256,128]{3,2,1,0:T(8,128)(2,1)S(1)} %get-tuple-element.35.refs_5_.refs_3_.refs_7_, ...), custom_call_target="tpu_custom_call" | custom-call | flops 301989888 | bytes 1603592 | tf_op jit(solution)/shard_map/late/pallas_call | solution.py:54
  60.6 0.0 copy-start.3
  60.6 1.4 %collective-permute-start.13 = (f32[2,6,256]{2,1,0:T(8,128)S(1)}, f32[2,6,256]{2,1,0:T(8,128)S(1)}, u32[]{:S(2)}, u32[]{:S(2)}) collective-permute-start(f32[2,6,256]{2,1,0:T(8,128)S(1)} %late.1.refs_9_), channel_id=1, source_target_pairs={{8,0},{12,4},{16,8},{20,12},{24,16},{28,20},{9,1},{13,5},{17,9},{2... | collective-permute-start | bytes 36872 | tf_op jit(solution)/shard_map/ppermute | solution.py:35
  62.0 1.3 %collective-permute-start.14 = (f32[2,6,256]{2,1,0:T(8,128)S(1)}, f32[2,6,256]{2,1,0:T(8,128)S(1)}, u32[]{:S(2)}, u32[]{:S(2)}) collective-permute-start(f32[2,6,256]{2,1,0:T(8,128)S(1)} %late.1.refs_9_), channel_id=1, source_target_pairs={{16,0},{20,4},{24,8},{28,12},{17,1},{21,5},{25,9},{29,13},{18,2},{... | collective-permute-start | bytes 36872 | tf_op jit(solution)/shard_map/ppermute | solution.py:35
  63.4 5.7 %scan.1 = (bf16[12,256,128]{2,1,0:T(8,128)(2,1)}, f32[256,12]{1,0:T(8,128)S(1)}, bf16[256,128]{1,0:T(8,128)(2,1)}, f32[8,128]{1,0:T(8,128)S(1)}) custom-call(f32[12]{0:T(128)S(1)} %copy-done.6, f32[12]{0:T(128)S(1)} %copy-done.11, bf16[12,256,128]{2,1,0:T(8,128)(2,1)S(1)} %bitcast.39, bf16[12,256,128]{2,1,0:T(8,128)(2,1)S(1)} %bitcast.38, ...), custom_call_target="tpu_custom_call" | custom-call | flops 805306368 | bytes 3461216 | tf_op jit(solution)/shard_map/scan/pallas_call | solution.py:54
  69.0 3.5 %all-to-all-start = ((bf16[4,64,128]{2,1,0:T(8,128)(2,1)}), bf16[4,64,128]{2,1,0:T(8,128)(2,1)S(1)}, u32[]{:S(2)}, u32[]{:S(2)}) async-start(bf16[4,64,128]{2,1,0:T(8,128)(2,1)} %bitcast.21), calls=%async_computation | async-start | bytes 131072 | tf_op jit(solution)/shard_map/all_to_all | solution.py:512
  72.5 6.6 %query.1 = (bf16[3,256,128]{2,1,0:T(8,128)(2,1)S(1)}, bf16[3,256,128]{2,1,0:T(8,128)(2,1)S(1)}, f32[2,2,3,256,128]{4,3,2,1,0:T(8,128)S(1)}) custom-call(s32[2]{0:T(128)S(1)} %pad_add_fusion.refs_0_, bf16[2,3,256,128]{3,2,1,0:T(8,128)(2,1)S(1)} %collective-permute-done.1.refs_1_, bf16[2,3,256,128]{3,2,1,0:T(8,128)(2,1)} %collective-permute-done.4.refs_2_, ...), custom_call_target="tpu_custom_call" | custom-call | flops 1509949440 | bytes 5124104 | tf_op jit(solution)/shard_map/query/pallas_call | solution.py:54
  79.1 1.2 %copy-done.12 = f32[2,2,3,256,128]{4,3,2,1,0:T(8,128)} copy-done((f32[2,2,3,256,128]{4,3,2,1,0:T(8,128)}, f32[2,2,3,256,128]{4,3,2,1,0:T(8,128)S(1)}, u32[]{:S(2)}) %copy-start.12) | copy-done | bytes 1572888
  80.3 0.7 copy.24
  81.0 0.0 all-to-all-done
  81.0 0.6 convert_reduce_fusion
  81.6 0.0 collective-permute-done.11.refs_5_
  81.6 0.0 collective-permute-done.13.refs_7_
  81.6 0.0 collective-permute-done.14.refs_8_
  81.6 1.4 %copy-done.13 = f32[2,2,3,256,128]{4,3,2,1,0:T(8,128)S(1)} copy-done((f32[2,2,3,256,128]{4,3,2,1,0:T(8,128)S(1)}, f32[2,2,3,256,128]{4,3,2,1,0:T(8,128)}, u32[]{:S(2)}) %copy-start.13) | copy-done | bytes 1572888
  83.0 4.7 %later.1 = (bf16[2,3,256,128]{3,2,1,0:T(8,128)(2,1)S(1)}, bf16[2,3,256,128]{3,2,1,0:T(8,128)(2,1)S(1)}) custom-call(s32[2]{0:T(128)S(1)} %pad_add_fusion.refs_0_, bf16[2,3,256,128]{3,2,1,0:T(8,128)(2,1)S(1)} %get-tuple-element.79.refs_3_.refs_5_.refs_1_, bf16[2,3,256,128]{3,2,1,0:T(8,128)(2,1)S(1)} %copy-done.3, ...), custom_call_target="tpu_custom_call" | custom-call | flops 1610612736 | bytes 4743176 | tf_op jit(solution)/shard_map/later/pallas_call | solution.py:54
  87.8 2.1 %collective-permute-start.15 = (bf16[2,3,256,128]{3,2,1,0:T(8,128)(2,1)S(1)}, bf16[2,3,256,128]{3,2,1,0:T(8,128)(2,1)S(1)}, u32[]{:S(2)}, u32[]{:S(2)}) collective-permute-start(bf16[2,3,256,128]{3,2,1,0:T(8,128)(2,1)S(1)} %get-tuple-element.42), channel_id=1, source_target_pairs={{0,4},{4,0},{8,12},{12,8},{16,20},{20,16},{24,28},{28,24},{1,5},{5... | collective-permute-start | bytes 1179656 | tf_op jit(solution)/shard_map/ppermute | solution.py:40
  89.9 0.6 broadcast_in_dim.2
  90.5 6.9 %all-to-all-start.1 = ((f32[8,8,128]{2,1,0:T(8,128)}), f32[8,8,128]{2,1,0:T(8,128)S(1)}, u32[]{:S(2)}, u32[]{:S(2)}) async-start(f32[8,8,128]{2,1,0:T(8,128)} %broadcast_in_dim.2), calls=%async_computation.1 | async-start | bytes 65536 | tf_op jit(solution)/shard_map/all_to_all | solution.py:545
  97.4 0.8 maximum_bitcast_fusion
  98.2 5.9 %all-to-all-done.1 = f32[8,8,128]{2,1,0:T(8,128)S(1)} async-done(((f32[8,8,128]{2,1,0:T(8,128)}), f32[8,8,128]{2,1,0:T(8,128)S(1)}, u32[]{:S(2)}, u32[]{:S(2)}) %all-to-all-start.1) | async-done | bytes 32800 | tf_op jit(solution)/shard_map/all_to_all | solution.py:545
  104.1 0.5 slice_bitcast_fusion
  104.6 0.1 select_bitcast_fusion.1
  104.7 0.9 maximum_bitcast_fusion.1
  (28 shorter events, 0.1 us)
Async XLA Ops:
  0.6 9.4 %copy-start.15 = (f32[256,12]{0,1:T(8,128)S(1)}, f32[256,12]{0,1:T(8,128)}, u32[]{:S(2)}) copy-start(f32[256,12]{0,1:T(8,128)} %param.17) | copy-start | bytes 36868
  0.6 9.5 %copy-start.6 = (f32[12]{0:T(128)S(1)}, f32[12]{0:T(128)}, u32[]{:S(2)}) copy-start(f32[12]{0:T(128)} %rates_ref.3) | copy-start | bytes 148
  0.7 9.5 %copy-start = (bf16[256,12,128]{2,0,1:T(8,128)(2,1)S(1)}, bf16[256,12,128]{2,0,1:T(8,128)(2,1)}, u32[]{:S(2)}) copy-start(bf16[256,12,128]{2,0,1:T(8,128)(2,1)} %param.16) | copy-start | bytes 2359300
  0.7 9.5 %copy-start.4 = (bf16[256,128]{1,0:T(8,128)(2,1)S(1)}, bf16[256,128]{1,0:T(8,128)(2,1)}, u32[]{:S(2)}) copy-start(bf16[256,128]{1,0:T(8,128)(2,1)} %bc_ref.3) | copy-start | bytes 196612
  0.7 13.0 %copy-start.14 = (bf16[256,6,128]{2,0,1:T(8,128)(2,1)S(1)}, bf16[256,6,128]{2,0,1:T(8,128)(2,1)}, u32[]{:S(2)}) copy-start(bf16[256,6,128]{2,0,1:T(8,128)(2,1)} %param.11) | copy-start | bytes 1179652
  2.8 14.6 %collective-permute-start.2 = (bf16[2,3,256,128]{3,2,1,0:T(8,128)(2,1)}, bf16[2,3,256,128]{3,2,1,0:T(8,128)(2,1)S(1)}, u32[]{:S(2)}, u32[]{:S(2)}) collective-permute-start(bf16[2,3,256,128]{3,2,1,0:T(8,128)(2,1)} %get-tuple-element.78), channel_id=1, source_target_pairs={{0,4},{4,0},{8,12},{12,8},{16,20},{20,16},{24,28},{28,24},{1,5},{5... | collective-permute-start | bytes 1179656 | tf_op jit(solution)/shard_map/ppermute | solution.py:40
  5.8 15.2 %collective-permute-start = (bf16[2,3,256,128]{3,2,1,0:T(8,128)(2,1)S(1)}, bf16[2,3,256,128]{3,2,1,0:T(8,128)(2,1)}, u32[]{:S(2)}, u32[]{:S(2)}) collective-permute-start(bf16[2,3,256,128]{3,2,1,0:T(8,128)(2,1)S(1)} %get-tuple-element.79.refs_3_.refs_5_.refs_1_), channel_id=1, source_target_pairs={{0,8},{4,12},{8,16},{12,20},{16,24},{20,28},{1,9},{5,13},{9,17},{1... | collective-permute-start | bytes 1179656 | tf_op jit(solution)/shard_map/ppermute | solution.py:35
  12.3 19.7 %copy-start.9 = (f32[256,128]{1,0:T(8,128)}, f32[256,128]{1,0:T(8,128)S(1)}, u32[]{:S(2)}) copy-start(f32[256,128]{1,0:T(8,128)S(1)} %get-tuple-element.49.cum_ref) | copy-start | bytes 393220
  12.4 9.8 %collective-permute-start.7 = (bf16[784,128]{1,0:T(8,128)(2,1)S(1)}, bf16[784,128]{1,0:T(8,128)(2,1)S(1)}, u32[]{:S(2)}, u32[]{:S(2)}) collective-permute-start(bf16[784,128]{1,0:T(8,128)(2,1)S(1)} %get-tuple-element.34), channel_id=1, source_target_pairs={{4,0},{8,4},{12,8},{16,12},{20,16},{24,20},{28,24},{5,1},{9,5},{13... | collective-permute-start | bytes 602120 | tf_op jit(solution)/shard_map/ppermute | solution.py:35
  14.8 14.1 %collective-permute-start.5 = (bf16[2,3,256,128]{3,2,1,0:T(8,128)(2,1)S(1)}, bf16[2,3,256,128]{3,2,1,0:T(8,128)(2,1)S(1)}, u32[]{:S(2)}, u32[]{:S(2)}) collective-permute-start(bf16[2,3,256,128]{3,2,1,0:T(8,128)(2,1)S(1)} %get-tuple-element.76), channel_id=1, source_target_pairs={{0,4},{4,0},{8,12},{12,8},{16,20},{20,16},{24,28},{28,24},{1,5},{5... | collective-permute-start | bytes 1179656 | tf_op jit(solution)/shard_map/ppermute | solution.py:40
  17.5 23.9 %copy-start.1 = (bf16[2,3,256,128]{3,2,1,0:T(8,128)(2,1)}, bf16[2,3,256,128]{3,2,1,0:T(8,128)(2,1)S(1)}, u32[]{:S(2)}) copy-start(bf16[2,3,256,128]{3,2,1,0:T(8,128)(2,1)S(1)} %collective-permute-done.2.refs_4_.refs_6_.refs_2_) | copy-start | bytes 1179652
  17.5 20.5 %collective-permute-start.3 = (bf16[2,3,256,128]{3,2,1,0:T(8,128)(2,1)S(1)}, bf16[2,3,256,128]{3,2,1,0:T(8,128)(2,1)}, u32[]{:S(2)}, u32[]{:S(2)}) collective-permute-start(bf16[2,3,256,128]{3,2,1,0:T(8,128)(2,1)S(1)} %collective-permute-done.2.refs_4_.refs_6_.refs_2_), channel_id=1, source_target_pairs={{0,8},{4,12},{8,16},{12,20},{16,24},{20,28},{1,9},{5,13},{9,17},{1... | collective-permute-start | bytes 1179656 | tf_op jit(solution)/shard_map/ppermute | solution.py:35
  22.3 9.8 %collective-permute-start.9 = (bf16[784,128]{1,0:T(8,128)(2,1)S(1)}, bf16[784,128]{1,0:T(8,128)(2,1)S(1)}, u32[]{:S(2)}, u32[]{:S(2)}) collective-permute-start(bf16[784,128]{1,0:T(8,128)(2,1)S(1)} %get-tuple-element.38), channel_id=1, source_target_pairs={{8,0},{12,4},{16,8},{20,12},{24,16},{28,20},{9,1},{13,5},{17,9},{2... | collective-permute-start | bytes 602120 | tf_op jit(solution)/shard_map/ppermute | solution.py:35
  23.6 20.0 %collective-permute-start.8 = (bf16[2,3,256,128]{3,2,1,0:T(8,128)(2,1)S(1)}, bf16[2,3,256,128]{3,2,1,0:T(8,128)(2,1)}, u32[]{:S(2)}, u32[]{:S(2)}) collective-permute-start(bf16[2,3,256,128]{3,2,1,0:T(8,128)(2,1)S(1)} %get-tuple-element.35.refs_5_.refs_3_.refs_7_), channel_id=1, source_target_pairs={{8,0},{12,4},{16,8},{20,12},{24,16},{28,20},{9,1},{13,5},{17,9},{2... | collective-permute-start | bytes 1179656 | tf_op jit(solution)/shard_map/ppermute | solution.py:35
  32.1 17.0 %collective-permute-start.10 = (bf16[2,3,256,128]{3,2,1,0:T(8,128)(2,1)S(1)}, bf16[2,3,256,128]{3,2,1,0:T(8,128)(2,1)}, u32[]{:S(2)}, u32[]{:S(2)}) collective-permute-start(bf16[2,3,256,128]{3,2,1,0:T(8,128)(2,1)S(1)} %collective-permute-done.5.refs_6_.refs_4_.refs_8_), channel_id=1, source_target_pairs={{8,0},{12,4},{16,8},{20,12},{24,16},{28,20},{9,1},{13,5},{17,9},{2... | collective-permute-start | bytes 1179656 | tf_op jit(solution)/shard_map/ppermute | solution.py:35
  33.4 25.1 %collective-permute-start.1 = (bf16[2,3,256,128]{3,2,1,0:T(8,128)(2,1)}, bf16[2,3,256,128]{3,2,1,0:T(8,128)(2,1)S(1)}, u32[]{:S(2)}, u32[]{:S(2)}) collective-permute-start(bf16[2,3,256,128]{3,2,1,0:T(8,128)(2,1)} %collective-permute-done.refs_1_.refs_3_), channel_id=1, source_target_pairs={{0,8},{4,12},{8,16},{12,20},{16,24},{20,28},{1,9},{5,13},{9,17},{1... | collective-permute-start | bytes 1179656 | tf_op jit(solution)/shard_map/ppermute | solution.py:35
  38.0 20.5 %collective-permute-start.4 = (bf16[2,3,256,128]{3,2,1,0:T(8,128)(2,1)}, bf16[2,3,256,128]{3,2,1,0:T(8,128)(2,1)}, u32[]{:S(2)}, u32[]{:S(2)}) collective-permute-start(bf16[2,3,256,128]{3,2,1,0:T(8,128)(2,1)} %collective-permute-done.3.refs_2_.refs_4_), channel_id=1, source_target_pairs={{0,8},{4,12},{8,16},{12,20},{16,24},{20,28},{1,9},{5,13},{9,17},{1... | collective-permute-start | bytes 1179656 | tf_op jit(solution)/shard_map/ppermute | solution.py:35
  42.1 15.6 %collective-permute-start.16 = (bf16[784,128]{1,0:T(8,128)(2,1)}, bf16[784,128]{1,0:T(8,128)(2,1)S(1)}, u32[]{:S(2)}, u32[]{:S(2)}) collective-permute-start(bf16[784,128]{1,0:T(8,128)(2,1)} %get-tuple-element.46), channel_id=1, source_target_pairs={{16,0},{20,4},{24,8},{28,12},{17,1},{21,5},{25,9},{29,13},{18,2},{... | collective-permute-start | bytes 602120 | tf_op jit(solution)/shard_map/ppermute | solution.py:35
  43.5 38.1 %collective-permute-start.11 = (bf16[2,3,256,128]{3,2,1,0:T(8,128)(2,1)}, bf16[2,3,256,128]{3,2,1,0:T(8,128)(2,1)}, u32[]{:S(2)}, u32[]{:S(2)}) collective-permute-start(bf16[2,3,256,128]{3,2,1,0:T(8,128)(2,1)} %collective-permute-done.8.refs_3_), channel_id=1, source_target_pairs={{8,0},{12,4},{16,8},{20,12},{24,16},{28,20},{9,1},{13,5},{17,9},{2... | collective-permute-start | bytes 1179656 | tf_op jit(solution)/shard_map/ppermute | solution.py:35
  49.1 32.5 %collective-permute-start.12 = (bf16[2,3,256,128]{3,2,1,0:T(8,128)(2,1)}, bf16[2,3,256,128]{3,2,1,0:T(8,128)(2,1)}, u32[]{:S(2)}, u32[]{:S(2)}) collective-permute-start(bf16[2,3,256,128]{3,2,1,0:T(8,128)(2,1)} %collective-permute-done.10.refs_4_), channel_id=1, source_target_pairs={{8,0},{12,4},{16,8},{20,12},{24,16},{28,20},{9,1},{13,5},{17,9},{2... | collective-permute-start | bytes 1179656 | tf_op jit(solution)/shard_map/ppermute | solution.py:35
  50.4 1.0 copy-start.2
  54.6 8.7 %copy-start.5 = (bf16[256,128]{1,0:T(8,128)(2,1)S(1)}, bf16[256,128]{1,0:T(8,128)(2,1)}, u32[]{:S(2)}) copy-start(bf16[256,128]{1,0:T(8,128)(2,1)} %bc_ref.3) | copy-start | bytes 196612
  54.6 8.7 %copy-start.7 = (bf16[256,12,128]{2,0,1:T(8,128)(2,1)S(1)}, bf16[256,12,128]{2,0,1:T(8,128)(2,1)}, u32[]{:S(2)}) copy-start(bf16[256,12,128]{2,0,1:T(8,128)(2,1)} %param.15) | copy-start | bytes 2359300
  54.6 8.7 %copy-start.8 = (f32[1,12,64,128]{3,2,1,0:T(8,128)S(1)}, f32[1,12,64,128]{3,2,1,0:T(8,128)}, u32[]{:S(2)}) copy-start(f32[1,12,64,128]{3,2,1,0:T(8,128)} %param.21) | copy-start | bytes 1179652
  54.6 8.7 %copy-start.10 = (f32[256,128]{1,0:T(8,128)S(1)}, f32[256,128]{1,0:T(8,128)}, u32[]{:S(2)}) copy-start(f32[256,128]{1,0:T(8,128)} %copy-done.9) | copy-start | bytes 393220
  54.6 8.7 %copy-start.11 = (f32[12]{0:T(128)S(1)}, f32[12]{0:T(128)}, u32[]{:S(2)}) copy-start(f32[12]{0:T(128)} %skips_ref.1) | copy-start | bytes 148
  60.6 11.9 %copy-start.3 = (bf16[2,3,256,128]{3,2,1,0:T(8,128)(2,1)S(1)}, bf16[2,3,256,128]{3,2,1,0:T(8,128)(2,1)}, u32[]{:S(2)}) copy-start(bf16[2,3,256,128]{3,2,1,0:T(8,128)(2,1)} %copy-done.1) | copy-start | bytes 1179652
  60.6 21.0 %collective-permute-start.13 = (f32[2,6,256]{2,1,0:T(8,128)S(1)}, f32[2,6,256]{2,1,0:T(8,128)S(1)}, u32[]{:S(2)}, u32[]{:S(2)}) collective-permute-start(f32[2,6,256]{2,1,0:T(8,128)S(1)} %late.1.refs_9_), channel_id=1, source_target_pairs={{8,0},{12,4},{16,8},{20,12},{24,16},{28,20},{9,1},{13,5},{17,9},{2... | collective-permute-start | bytes 36872 | tf_op jit(solution)/shard_map/ppermute | solution.py:35
  62.0 19.6 %collective-permute-start.14 = (f32[2,6,256]{2,1,0:T(8,128)S(1)}, f32[2,6,256]{2,1,0:T(8,128)S(1)}, u32[]{:S(2)}, u32[]{:S(2)}) collective-permute-start(f32[2,6,256]{2,1,0:T(8,128)S(1)} %late.1.refs_9_), channel_id=1, source_target_pairs={{16,0},{20,4},{24,8},{28,12},{17,1},{21,5},{25,9},{29,13},{18,2},{... | collective-permute-start | bytes 36872 | tf_op jit(solution)/shard_map/ppermute | solution.py:35
  69.0 12.0 %all-to-all-start = ((bf16[4,64,128]{2,1,0:T(8,128)(2,1)}), bf16[4,64,128]{2,1,0:T(8,128)(2,1)S(1)}, u32[]{:S(2)}, u32[]{:S(2)}) async-start(bf16[4,64,128]{2,1,0:T(8,128)(2,1)} %bitcast.21), calls=%async_computation | async-start | bytes 131072 | tf_op jit(solution)/shard_map/all_to_all | solution.py:512
  79.1 1.2 %copy-start.12 = (f32[2,2,3,256,128]{4,3,2,1,0:T(8,128)}, f32[2,2,3,256,128]{4,3,2,1,0:T(8,128)S(1)}, u32[]{:S(2)}) copy-start(f32[2,2,3,256,128]{4,3,2,1,0:T(8,128)S(1)} %get-tuple-element.40.refs_9_) | copy-start | bytes 4718596
  80.3 9.6 %collective-permute-start.6 = (bf16[3,256,128]{2,1,0:T(8,128)(2,1)S(1)}, bf16[3,256,128]{2,1,0:T(8,128)(2,1)S(1)}, u32[]{:S(2)}, u32[]{:S(2)}) collective-permute-start(bf16[3,256,128]{2,1,0:T(8,128)(2,1)S(1)} %get-tuple-element.33), channel_id=1, source_target_pairs={{0,4},{4,0},{8,12},{12,8},{16,20},{20,16},{24,28},{28,24},{1,5},{5... | collective-permute-start | bytes 589832 | tf_op jit(solution)/shard_map/ppermute | solution.py:40
  81.6 1.4 %copy-start.13 = (f32[2,2,3,256,128]{4,3,2,1,0:T(8,128)S(1)}, f32[2,2,3,256,128]{4,3,2,1,0:T(8,128)}, u32[]{:S(2)}) copy-start(f32[2,2,3,256,128]{4,3,2,1,0:T(8,128)} %copy-done.12) | copy-start | bytes 4718596
  87.8 16.9 %collective-permute-start.15 = (bf16[2,3,256,128]{3,2,1,0:T(8,128)(2,1)S(1)}, bf16[2,3,256,128]{3,2,1,0:T(8,128)(2,1)S(1)}, u32[]{:S(2)}, u32[]{:S(2)}) collective-permute-start(bf16[2,3,256,128]{3,2,1,0:T(8,128)(2,1)S(1)} %get-tuple-element.42), channel_id=1, source_target_pairs={{0,4},{4,0},{8,12},{12,8},{16,20},{20,16},{24,28},{28,24},{1,5},{5... | collective-permute-start | bytes 1179656 | tf_op jit(solution)/shard_map/ppermute | solution.py:40
  90.5 13.6 %all-to-all-start.1 = ((f32[8,8,128]{2,1,0:T(8,128)}), f32[8,8,128]{2,1,0:T(8,128)S(1)}, u32[]{:S(2)}, u32[]{:S(2)}) async-start(f32[8,8,128]{2,1,0:T(8,128)} %broadcast_in_dim.2), calls=%async_computation.1 | async-start | bytes 65536 | tf_op jit(solution)/shard_map/all_to_all | solution.py:545

commit v3 on v2

--- a/solution.py
+++ b/solution.py
@@ -452,6 +452,7 @@
     for _ in range(hops):
         keys.insert(0, tuple(moved(v, 2) for v in keys[0]))
 
+    rows = [(qg_mine, qg_theirs), (moved(qg_mine, -2), moved(qg_theirs, -2))]
     gots = []
     far = None
     step = 1
@@ -461,7 +462,7 @@
         if step == 2:
             base = after(base, keys[-2][1])
         if far is None:
-            base = after(base, keys[-2][0])
+            base = after(base, keys[-2][0], rows[1][0])
         ins = [base, got] if far is None else [base, far, got]
         far, sent = call(
             functools.partial(join_body, sets, far is None),
@@ -469,11 +470,6 @@
             ins, packed * width * 4, name="join",
         )
         step *= 2
-    rows = [(qg_mine, qg_theirs)]
-    source = (after(qg_mine, gots[0]), after(qg_theirs, gots[min(1, len(gots) - 1)]))
-    for _ in range(hops):
-        source = tuple(moved(v, -2) for v in source)
-        rows.append(source)
     flat = [v for both in keys for v in both]
     kv_space = pltpu.VMEM((2 * (hops + 1), 2, half, tokens, width), BF16)
     qg_space = pltpu.VMEM((2, 2, half, tokens, width), BF16)
@@ -529,7 +525,11 @@
         smem=1, name="query",
     )
     dq_theirs = swapped(dq_give)
+    for hop in range(1, hops):
+        one, two = rows[-1]
+        rows.append((moved(after(one, early), -2), moved(after(two, early), -2)))
     later = [v for both in rows[1:] for v in both]
+    pair_sums = swapped(sums)
     dkv_mine, dkv_give = call(
         functools.partial(later_body, reach),
         [shape((2, half, tokens, width), BF16)] * 2,
@@ -540,9 +540,13 @@
     )
     dkv_theirs = swapped(dkv_give)
 
-    sums = after(sums, dkv_give)
-    spread = jnp.broadcast_to(sums[None], (members, *sums.shape))
-    summed = jnp.sum(lax.all_to_all(spread, "seq", 0, 0, tiled=True), axis=0)
+    sums = after(sums + pair_sums, dkv_give)
+    pairs = members // 2
+    spread = jnp.broadcast_to(sums[None], (pairs, *sums.shape))
+    lines = [[2 * at + one for at in range(pairs)] for one in range(2)]
+    summed = jnp.sum(
+        lax.all_to_all(spread, "seq", 0, 0, axis_index_groups=lines, tiled=True), axis=0
+    )
     grad_decay, grad_skip = summed[0, :sets], summed[1, :sets]
 
     def by_token(mine, theirs):

time: 106 us -> 104 us (0.981)
  starting transfers between devices: 45.5 us -> 49.3 us
  waiting for transfers between devices: 21.7 us -> 18.5 us
  local copies, waits for them, and re-layouts: 5.57 us -> 4.37 us
    ppermute x13, waiting for transfers between devices: 11.8 us -> 8.1 us  [moved(): return lax.ppermute(value, 'seq', pairs)]
    all_to_all x1, waiting for transfers between devices: 0.01 us -> 3.55 us  [shards(): gbc = lax.all_to_all(gbc, 'head', 0, 0, tiled=True)]
    ppermute x13, starting transfers between devices: 27.4 us -> 30.7 us  [moved(): return lax.ppermute(value, 'seq', pairs)]
    all_to_all x1, waiting for transfers between devices: 5.9 us -> 2.9 us  [shards(): lax.all_to_all(spread, 'seq', 0, 0, axis_index_groups=lines, tiled=True)]
    unnamed x34 -> x32, local copies, waits for them, and re-layouts: 4.43 us -> 3.24 us
    ppermute x4 -> x5, starting transfers between devices: 7.73 us -> 8.35 us  [swapped(): return lax.ppermute(value, 'seq', [(at, at ^ 1) for at in range(count)])]
    ppermute x4 -> x5, waiting for transfers between devices: 3.99 us -> 3.9 us  [swapped(): return lax.ppermute(value, 'seq', [(at, at ^ 1) for at in range(count)])]
  transfers between devices with their start and end apart: 19 -> 20, of which waited for: 6 -> 6; matrix products, arithmetic and copies ran while one was open for 4% -> 4% of each run, Pallas kernels for 25% -> 20%
where the time goes in v3:
time: 104 us
  starting transfers between devices  49.3 us (47%)
  Pallas kernels  25.8 us (25%)
  waiting for transfers between devices  18.5 us (18%)
  other arithmetic  4.74 us (5%)
  local copies, waits for them, and re-layouts  4.37 us (4%)
  between operations  1.09 us (1%)
    ppermute x13, starting transfers between devices, moved(): return lax.ppermute(value, 'seq', pairs)  30.7 us
    pallas_call x9, Pallas kernels, call(): pl.pallas_call(body, out_shape=outs, in_specs=specs, out_specs=vmem(len(o...  25.8 us
    ppermute x5, starting transfers between devices, swapped(): return lax.ppermute(value, 'seq', [(at, at ^ 1) for at in range(count)])  8.35 us
    ppermute x13, waiting for transfers between devices, moved(): return lax.ppermute(value, 'seq', pairs)  8.1 us
    all_to_all x1, starting transfers between devices, shards(): lax.all_to_all(spread, 'seq', 0, 0, axis_index_groups=lines, tiled=True)  6.89 us
    ppermute x5, waiting for transfers between devices, swapped(): return lax.ppermute(value, 'seq', [(at, at ^ 1) for at in range(count)])  3.9 us
    all_to_all x1, waiting for transfers between devices, shards(): gbc = lax.all_to_all(gbc, 'head', 0, 0, tiled=True)  3.55 us
    all_to_all x1, starting transfers between devices, shards(): gbc = lax.all_to_all(gbc, 'head', 0, 0, tiled=True)  3.29 us
  transfers between devices with their start and end apart: 20, of which 6 were waited for; matrix products, arithmetic and copies ran while one was open for 4% of the time, Pallas kernels for 20%

profile of v3, /device:TPU:0, one launch (start us, length us, event | category | flops | bytes accessed | tf_op | source)
XLA Modules:
  0.0 103.7 jit_solution(18339733442913712185)
XLA Ops:
  0.7 0.0 copy-start.4
  0.7 1.4 %fusion.5 = (bf16[2,3,256,128]{3,2,1,0:T(8,128)(2,1)S(1)}, bf16[2,3,256,128]{3,2,1,0:T(8,128)(2,1)S(1)}) fusion(s32[]{:T(128)S(6)} %select_n.65, bf16[1,256,6,128]{3,1,2,0:T(8,128)(2,1)} %bitcast.41, bf16[1,256,6,128]{3,1,2,0:T(8,128)(2,1)} %bitcast.42, s32[]{:T(128)S(6)} %select_n.64), kind=kLoop, calls=%fused_computation.13 | loop fusion | flops 393216 | bytes 1572872 | tf_op jit(solution)/shard_map/dynamic_slice | solution.py:444
  2.1 3.0 %collective-permute-start.2 = (bf16[2,3,256,128]{3,2,1,0:T(8,128)(2,1)S(1)}, bf16[2,3,256,128]{3,2,1,0:T(8,128)(2,1)}, u32[]{:S(2)}, u32[]{:S(2)}) collective-permute-start(bf16[2,3,256,128]{3,2,1,0:T(8,128)(2,1)S(1)} %get-tuple-element.78), channel_id=1, source_target_pairs={{0,4},{4,0},{8,12},{12,8},{16,20},{20,16},{24,28},{28,24},{1,5},{5... | collective-permute-start | bytes 1179656 | tf_op jit(solution)/shard_map/ppermute | solution.py:40
  5.1 0.8 fusion.1
  5.9 0.0 collective-permute-start.5
  6.0 4.0 %collective-permute-start = (bf16[2,3,256,128]{3,2,1,0:T(8,128)(2,1)S(1)}, bf16[2,3,256,128]{3,2,1,0:T(8,128)(2,1)S(1)}, u32[]{:S(2)}, u32[]{:S(2)}) collective-permute-start(bf16[2,3,256,128]{3,2,1,0:T(8,128)(2,1)S(1)} %get-tuple-element.79.refs_3_.refs_5_.refs_1_), channel_id=1, source_target_pairs={{0,8},{4,12},{8,16},{12,20},{16,24},{20,28},{1,9},{5,13},{9,17},{1... | collective-permute-start | bytes 1179656 | tf_op jit(solution)/shard_map/ppermute | solution.py:35
  10.0 1.3 %collective-permute-start.7 = (bf16[2,3,256,128]{3,2,1,0:T(8,128)(2,1)S(1)}, bf16[2,3,256,128]{3,2,1,0:T(8,128)(2,1)}, u32[]{:S(2)}, u32[]{:S(2)}) collective-permute-start(bf16[2,3,256,128]{3,2,1,0:T(8,128)(2,1)S(1)} %get-tuple-element.77.refs_5_.refs_3_.refs_7_), channel_id=1, source_target_pairs={{8,0},{12,4},{16,8},{20,12},{24,16},{28,20},{9,1},{13,5},{17,9},{2... | collective-permute-start | bytes 1179656 | tf_op jit(solution)/shard_map/ppermute | solution.py:35
  11.3 3.9 %collective-permute-done.2.refs_4_.refs_6_.refs_2_ = bf16[2,3,256,128]{3,2,1,0:T(8,128)(2,1)} collective-permute-done((bf16[2,3,256,128]{3,2,1,0:T(8,128)(2,1)S(1)}, bf16[2,3,256,128]{3,2,1,0:T(8,128)(2,1)}, u32[]{:S(2)}, u32[]{:S(2)}) %collective-permute-start.2) | collective-permute-done | bytes 393248 | tf_op jit(solution)/shard_map/ppermute | solution.py:40
  15.2 4.8 %collective-permute-start.3 = (bf16[2,3,256,128]{3,2,1,0:T(8,128)(2,1)}, bf16[2,3,256,128]{3,2,1,0:T(8,128)(2,1)}, u32[]{:S(2)}, u32[]{:S(2)}) collective-permute-start(bf16[2,3,256,128]{3,2,1,0:T(8,128)(2,1)} %collective-permute-done.2.refs_4_.refs_6_.refs_2_), channel_id=1, source_target_pairs={{0,8},{4,12},{8,16},{12,20},{16,24},{20,28},{1,9},{5,13},{9,17},{1... | collective-permute-start | bytes 1179656 | tf_op jit(solution)/shard_map/ppermute | solution.py:35
  20.0 0.1 copy.23.dt_ref
  20.1 2.2 %summary.1 = (f32[784,128]{1,0:T(8,128)S(1)}, bf16[784,128]{1,0:T(8,128)(2,1)S(1)}, f32[256,128]{1,0:T(8,128)S(1)}, f32[16,256]{1,0:T(8,128)S(1)}) custom-call(f32[12]{0:T(128)S(1)} %copy-done.6, bf16[12,256,128]{2,1,0:T(8,128)(2,1)S(1)} %bitcast.37, f32[256,12]{1,0:T(8,128)S(1)} %copy.23.dt_ref, bf16[256,128]{1,0:T(8,128)(2,1)S(1)} %copy-done.4), custom_call_target="tpu_custom_call" | custom-call | flops 100663296 | bytes 1613872 | tf_op jit(solution)/shard_map/summary/pallas_call | solution.py:54
  22.3 0.0 copy-start.9
  22.3 0.6 copy-done.9
  23.0 1.3 %collective-permute-start.14 = (bf16[784,128]{1,0:T(8,128)(2,1)S(1)}, bf16[784,128]{1,0:T(8,128)(2,1)S(1)}, u32[]{:S(2)}, u32[]{:S(2)}) collective-permute-start(bf16[784,128]{1,0:T(8,128)(2,1)S(1)} %get-tuple-element.42), channel_id=1, source_target_pairs={{4,0},{8,4},{12,8},{16,12},{20,16},{24,20},{28,24},{5,1},{9,5},{13... | collective-permute-start | bytes 602120 | tf_op jit(solution)/shard_map/ppermute | solution.py:35
  24.3 0.0 collective-permute-done.5.refs_6_.refs_4_.refs_8_
  24.3 1.3 %collective-permute-start.8 = (bf16[2,3,256,128]{3,2,1,0:T(8,128)(2,1)S(1)}, bf16[2,3,256,128]{3,2,1,0:T(8,128)(2,1)}, u32[]{:S(2)}, u32[]{:S(2)}) collective-permute-start(bf16[2,3,256,128]{3,2,1,0:T(8,128)(2,1)S(1)} %collective-permute-done.5.refs_6_.refs_4_.refs_8_), channel_id=1, source_target_pairs={{8,0},{12,4},{16,8},{20,12},{24,16},{28,20},{9,1},{13,5},{17,9},{2... | collective-permute-start | bytes 1179656 | tf_op jit(solution)/shard_map/ppermute | solution.py:35
  25.6 0.0 copy-start.1
  25.6 0.0 collective-permute-done.7.refs_3_
  25.6 0.7 copy-done.1
  26.3 4.2 %collective-permute-done.14.refs_0_ = bf16[784,128]{1,0:T(8,128)(2,1)S(1)} collective-permute-done((bf16[784,128]{1,0:T(8,128)(2,1)S(1)}, bf16[784,128]{1,0:T(8,128)(2,1)S(1)}, u32[]{:S(2)}, u32[]{:S(2)}) %collective-permute-start.14) | collective-permute-done | bytes 200736 | tf_op jit(solution)/shard_map/ppermute | solution.py:35
  30.6 0.8 join.3
  31.3 1.3 %collective-permute-start.15 = (bf16[784,128]{1,0:T(8,128)(2,1)}, bf16[784,128]{1,0:T(8,128)(2,1)S(1)}, u32[]{:S(2)}, u32[]{:S(2)}) collective-permute-start(bf16[784,128]{1,0:T(8,128)(2,1)} %get-tuple-element.44), channel_id=1, source_target_pairs={{8,0},{12,4},{16,8},{20,12},{24,16},{28,20},{9,1},{13,5},{17,9},{2... | collective-permute-start | bytes 602120 | tf_op jit(solution)/shard_map/ppermute | solution.py:35
  32.6 5.2 %collective-permute-start.1 = (bf16[2,3,256,128]{3,2,1,0:T(8,128)(2,1)}, bf16[2,3,256,128]{3,2,1,0:T(8,128)(2,1)S(1)}, u32[]{:S(2)}, u32[]{:S(2)}) collective-permute-start(bf16[2,3,256,128]{3,2,1,0:T(8,128)(2,1)} %copy-done.1), channel_id=1, source_target_pairs={{0,8},{4,12},{8,16},{12,20},{16,24},{20,28},{1,9},{5,13},{9,17},{1... | collective-permute-start | bytes 1179656 | tf_op jit(solution)/shard_map/ppermute | solution.py:35
  37.9 0.0 collective-permute-done.3.refs_2_.refs_4_
  37.9 4.6 %collective-permute-start.4 = (bf16[2,3,256,128]{3,2,1,0:T(8,128)(2,1)}, bf16[2,3,256,128]{3,2,1,0:T(8,128)(2,1)}, u32[]{:S(2)}, u32[]{:S(2)}) collective-permute-start(bf16[2,3,256,128]{3,2,1,0:T(8,128)(2,1)} %collective-permute-done.3.refs_2_.refs_4_), channel_id=1, source_target_pairs={{0,8},{4,12},{8,16},{12,20},{16,24},{20,28},{1,9},{5,13},{9,17},{1... | collective-permute-start | bytes 1179656 | tf_op jit(solution)/shard_map/ppermute | solution.py:35
  42.5 0.1 pad_add_fusion.refs_0_
  42.6 0.3 collective-permute-done.15.refs_1_
  43.0 0.1 join.4
  43.1 1.3 %collective-permute-start.16 = (bf16[784,128]{1,0:T(8,128)(2,1)S(1)}, bf16[784,128]{1,0:T(8,128)(2,1)S(1)}, u32[]{:S(2)}, u32[]{:S(2)}) collective-permute-start(bf16[784,128]{1,0:T(8,128)(2,1)S(1)} %get-tuple-element.46), channel_id=1, source_target_pairs={{16,0},{20,4},{24,8},{28,12},{17,1},{21,5},{25,9},{29,13},{18,2},{... | collective-permute-start | bytes 602120 | tf_op jit(solution)/shard_map/ppermute | solution.py:35
  44.4 0.0 copy-start.2
  44.4 1.0 copy-done.2
  45.4 3.2 %early.1.refs_5_ = f32[3,6,256]{2,1,0:T(8,128)S(1)} custom-call(s32[2]{0:T(128)S(1)} %pad_add_fusion.refs_0_, bf16[2,3,256,128]{3,2,1,0:T(8,128)(2,1)S(1)} %copy-done.2, bf16[2,3,256,128]{3,2,1,0:T(8,128)(2,1)} %collective-permute-done.3.refs_2_.refs_4_, bf16[2,3,256,128]{3,2,1,0:T(8,128)(2,1)S(1)} %get-tuple-element.79.refs_3_.refs_5_.refs_1_, ...), custom_call_target="tpu_custom_call" | custom-call | flops 603979776 | bytes 2377736 | tf_op jit(solution)/shard_map/early/pallas_call | solution.py:54
  48.6 0.0 copy-start.5
  48.6 0.0 copy-start.7
  48.6 0.0 copy-start.8
  48.6 0.0 copy-start.10
  48.6 0.0 copy-start.11
  48.6 1.4 %collective-permute-start.9 = (bf16[2,3,256,128]{3,2,1,0:T(8,128)(2,1)}, bf16[2,3,256,128]{3,2,1,0:T(8,128)(2,1)S(1)}, u32[]{:S(2)}, u32[]{:S(2)}) collective-permute-start(bf16[2,3,256,128]{3,2,1,0:T(8,128)(2,1)} %collective-permute-done.7.refs_3_), channel_id=1, source_target_pairs={{8,0},{12,4},{16,8},{20,12},{24,16},{28,20},{9,1},{13,5},{17,9},{2... | collective-permute-start | bytes 1179656 | tf_op jit(solution)/shard_map/ppermute | solution.py:35
  50.1 1.3 %collective-permute-start.10 = (bf16[2,3,256,128]{3,2,1,0:T(8,128)(2,1)}, bf16[2,3,256,128]{3,2,1,0:T(8,128)(2,1)S(1)}, u32[]{:S(2)}, u32[]{:S(2)}) collective-permute-start(bf16[2,3,256,128]{3,2,1,0:T(8,128)(2,1)} %collective-permute-done.8.refs_4_), channel_id=1, source_target_pairs={{8,0},{12,4},{16,8},{20,12},{24,16},{28,20},{9,1},{13,5},{17,9},{2... | collective-permute-start | bytes 1179656 | tf_op jit(solution)/shard_map/ppermute | solution.py:35
  51.4 3.5 %collective-permute-done.16.refs_1_ = bf16[784,128]{1,0:T(8,128)(2,1)S(1)} collective-permute-done((bf16[784,128]{1,0:T(8,128)(2,1)S(1)}, bf16[784,128]{1,0:T(8,128)(2,1)S(1)}, u32[]{:S(2)}, u32[]{:S(2)}) %collective-permute-start.16) | collective-permute-done | bytes 200736 | tf_op jit(solution)/shard_map/ppermute | solution.py:35
  54.8 0.8 join.5
  55.6 0.0 collective-permute-done.1.refs_1_
  55.6 0.0 collective-permute-done.4.refs_2_
  55.6 2.1 %late.1.refs_9_ = f32[2,6,256]{2,1,0:T(8,128)S(1)} custom-call(s32[2]{0:T(128)S(1)} %pad_add_fusion.refs_0_, bf16[2,3,256,128]{3,2,1,0:T(8,128)(2,1)S(1)} %collective-permute-done.1.refs_1_, bf16[2,3,256,128]{3,2,1,0:T(8,128)(2,1)} %collective-permute-done.4.refs_2_, bf16[2,3,256,128]{3,2,1,0:T(8,128)(2,1)S(1)} %get-tuple-element.77.refs_5_.refs_3_.refs_7_, ...), custom_call_target="tpu_custom_call" | custom-call | flops 301989888 | bytes 1603592 | tf_op jit(solution)/shard_map/late/pallas_call | solution.py:54
  57.7 0.0 copy-start.3
  57.7 1.4 %collective-permute-start.11 = (f32[2,6,256]{2,1,0:T(8,128)S(1)}, f32[2,6,256]{2,1,0:T(8,128)S(1)}, u32[]{:S(2)}, u32[]{:S(2)}) collective-permute-start(f32[2,6,256]{2,1,0:T(8,128)S(1)} %late.1.refs_9_), channel_id=1, source_target_pairs={{8,0},{12,4},{16,8},{20,12},{24,16},{28,20},{9,1},{13,5},{17,9},{2... | collective-permute-start | bytes 36872 | tf_op jit(solution)/shard_map/ppermute | solution.py:35
  59.1 1.5 %collective-permute-start.12 = (f32[2,6,256]{2,1,0:T(8,128)S(1)}, f32[2,6,256]{2,1,0:T(8,128)S(1)}, u32[]{:S(2)}, u32[]{:S(2)}) collective-permute-start(f32[2,6,256]{2,1,0:T(8,128)S(1)} %late.1.refs_9_), channel_id=1, source_target_pairs={{16,0},{20,4},{24,8},{28,12},{17,1},{21,5},{25,9},{29,13},{18,2},{... | collective-permute-start | bytes 36872 | tf_op jit(solution)/shard_map/ppermute | solution.py:35
  60.7 5.6 %scan.1 = (bf16[12,256,128]{2,1,0:T(8,128)(2,1)}, f32[256,12]{1,0:T(8,128)S(1)}, bf16[256,128]{1,0:T(8,128)(2,1)}, f32[8,128]{1,0:T(8,128)S(1)}) custom-call(f32[12]{0:T(128)S(1)} %copy-done.6, f32[12]{0:T(128)S(1)} %copy-done.11, bf16[12,256,128]{2,1,0:T(8,128)(2,1)S(1)} %bitcast.39, bf16[12,256,128]{2,1,0:T(8,128)(2,1)S(1)} %bitcast.38, ...), custom_call_target="tpu_custom_call" | custom-call | flops 805306368 | bytes 3461216 | tf_op jit(solution)/shard_map/scan/pallas_call | solution.py:54
  66.3 3.3 %collective-permute-start.17 = (f32[8,128]{1,0:T(8,128)S(1)}, f32[8,128]{1,0:T(8,128)S(1)}, u32[]{:S(2)}, u32[]{:S(2)}) collective-permute-start(f32[8,128]{1,0:T(8,128)S(1)} %get-tuple-element.54), channel_id=1, source_target_pairs={{0,4},{4,0},{8,12},{12,8},{16,20},{20,16},{24,28},{28,24},{1,5},{5... | collective-permute-start | bytes 12296 | tf_op jit(solution)/shard_map/ppermute | solution.py:40
  69.5 6.6 %query.1 = (bf16[3,256,128]{2,1,0:T(8,128)(2,1)S(1)}, bf16[3,256,128]{2,1,0:T(8,128)(2,1)S(1)}, f32[2,2,3,256,128]{4,3,2,1,0:T(8,128)S(1)}) custom-call(s32[2]{0:T(128)S(1)} %pad_add_fusion.refs_0_, bf16[2,3,256,128]{3,2,1,0:T(8,128)(2,1)S(1)} %collective-permute-done.1.refs_1_, bf16[2,3,256,128]{3,2,1,0:T(8,128)(2,1)} %collective-permute-done.4.refs_2_, ...), custom_call_target="tpu_custom_call" | custom-call | flops 1509949440 | bytes 5124104 | tf_op jit(solution)/shard_map/query/pallas_call | solution.py:54
  76.2 0.0 collective-permute-done.9.refs_5_
  76.2 4.6 %later.1 = (bf16[2,3,256,128]{3,2,1,0:T(8,128)(2,1)S(1)}, bf16[2,3,256,128]{3,2,1,0:T(8,128)(2,1)S(1)}) custom-call(s32[2]{0:T(128)S(1)} %pad_add_fusion.refs_0_, bf16[2,3,256,128]{3,2,1,0:T(8,128)(2,1)S(1)} %get-tuple-element.79.refs_3_.refs_5_.refs_1_, bf16[2,3,256,128]{3,2,1,0:T(8,128)(2,1)} %collective-permute-done.2.refs_4_.refs_6_.refs_2_, ...), custom_call_target="tpu_custom_call" | custom-call | flops 1610612736 | bytes 4743176 | tf_op jit(solution)/shard_map/later/pallas_call | solution.py:54
  80.8 0.6 broadcast_in_dim.2
  81.4 6.9 %all-to-all-start.1 = ((f32[4,8,128]{2,1,0:T(8,128)}), f32[4,8,128]{2,1,0:T(8,128)S(1)}, u32[]{:S(2)}, u32[]{:S(2)}) async-start(f32[4,8,128]{2,1,0:T(8,128)} %broadcast_in_dim.2), calls=%async_computation.1 | async-start | bytes 32768 | tf_op jit(solution)/shard_map/all_to_all | solution.py:548
  88.3 0.7 copy.24
  89.0 2.0 %collective-permute-start.13 = (bf16[2,3,256,128]{3,2,1,0:T(8,128)(2,1)S(1)}, bf16[2,3,256,128]{3,2,1,0:T(8,128)(2,1)S(1)}, u32[]{:S(2)}, u32[]{:S(2)}) collective-permute-start(bf16[2,3,256,128]{3,2,1,0:T(8,128)(2,1)S(1)} %get-tuple-element.38), channel_id=1, source_target_pairs={{0,4},{4,0},{8,12},{12,8},{16,20},{20,16},{24,28},{28,24},{1,5},{5... | collective-permute-start | bytes 1179656 | tf_op jit(solution)/shard_map/ppermute | solution.py:40
  91.0 2.9 %all-to-all-done.1 = f32[4,8,128]{2,1,0:T(8,128)S(1)} async-done(((f32[4,8,128]{2,1,0:T(8,128)}), f32[4,8,128]{2,1,0:T(8,128)S(1)}, u32[]{:S(2)}, u32[]{:S(2)}) %all-to-all-start.1) | async-done | bytes 16416 | tf_op jit(solution)/shard_map/all_to_all | solution.py:548
  93.9 3.3 %all-to-all-start = ((bf16[4,64,128]{2,1,0:T(8,128)(2,1)}), bf16[4,64,128]{2,1,0:T(8,128)(2,1)S(1)}, u32[]{:S(2)}, u32[]{:S(2)}) async-start(bf16[4,64,128]{2,1,0:T(8,128)(2,1)} %bitcast.21), calls=%async_computation | async-start | bytes 131072 | tf_op jit(solution)/shard_map/all_to_all | solution.py:508
  97.2 0.5 slice_bitcast_fusion
  97.7 3.6 %all-to-all-done = bf16[4,64,128]{2,1,0:T(8,128)(2,1)S(1)} async-done(((bf16[4,64,128]{2,1,0:T(8,128)(2,1)}), bf16[4,64,128]{2,1,0:T(8,128)(2,1)S(1)}, u32[]{:S(2)}, u32[]{:S(2)}) %all-to-all-start) | async-done | bytes 65568 | tf_op jit(solution)/shard_map/all_to_all | solution.py:508
  101.3 0.6 convert_reduce_fusion
  101.9 0.8 maximum_bitcast_fusion
  102.7 0.1 select_bitcast_fusion.1
  102.8 0.9 maximum_bitcast_fusion.1
  (29 shorter events, 0.1 us)
Async XLA Ops:
  0.6 4.5 %copy-start.12 = (bf16[256,6,128]{2,0,1:T(8,128)(2,1)S(1)}, bf16[256,6,128]{2,0,1:T(8,128)(2,1)}, u32[]{:S(2)}) copy-start(bf16[256,6,128]{2,0,1:T(8,128)(2,1)} %param.11) | copy-start | bytes 1179652
  0.6 4.5 %copy-start.13 = (bf16[256,6,128]{2,0,1:T(8,128)(2,1)S(1)}, bf16[256,6,128]{2,0,1:T(8,128)(2,1)}, u32[]{:S(2)}) copy-start(bf16[256,6,128]{2,0,1:T(8,128)(2,1)} %param.14) | copy-start | bytes 1179652
  0.7 19.3 %copy-start.14 = (f32[256,12]{0,1:T(8,128)S(1)}, f32[256,12]{0,1:T(8,128)}, u32[]{:S(2)}) copy-start(f32[256,12]{0,1:T(8,128)} %param.17) | copy-start | bytes 36868
  0.7 19.4 %copy-start = (bf16[256,12,128]{2,0,1:T(8,128)(2,1)S(1)}, bf16[256,12,128]{2,0,1:T(8,128)(2,1)}, u32[]{:S(2)}) copy-start(bf16[256,12,128]{2,0,1:T(8,128)(2,1)} %param.16) | copy-start | bytes 2359300
  0.7 19.4 %copy-start.4 = (bf16[256,128]{1,0:T(8,128)(2,1)S(1)}, bf16[256,128]{1,0:T(8,128)(2,1)}, u32[]{:S(2)}) copy-start(bf16[256,128]{1,0:T(8,128)(2,1)} %bc_ref.3) | copy-start | bytes 196612
  0.7 19.4 %copy-start.6 = (f32[12]{0:T(128)S(1)}, f32[12]{0:T(128)}, u32[]{:S(2)}) copy-start(f32[12]{0:T(128)} %rates_ref.3) | copy-start | bytes 148
  2.1 13.1 %collective-permute-start.2 = (bf16[2,3,256,128]{3,2,1,0:T(8,128)(2,1)S(1)}, bf16[2,3,256,128]{3,2,1,0:T(8,128)(2,1)}, u32[]{:S(2)}, u32[]{:S(2)}) collective-permute-start(bf16[2,3,256,128]{3,2,1,0:T(8,128)(2,1)S(1)} %get-tuple-element.78), channel_id=1, source_target_pairs={{0,4},{4,0},{8,12},{12,8},{16,20},{20,16},{24,28},{28,24},{1,5},{5... | collective-permute-start | bytes 1179656 | tf_op jit(solution)/shard_map/ppermute | solution.py:40
  5.9 18.3 %collective-permute-start.5 = (bf16[2,3,256,128]{3,2,1,0:T(8,128)(2,1)}, bf16[2,3,256,128]{3,2,1,0:T(8,128)(2,1)S(1)}, u32[]{:S(2)}, u32[]{:S(2)}) collective-permute-start(bf16[2,3,256,128]{3,2,1,0:T(8,128)(2,1)} %get-tuple-element.76), channel_id=1, source_target_pairs={{0,4},{4,0},{8,12},{12,8},{16,20},{20,16},{24,28},{28,24},{1,5},{5... | collective-permute-start | bytes 1179656 | tf_op jit(solution)/shard_map/ppermute | solution.py:40
  6.0 19.6 %collective-permute-start = (bf16[2,3,256,128]{3,2,1,0:T(8,128)(2,1)S(1)}, bf16[2,3,256,128]{3,2,1,0:T(8,128)(2,1)S(1)}, u32[]{:S(2)}, u32[]{:S(2)}) collective-permute-start(bf16[2,3,256,128]{3,2,1,0:T(8,128)(2,1)S(1)} %get-tuple-element.79.refs_3_.refs_5_.refs_1_), channel_id=1, source_target_pairs={{0,8},{4,12},{8,16},{12,20},{16,24},{20,28},{1,9},{5,13},{9,17},{1... | collective-permute-start | bytes 1179656 | tf_op jit(solution)/shard_map/ppermute | solution.py:35
  10.0 15.6 %collective-permute-start.7 = (bf16[2,3,256,128]{3,2,1,0:T(8,128)(2,1)S(1)}, bf16[2,3,256,128]{3,2,1,0:T(8,128)(2,1)}, u32[]{:S(2)}, u32[]{:S(2)}) collective-permute-start(bf16[2,3,256,128]{3,2,1,0:T(8,128)(2,1)S(1)} %get-tuple-element.77.refs_5_.refs_3_.refs_7_), channel_id=1, source_target_pairs={{8,0},{12,4},{16,8},{20,12},{24,16},{28,20},{9,1},{13,5},{17,9},{2... | collective-permute-start | bytes 1179656 | tf_op jit(solution)/shard_map/ppermute | solution.py:35
  15.2 22.7 %collective-permute-start.3 = (bf16[2,3,256,128]{3,2,1,0:T(8,128)(2,1)}, bf16[2,3,256,128]{3,2,1,0:T(8,128)(2,1)}, u32[]{:S(2)}, u32[]{:S(2)}) collective-permute-start(bf16[2,3,256,128]{3,2,1,0:T(8,128)(2,1)} %collective-permute-done.2.refs_4_.refs_6_.refs_2_), channel_id=1, source_target_pairs={{0,8},{4,12},{8,16},{12,20},{16,24},{20,28},{1,9},{5,13},{9,17},{1... | collective-permute-start | bytes 1179656 | tf_op jit(solution)/shard_map/ppermute | solution.py:35
  22.3 0.7 copy-start.9
  23.0 7.6 %collective-permute-start.14 = (bf16[784,128]{1,0:T(8,128)(2,1)S(1)}, bf16[784,128]{1,0:T(8,128)(2,1)S(1)}, u32[]{:S(2)}, u32[]{:S(2)}) collective-permute-start(bf16[784,128]{1,0:T(8,128)(2,1)S(1)} %get-tuple-element.42), channel_id=1, source_target_pairs={{4,0},{8,4},{12,8},{16,12},{20,16},{24,20},{28,24},{5,1},{9,5},{13... | collective-permute-start | bytes 602120 | tf_op jit(solution)/shard_map/ppermute | solution.py:35
  24.3 25.8 %collective-permute-start.8 = (bf16[2,3,256,128]{3,2,1,0:T(8,128)(2,1)S(1)}, bf16[2,3,256,128]{3,2,1,0:T(8,128)(2,1)}, u32[]{:S(2)}, u32[]{:S(2)}) collective-permute-start(bf16[2,3,256,128]{3,2,1,0:T(8,128)(2,1)S(1)} %collective-permute-done.5.refs_6_.refs_4_.refs_8_), channel_id=1, source_target_pairs={{8,0},{12,4},{16,8},{20,12},{24,16},{28,20},{9,1},{13,5},{17,9},{2... | collective-permute-start | bytes 1179656 | tf_op jit(solution)/shard_map/ppermute | solution.py:35
  25.6 0.7 copy-start.1
  31.3 11.6 %collective-permute-start.15 = (bf16[784,128]{1,0:T(8,128)(2,1)}, bf16[784,128]{1,0:T(8,128)(2,1)S(1)}, u32[]{:S(2)}, u32[]{:S(2)}) collective-permute-start(bf16[784,128]{1,0:T(8,128)(2,1)} %get-tuple-element.44), channel_id=1, source_target_pairs={{8,0},{12,4},{16,8},{20,12},{24,16},{28,20},{9,1},{13,5},{17,9},{2... | collective-permute-start | bytes 602120 | tf_op jit(solution)/shard_map/ppermute | solution.py:35
  32.6 23.0 %collective-permute-start.1 = (bf16[2,3,256,128]{3,2,1,0:T(8,128)(2,1)}, bf16[2,3,256,128]{3,2,1,0:T(8,128)(2,1)S(1)}, u32[]{:S(2)}, u32[]{:S(2)}) collective-permute-start(bf16[2,3,256,128]{3,2,1,0:T(8,128)(2,1)} %copy-done.1), channel_id=1, source_target_pairs={{0,8},{4,12},{8,16},{12,20},{16,24},{20,28},{1,9},{5,13},{9,17},{1... | collective-permute-start | bytes 1179656 | tf_op jit(solution)/shard_map/ppermute | solution.py:35
  37.9 17.7 %collective-permute-start.4 = (bf16[2,3,256,128]{3,2,1,0:T(8,128)(2,1)}, bf16[2,3,256,128]{3,2,1,0:T(8,128)(2,1)}, u32[]{:S(2)}, u32[]{:S(2)}) collective-permute-start(bf16[2,3,256,128]{3,2,1,0:T(8,128)(2,1)} %collective-permute-done.3.refs_2_.refs_4_), channel_id=1, source_target_pairs={{0,8},{4,12},{8,16},{12,20},{16,24},{20,28},{1,9},{5,13},{9,17},{1... | collective-permute-start | bytes 1179656 | tf_op jit(solution)/shard_map/ppermute | solution.py:35
  43.1 11.8 %collective-permute-start.16 = (bf16[784,128]{1,0:T(8,128)(2,1)S(1)}, bf16[784,128]{1,0:T(8,128)(2,1)S(1)}, u32[]{:S(2)}, u32[]{:S(2)}) collective-permute-start(bf16[784,128]{1,0:T(8,128)(2,1)S(1)} %get-tuple-element.46), channel_id=1, source_target_pairs={{16,0},{20,4},{24,8},{28,12},{17,1},{21,5},{25,9},{29,13},{18,2},{... | collective-permute-start | bytes 602120 | tf_op jit(solution)/shard_map/ppermute | solution.py:35
  44.4 1.0 copy-start.2
  48.6 12.1 %copy-start.5 = (bf16[256,128]{1,0:T(8,128)(2,1)S(1)}, bf16[256,128]{1,0:T(8,128)(2,1)}, u32[]{:S(2)}) copy-start(bf16[256,128]{1,0:T(8,128)(2,1)} %bc_ref.3) | copy-start | bytes 196612
  48.6 12.1 %copy-start.7 = (bf16[256,12,128]{2,0,1:T(8,128)(2,1)S(1)}, bf16[256,12,128]{2,0,1:T(8,128)(2,1)}, u32[]{:S(2)}) copy-start(bf16[256,12,128]{2,0,1:T(8,128)(2,1)} %param.15) | copy-start | bytes 2359300
  48.6 12.1 %copy-start.8 = (f32[1,12,64,128]{3,2,1,0:T(8,128)S(1)}, f32[1,12,64,128]{3,2,1,0:T(8,128)}, u32[]{:S(2)}) copy-start(f32[1,12,64,128]{3,2,1,0:T(8,128)} %param.21) | copy-start | bytes 1179652
  48.6 12.0 %copy-start.10 = (f32[256,128]{1,0:T(8,128)S(1)}, f32[256,128]{1,0:T(8,128)}, u32[]{:S(2)}) copy-start(f32[256,128]{1,0:T(8,128)} %copy-done.9) | copy-start | bytes 393220
  48.6 12.0 %copy-start.11 = (f32[12]{0:T(128)S(1)}, f32[12]{0:T(128)}, u32[]{:S(2)}) copy-start(f32[12]{0:T(128)} %skips_ref.1) | copy-start | bytes 148
  48.6 27.5 %collective-permute-start.9 = (bf16[2,3,256,128]{3,2,1,0:T(8,128)(2,1)}, bf16[2,3,256,128]{3,2,1,0:T(8,128)(2,1)S(1)}, u32[]{:S(2)}, u32[]{:S(2)}) collective-permute-start(bf16[2,3,256,128]{3,2,1,0:T(8,128)(2,1)} %collective-permute-done.7.refs_3_), channel_id=1, source_target_pairs={{8,0},{12,4},{16,8},{20,12},{24,16},{28,20},{9,1},{13,5},{17,9},{2... | collective-permute-start | bytes 1179656 | tf_op jit(solution)/shard_map/ppermute | solution.py:35
  50.1 26.1 %collective-permute-start.10 = (bf16[2,3,256,128]{3,2,1,0:T(8,128)(2,1)}, bf16[2,3,256,128]{3,2,1,0:T(8,128)(2,1)S(1)}, u32[]{:S(2)}, u32[]{:S(2)}) collective-permute-start(bf16[2,3,256,128]{3,2,1,0:T(8,128)(2,1)} %collective-permute-done.8.refs_4_), channel_id=1, source_target_pairs={{8,0},{12,4},{16,8},{20,12},{24,16},{28,20},{9,1},{13,5},{17,9},{2... | collective-permute-start | bytes 1179656 | tf_op jit(solution)/shard_map/ppermute | solution.py:35
  57.7 11.9 %copy-start.3 = (bf16[2,3,256,128]{3,2,1,0:T(8,128)(2,1)S(1)}, bf16[2,3,256,128]{3,2,1,0:T(8,128)(2,1)}, u32[]{:S(2)}) copy-start(bf16[2,3,256,128]{3,2,1,0:T(8,128)(2,1)} %copy-done.1) | copy-start | bytes 1179652
  57.7 18.5 %collective-permute-start.11 = (f32[2,6,256]{2,1,0:T(8,128)S(1)}, f32[2,6,256]{2,1,0:T(8,128)S(1)}, u32[]{:S(2)}, u32[]{:S(2)}) collective-permute-start(f32[2,6,256]{2,1,0:T(8,128)S(1)} %late.1.refs_9_), channel_id=1, source_target_pairs={{8,0},{12,4},{16,8},{20,12},{24,16},{28,20},{9,1},{13,5},{17,9},{2... | collective-permute-start | bytes 36872 | tf_op jit(solution)/shard_map/ppermute | solution.py:35
  59.1 17.1 %collective-permute-start.12 = (f32[2,6,256]{2,1,0:T(8,128)S(1)}, f32[2,6,256]{2,1,0:T(8,128)S(1)}, u32[]{:S(2)}, u32[]{:S(2)}) collective-permute-start(f32[2,6,256]{2,1,0:T(8,128)S(1)} %late.1.refs_9_), channel_id=1, source_target_pairs={{16,0},{20,4},{24,8},{28,12},{17,1},{21,5},{25,9},{29,13},{18,2},{... | collective-permute-start | bytes 36872 | tf_op jit(solution)/shard_map/ppermute | solution.py:35
  66.3 9.9 %collective-permute-start.17 = (f32[8,128]{1,0:T(8,128)S(1)}, f32[8,128]{1,0:T(8,128)S(1)}, u32[]{:S(2)}, u32[]{:S(2)}) collective-permute-start(f32[8,128]{1,0:T(8,128)S(1)} %get-tuple-element.54), channel_id=1, source_target_pairs={{0,4},{4,0},{8,12},{12,8},{16,20},{20,16},{24,28},{28,24},{1,5},{5... | collective-permute-start | bytes 12296 | tf_op jit(solution)/shard_map/ppermute | solution.py:40
  81.4 12.5 %all-to-all-start.1 = ((f32[4,8,128]{2,1,0:T(8,128)}), f32[4,8,128]{2,1,0:T(8,128)S(1)}, u32[]{:S(2)}, u32[]{:S(2)}) async-start(f32[4,8,128]{2,1,0:T(8,128)} %broadcast_in_dim.2), calls=%async_computation.1 | async-start | bytes 32768 | tf_op jit(solution)/shard_map/all_to_all | solution.py:548
  88.3 13.6 %collective-permute-start.6 = (bf16[3,256,128]{2,1,0:T(8,128)(2,1)S(1)}, bf16[3,256,128]{2,1,0:T(8,128)(2,1)S(1)}, u32[]{:S(2)}, u32[]{:S(2)}) collective-permute-start(bf16[3,256,128]{2,1,0:T(8,128)(2,1)S(1)} %get-tuple-element.33), channel_id=1, source_target_pairs={{0,4},{4,0},{8,12},{12,8},{16,20},{20,16},{24,28},{28,24},{1,5},{5... | collective-permute-start | bytes 589832 | tf_op jit(solution)/shard_map/ppermute | solution.py:40
  89.0 13.8 %collective-permute-start.13 = (bf16[2,3,256,128]{3,2,1,0:T(8,128)(2,1)S(1)}, bf16[2,3,256,128]{3,2,1,0:T(8,128)(2,1)S(1)}, u32[]{:S(2)}, u32[]{:S(2)}) collective-permute-start(bf16[2,3,256,128]{3,2,1,0:T(8,128)(2,1)S(1)} %get-tuple-element.38), channel_id=1, source_target_pairs={{0,4},{4,0},{8,12},{12,8},{16,20},{20,16},{24,28},{28,24},{1,5},{5... | collective-permute-start | bytes 1179656 | tf_op jit(solution)/shard_map/ppermute | solution.py:40
  93.9 7.4 %all-to-all-start = ((bf16[4,64,128]{2,1,0:T(8,128)(2,1)}), bf16[4,64,128]{2,1,0:T(8,128)(2,1)S(1)}, u32[]{:S(2)}, u32[]{:S(2)}) async-start(bf16[4,64,128]{2,1,0:T(8,128)(2,1)} %bitcast.21), calls=%async_computation | async-start | bytes 131072 | tf_op jit(solution)/shard_map/all_to_all | solution.py:508

commit v4 on v3

--- a/solution.py
+++ b/solution.py
@@ -403,7 +403,7 @@
     gathered = rows_one[...].T - dt * direct
     beyond = jnp.sum(dt * late, axis=0, keepdims=True) + jnp.exp(last) * whole
     grad_log = dot(seen.astype(F32), gathered, NN, EXACT) + beyond
-    steps_ref[...] = (direct + rates * grad_log)[:, :heads]
+    steps_ref[...] = (direct + rates * grad_log).T[:heads]
     sums_ref[...] = jnp.zeros_like(sums_ref)
     sums_ref[0:1] = jnp.sum(dt * grad_log, axis=0, keepdims=True)
     sums_ref[1:2] = skip_sum
@@ -490,7 +490,7 @@
     du, grad_steps, gbc, sums = call(
         scan_body,
         [
-            shape((sets, tokens, width), BF16), shape((tokens, sets), F32),
+            shape((sets, tokens, width), BF16), shape((sets, tokens), F32),
             shape((tokens, 2 * NSTATE), BF16), shape((8, 128), F32),
         ],
         [
@@ -505,6 +505,7 @@
         smem=2, name="scan",
     )
     grad_inputs = jnp.transpose(du, (1, 0, 2))
+    grad_steps = grad_steps.T
     gbc = lax.all_to_all(gbc, "head", 0, 0, tiled=True)
     grad_bc = jnp.sum(
         gbc.reshape(lax.axis_size("head"), -1, 2 * NSTATE).astype(F32), axis=0

time: 104 us -> 105 us (level)
    unnamed x32 -> x31, local copies, waits for them, and re-layouts: 3.24 us -> 2.55 us
  transfers between devices with their start and end apart: 20 -> 20, of which waited for: 6 -> 6; matrix products, arithmetic and copies ran while one was open for 4% -> 3% of each run, Pallas kernels for 20% -> 21%
where the time goes in v4:
time: 105 us; the launch traced here: 104 us
  starting transfers between devices  49.3 us (47%)
  Pallas kernels  25.9 us (25%)
  waiting for transfers between devices  19.1 us (18%)
  other arithmetic  4.74 us (5%)
  local copies, waits for them, and re-layouts  3.68 us (4%)
  between operations  1.09 us (1%)
    ppermute x13, starting transfers between devices, moved(): return lax.ppermute(value, 'seq', pairs)  30.7 us
    pallas_call x9, Pallas kernels, call(): pl.pallas_call(body, out_shape=outs, in_specs=specs, out_specs=vmem(len(o...  25.9 us
    ppermute x5, starting transfers between devices, swapped(): return lax.ppermute(value, 'seq', [(at, at ^ 1) for at in range(count)])  8.35 us
    ppermute x13, waiting for transfers between devices, moved(): return lax.ppermute(value, 'seq', pairs)  8.1 us
    all_to_all x1, starting transfers between devices, shards(): lax.all_to_all(spread, 'seq', 0, 0, axis_index_groups=lines, tiled=True)  6.89 us
    ppermute x5, waiting for transfers between devices, swapped(): return lax.ppermute(value, 'seq', [(at, at ^ 1) for at in range(count)])  3.9 us
    all_to_all x1, waiting for transfers between devices, shards(): lax.all_to_all(spread, 'seq', 0, 0, axis_index_groups=lines, tiled=True)  3.59 us
    all_to_all x1, waiting for transfers between devices, shards(): gbc = lax.all_to_all(gbc, 'head', 0, 0, tiled=True)  3.55 us
  transfers between devices with their start and end apart: 20, of which 6 were waited for; matrix products, arithmetic and copies ran while one was open for 3% of the time, Pallas kernels for 21%

profile of v4, /device:TPU:0, one launch (start us, length us, event | category | flops | bytes accessed | tf_op | source)
XLA Modules:
  0.0 103.8 jit_solution(14350358349244651372)
XLA Ops:
  0.7 0.0 copy-start.4
  0.7 1.4 %fusion.5 = (bf16[2,3,256,128]{3,2,1,0:T(8,128)(2,1)S(1)}, bf16[2,3,256,128]{3,2,1,0:T(8,128)(2,1)S(1)}) fusion(s32[]{:T(128)S(6)} %select_n.65, bf16[1,256,6,128]{3,1,2,0:T(8,128)(2,1)} %bitcast.42, bf16[1,256,6,128]{3,1,2,0:T(8,128)(2,1)} %bitcast.43, s32[]{:T(128)S(6)} %select_n.64), kind=kLoop, calls=%fused_computation.13 | loop fusion | flops 393216 | bytes 1572872 | tf_op jit(solution)/shard_map/dynamic_slice | solution.py:444
  2.1 3.0 %collective-permute-start.2 = (bf16[2,3,256,128]{3,2,1,0:T(8,128)(2,1)S(1)}, bf16[2,3,256,128]{3,2,1,0:T(8,128)(2,1)}, u32[]{:S(2)}, u32[]{:S(2)}) collective-permute-start(bf16[2,3,256,128]{3,2,1,0:T(8,128)(2,1)S(1)} %get-tuple-element.62), channel_id=1, source_target_pairs={{0,4},{4,0},{8,12},{12,8},{16,20},{20,16},{24,28},{28,24},{1,5},{5... | collective-permute-start | bytes 1179656 | tf_op jit(solution)/shard_map/ppermute | solution.py:40
  5.1 0.8 fusion.1
  5.9 0.0 collective-permute-start.5
  6.0 4.0 %collective-permute-start = (bf16[2,3,256,128]{3,2,1,0:T(8,128)(2,1)S(1)}, bf16[2,3,256,128]{3,2,1,0:T(8,128)(2,1)S(1)}, u32[]{:S(2)}, u32[]{:S(2)}) collective-permute-start(bf16[2,3,256,128]{3,2,1,0:T(8,128)(2,1)S(1)} %get-tuple-element.63.refs_3_.refs_5_.refs_1_), channel_id=1, source_target_pairs={{0,8},{4,12},{8,16},{12,20},{16,24},{20,28},{1,9},{5,13},{9,17},{1... | collective-permute-start | bytes 1179656 | tf_op jit(solution)/shard_map/ppermute | solution.py:35
  10.0 1.3 %collective-permute-start.7 = (bf16[2,3,256,128]{3,2,1,0:T(8,128)(2,1)S(1)}, bf16[2,3,256,128]{3,2,1,0:T(8,128)(2,1)}, u32[]{:S(2)}, u32[]{:S(2)}) collective-permute-start(bf16[2,3,256,128]{3,2,1,0:T(8,128)(2,1)S(1)} %get-tuple-element.61.refs_5_.refs_3_.refs_7_), channel_id=1, source_target_pairs={{8,0},{12,4},{16,8},{20,12},{24,16},{28,20},{9,1},{13,5},{17,9},{2... | collective-permute-start | bytes 1179656 | tf_op jit(solution)/shard_map/ppermute | solution.py:35
  11.3 3.9 %collective-permute-done.2.refs_4_.refs_6_.refs_2_ = bf16[2,3,256,128]{3,2,1,0:T(8,128)(2,1)} collective-permute-done((bf16[2,3,256,128]{3,2,1,0:T(8,128)(2,1)S(1)}, bf16[2,3,256,128]{3,2,1,0:T(8,128)(2,1)}, u32[]{:S(2)}, u32[]{:S(2)}) %collective-permute-start.2) | collective-permute-done | bytes 393248 | tf_op jit(solution)/shard_map/ppermute | solution.py:40
  15.2 4.8 %collective-permute-start.3 = (bf16[2,3,256,128]{3,2,1,0:T(8,128)(2,1)}, bf16[2,3,256,128]{3,2,1,0:T(8,128)(2,1)}, u32[]{:S(2)}, u32[]{:S(2)}) collective-permute-start(bf16[2,3,256,128]{3,2,1,0:T(8,128)(2,1)} %collective-permute-done.2.refs_4_.refs_6_.refs_2_), channel_id=1, source_target_pairs={{0,8},{4,12},{8,16},{12,20},{16,24},{20,28},{1,9},{5,13},{9,17},{1... | collective-permute-start | bytes 1179656 | tf_op jit(solution)/shard_map/ppermute | solution.py:35
  20.0 0.1 copy.22.dt_ref
  20.1 2.2 %summary.1 = (f32[784,128]{1,0:T(8,128)S(1)}, bf16[784,128]{1,0:T(8,128)(2,1)S(1)}, f32[256,128]{1,0:T(8,128)S(1)}, f32[16,256]{1,0:T(8,128)S(1)}) custom-call(f32[12]{0:T(128)S(1)} %copy-done.6, bf16[12,256,128]{2,1,0:T(8,128)(2,1)S(1)} %bitcast.38, f32[256,12]{1,0:T(8,128)S(1)} %copy.22.dt_ref, bf16[256,128]{1,0:T(8,128)(2,1)S(1)} %copy-done.4), custom_call_target="tpu_custom_call" | custom-call | flops 100663296 | bytes 1613872 | tf_op jit(solution)/shard_map/summary/pallas_call | solution.py:54
  22.3 0.0 copy-start.9
  22.3 0.6 copy-done.9
  23.0 1.3 %collective-permute-start.14 = (bf16[784,128]{1,0:T(8,128)(2,1)S(1)}, bf16[784,128]{1,0:T(8,128)(2,1)S(1)}, u32[]{:S(2)}, u32[]{:S(2)}) collective-permute-start(bf16[784,128]{1,0:T(8,128)(2,1)S(1)} %get-tuple-element.42), channel_id=1, source_target_pairs={{4,0},{8,4},{12,8},{16,12},{20,16},{24,20},{28,24},{5,1},{9,5},{13... | collective-permute-start | bytes 602120 | tf_op jit(solution)/shard_map/ppermute | solution.py:35
  24.3 0.0 collective-permute-done.5.refs_6_.refs_4_.refs_8_
  24.3 1.3 %collective-permute-start.8 = (bf16[2,3,256,128]{3,2,1,0:T(8,128)(2,1)S(1)}, bf16[2,3,256,128]{3,2,1,0:T(8,128)(2,1)}, u32[]{:S(2)}, u32[]{:S(2)}) collective-permute-start(bf16[2,3,256,128]{3,2,1,0:T(8,128)(2,1)S(1)} %collective-permute-done.5.refs_6_.refs_4_.refs_8_), channel_id=1, source_target_pairs={{8,0},{12,4},{16,8},{20,12},{24,16},{28,20},{9,1},{13,5},{17,9},{2... | collective-permute-start | bytes 1179656 | tf_op jit(solution)/shard_map/ppermute | solution.py:35
  25.6 0.0 copy-start.1
  25.6 0.0 collective-permute-done.7.refs_3_
  25.6 0.7 copy-done.1
  26.3 4.2 %collective-permute-done.14.refs_0_ = bf16[784,128]{1,0:T(8,128)(2,1)S(1)} collective-permute-done((bf16[784,128]{1,0:T(8,128)(2,1)S(1)}, bf16[784,128]{1,0:T(8,128)(2,1)S(1)}, u32[]{:S(2)}, u32[]{:S(2)}) %collective-permute-start.14) | collective-permute-done | bytes 200736 | tf_op jit(solution)/shard_map/ppermute | solution.py:35
  30.6 0.8 join.3
  31.3 1.3 %collective-permute-start.15 = (bf16[784,128]{1,0:T(8,128)(2,1)}, bf16[784,128]{1,0:T(8,128)(2,1)S(1)}, u32[]{:S(2)}, u32[]{:S(2)}) collective-permute-start(bf16[784,128]{1,0:T(8,128)(2,1)} %get-tuple-element.44), channel_id=1, source_target_pairs={{8,0},{12,4},{16,8},{20,12},{24,16},{28,20},{9,1},{13,5},{17,9},{2... | collective-permute-start | bytes 602120 | tf_op jit(solution)/shard_map/ppermute | solution.py:35
  32.6 5.2 %collective-permute-start.1 = (bf16[2,3,256,128]{3,2,1,0:T(8,128)(2,1)}, bf16[2,3,256,128]{3,2,1,0:T(8,128)(2,1)S(1)}, u32[]{:S(2)}, u32[]{:S(2)}) collective-permute-start(bf16[2,3,256,128]{3,2,1,0:T(8,128)(2,1)} %copy-done.1), channel_id=1, source_target_pairs={{0,8},{4,12},{8,16},{12,20},{16,24},{20,28},{1,9},{5,13},{9,17},{1... | collective-permute-start | bytes 1179656 | tf_op jit(solution)/shard_map/ppermute | solution.py:35
  37.9 0.0 collective-permute-done.3.refs_2_.refs_4_
  37.9 4.6 %collective-permute-start.4 = (bf16[2,3,256,128]{3,2,1,0:T(8,128)(2,1)}, bf16[2,3,256,128]{3,2,1,0:T(8,128)(2,1)}, u32[]{:S(2)}, u32[]{:S(2)}) collective-permute-start(bf16[2,3,256,128]{3,2,1,0:T(8,128)(2,1)} %collective-permute-done.3.refs_2_.refs_4_), channel_id=1, source_target_pairs={{0,8},{4,12},{8,16},{12,20},{16,24},{20,28},{1,9},{5,13},{9,17},{1... | collective-permute-start | bytes 1179656 | tf_op jit(solution)/shard_map/ppermute | solution.py:35
  42.5 0.1 pad_add_fusion.refs_0_
  42.6 0.3 collective-permute-done.15.refs_1_
  43.0 0.1 join.4
  43.1 1.3 %collective-permute-start.16 = (bf16[784,128]{1,0:T(8,128)(2,1)S(1)}, bf16[784,128]{1,0:T(8,128)(2,1)S(1)}, u32[]{:S(2)}, u32[]{:S(2)}) collective-permute-start(bf16[784,128]{1,0:T(8,128)(2,1)S(1)} %get-tuple-element.46), channel_id=1, source_target_pairs={{16,0},{20,4},{24,8},{28,12},{17,1},{21,5},{25,9},{29,13},{18,2},{... | collective-permute-start | bytes 602120 | tf_op jit(solution)/shard_map/ppermute | solution.py:35
  44.4 0.0 copy-start.2
  44.4 1.0 copy-done.2
  45.4 3.2 %early.1.refs_5_ = f32[3,6,256]{2,1,0:T(8,128)S(1)} custom-call(s32[2]{0:T(128)S(1)} %pad_add_fusion.refs_0_, bf16[2,3,256,128]{3,2,1,0:T(8,128)(2,1)S(1)} %copy-done.2, bf16[2,3,256,128]{3,2,1,0:T(8,128)(2,1)} %collective-permute-done.3.refs_2_.refs_4_, bf16[2,3,256,128]{3,2,1,0:T(8,128)(2,1)S(1)} %get-tuple-element.63.refs_3_.refs_5_.refs_1_, ...), custom_call_target="tpu_custom_call" | custom-call | flops 603979776 | bytes 2377736 | tf_op jit(solution)/shard_map/early/pallas_call | solution.py:54
  48.6 0.0 copy-start.5
  48.6 0.0 copy-start.7
  48.6 0.0 copy-start.8
  48.6 0.0 copy-start.10
  48.6 0.0 copy-start.11
  48.6 1.4 %collective-permute-start.9 = (bf16[2,3,256,128]{3,2,1,0:T(8,128)(2,1)}, bf16[2,3,256,128]{3,2,1,0:T(8,128)(2,1)S(1)}, u32[]{:S(2)}, u32[]{:S(2)}) collective-permute-start(bf16[2,3,256,128]{3,2,1,0:T(8,128)(2,1)} %collective-permute-done.7.refs_3_), channel_id=1, source_target_pairs={{8,0},{12,4},{16,8},{20,12},{24,16},{28,20},{9,1},{13,5},{17,9},{2... | collective-permute-start | bytes 1179656 | tf_op jit(solution)/shard_map/ppermute | solution.py:35
  50.1 1.3 %collective-permute-start.10 = (bf16[2,3,256,128]{3,2,1,0:T(8,128)(2,1)}, bf16[2,3,256,128]{3,2,1,0:T(8,128)(2,1)S(1)}, u32[]{:S(2)}, u32[]{:S(2)}) collective-permute-start(bf16[2,3,256,128]{3,2,1,0:T(8,128)(2,1)} %collective-permute-done.8.refs_4_), channel_id=1, source_target_pairs={{8,0},{12,4},{16,8},{20,12},{24,16},{28,20},{9,1},{13,5},{17,9},{2... | collective-permute-start | bytes 1179656 | tf_op jit(solution)/shard_map/ppermute | solution.py:35
  51.4 3.5 %collective-permute-done.16.refs_1_ = bf16[784,128]{1,0:T(8,128)(2,1)S(1)} collective-permute-done((bf16[784,128]{1,0:T(8,128)(2,1)S(1)}, bf16[784,128]{1,0:T(8,128)(2,1)S(1)}, u32[]{:S(2)}, u32[]{:S(2)}) %collective-permute-start.16) | collective-permute-done | bytes 200736 | tf_op jit(solution)/shard_map/ppermute | solution.py:35
  54.8 0.8 join.5
  55.6 0.0 collective-permute-done.1.refs_1_
  55.6 0.0 collective-permute-done.4.refs_2_
  55.6 2.1 %late.1.refs_9_ = f32[2,6,256]{2,1,0:T(8,128)S(1)} custom-call(s32[2]{0:T(128)S(1)} %pad_add_fusion.refs_0_, bf16[2,3,256,128]{3,2,1,0:T(8,128)(2,1)S(1)} %collective-permute-done.1.refs_1_, bf16[2,3,256,128]{3,2,1,0:T(8,128)(2,1)} %collective-permute-done.4.refs_2_, bf16[2,3,256,128]{3,2,1,0:T(8,128)(2,1)S(1)} %get-tuple-element.61.refs_5_.refs_3_.refs_7_, ...), custom_call_target="tpu_custom_call" | custom-call | flops 301989888 | bytes 1603592 | tf_op jit(solution)/shard_map/late/pallas_call | solution.py:54
  57.7 0.0 copy-start.3
  57.7 1.4 %collective-permute-start.11 = (f32[2,6,256]{2,1,0:T(8,128)S(1)}, f32[2,6,256]{2,1,0:T(8,128)S(1)}, u32[]{:S(2)}, u32[]{:S(2)}) collective-permute-start(f32[2,6,256]{2,1,0:T(8,128)S(1)} %late.1.refs_9_), channel_id=1, source_target_pairs={{8,0},{12,4},{16,8},{20,12},{24,16},{28,20},{9,1},{13,5},{17,9},{2... | collective-permute-start | bytes 36872 | tf_op jit(solution)/shard_map/ppermute | solution.py:35
  59.1 1.5 %collective-permute-start.12 = (f32[2,6,256]{2,1,0:T(8,128)S(1)}, f32[2,6,256]{2,1,0:T(8,128)S(1)}, u32[]{:S(2)}, u32[]{:S(2)}) collective-permute-start(f32[2,6,256]{2,1,0:T(8,128)S(1)} %late.1.refs_9_), channel_id=1, source_target_pairs={{16,0},{20,4},{24,8},{28,12},{17,1},{21,5},{25,9},{29,13},{18,2},{... | collective-permute-start | bytes 36872 | tf_op jit(solution)/shard_map/ppermute | solution.py:35
  60.7 5.7 %scan.1 = (bf16[12,256,128]{2,1,0:T(8,128)(2,1)}, f32[12,256]{1,0:T(8,128)}, bf16[256,128]{1,0:T(8,128)(2,1)}, f32[8,128]{1,0:T(8,128)S(1)}) custom-call(f32[12]{0:T(128)S(1)} %copy-done.6, f32[12]{0:T(128)S(1)} %copy-done.11, bf16[12,256,128]{2,1,0:T(8,128)(2,1)S(1)} %bitcast.40, bf16[12,256,128]{2,1,0:T(8,128)(2,1)S(1)} %bitcast.39, ...), custom_call_target="tpu_custom_call" | custom-call | flops 805306368 | bytes 3461216 | tf_op jit(solution)/shard_map/scan/pallas_call | solution.py:54
  66.3 3.3 %collective-permute-start.17 = (f32[8,128]{1,0:T(8,128)S(1)}, f32[8,128]{1,0:T(8,128)S(1)}, u32[]{:S(2)}, u32[]{:S(2)}) collective-permute-start(f32[8,128]{1,0:T(8,128)S(1)} %get-tuple-element.54), channel_id=1, source_target_pairs={{0,4},{4,0},{8,12},{12,8},{16,20},{20,16},{24,28},{28,24},{1,5},{5... | collective-permute-start | bytes 12296 | tf_op jit(solution)/shard_map/ppermute | solution.py:40
  69.6 6.6 %query.1 = (bf16[3,256,128]{2,1,0:T(8,128)(2,1)S(1)}, bf16[3,256,128]{2,1,0:T(8,128)(2,1)S(1)}, f32[2,2,3,256,128]{4,3,2,1,0:T(8,128)S(1)}) custom-call(s32[2]{0:T(128)S(1)} %pad_add_fusion.refs_0_, bf16[2,3,256,128]{3,2,1,0:T(8,128)(2,1)S(1)} %collective-permute-done.1.refs_1_, bf16[2,3,256,128]{3,2,1,0:T(8,128)(2,1)} %collective-permute-done.4.refs_2_, ...), custom_call_target="tpu_custom_call" | custom-call | flops 1509949440 | bytes 5124104 | tf_op jit(solution)/shard_map/query/pallas_call | solution.py:54
  76.2 0.0 collective-permute-done.9.refs_5_
  76.3 4.6 %later.1 = (bf16[2,3,256,128]{3,2,1,0:T(8,128)(2,1)S(1)}, bf16[2,3,256,128]{3,2,1,0:T(8,128)(2,1)S(1)}) custom-call(s32[2]{0:T(128)S(1)} %pad_add_fusion.refs_0_, bf16[2,3,256,128]{3,2,1,0:T(8,128)(2,1)S(1)} %get-tuple-element.63.refs_3_.refs_5_.refs_1_, bf16[2,3,256,128]{3,2,1,0:T(8,128)(2,1)} %collective-permute-done.2.refs_4_.refs_6_.refs_2_, ...), custom_call_target="tpu_custom_call" | custom-call | flops 1610612736 | bytes 4743176 | tf_op jit(solution)/shard_map/later/pallas_call | solution.py:54
  80.9 0.6 broadcast_in_dim.2
  81.5 6.9 %all-to-all-start.1 = ((f32[4,8,128]{2,1,0:T(8,128)}), f32[4,8,128]{2,1,0:T(8,128)S(1)}, u32[]{:S(2)}, u32[]{:S(2)}) async-start(f32[4,8,128]{2,1,0:T(8,128)} %broadcast_in_dim.2), calls=%async_computation.1 | async-start | bytes 32768 | tf_op jit(solution)/shard_map/all_to_all | solution.py:549
  88.4 0.0 collective-permute-start.6
  88.4 2.0 %collective-permute-start.13 = (bf16[2,3,256,128]{3,2,1,0:T(8,128)(2,1)S(1)}, bf16[2,3,256,128]{3,2,1,0:T(8,128)(2,1)S(1)}, u32[]{:S(2)}, u32[]{:S(2)}) collective-permute-start(bf16[2,3,256,128]{3,2,1,0:T(8,128)(2,1)S(1)} %get-tuple-element.38), channel_id=1, source_target_pairs={{0,4},{4,0},{8,12},{12,8},{16,20},{20,16},{24,28},{28,24},{1,5},{5... | collective-permute-start | bytes 1179656 | tf_op jit(solution)/shard_map/ppermute | solution.py:40
  90.4 3.6 %all-to-all-done.1 = f32[4,8,128]{2,1,0:T(8,128)S(1)} async-done(((f32[4,8,128]{2,1,0:T(8,128)}), f32[4,8,128]{2,1,0:T(8,128)S(1)}, u32[]{:S(2)}, u32[]{:S(2)}) %all-to-all-start.1) | async-done | bytes 16416 | tf_op jit(solution)/shard_map/all_to_all | solution.py:549
  94.0 3.3 %all-to-all-start = ((bf16[4,64,128]{2,1,0:T(8,128)(2,1)}), bf16[4,64,128]{2,1,0:T(8,128)(2,1)S(1)}, u32[]{:S(2)}, u32[]{:S(2)}) async-start(bf16[4,64,128]{2,1,0:T(8,128)(2,1)} %bitcast.22), calls=%async_computation | async-start | bytes 131072 | tf_op jit(solution)/shard_map/all_to_all | solution.py:509
  97.3 0.5 slice_bitcast_fusion
  97.8 3.6 %all-to-all-done = bf16[4,64,128]{2,1,0:T(8,128)(2,1)S(1)} async-done(((bf16[4,64,128]{2,1,0:T(8,128)(2,1)}), bf16[4,64,128]{2,1,0:T(8,128)(2,1)S(1)}, u32[]{:S(2)}, u32[]{:S(2)}) %all-to-all-start) | async-done | bytes 65568 | tf_op jit(solution)/shard_map/all_to_all | solution.py:509
  101.3 0.6 convert_reduce_fusion
  102.0 0.8 maximum_bitcast_fusion
  102.8 0.1 select_bitcast_fusion.1
  102.9 0.9 maximum_bitcast_fusion.1
  (28 shorter events, 0.1 us)
Async XLA Ops:
  0.6 4.5 %copy-start.12 = (bf16[256,6,128]{2,0,1:T(8,128)(2,1)S(1)}, bf16[256,6,128]{2,0,1:T(8,128)(2,1)}, u32[]{:S(2)}) copy-start(bf16[256,6,128]{2,0,1:T(8,128)(2,1)} %param.11) | copy-start | bytes 1179652
  0.6 4.5 %copy-start.13 = (bf16[256,6,128]{2,0,1:T(8,128)(2,1)S(1)}, bf16[256,6,128]{2,0,1:T(8,128)(2,1)}, u32[]{:S(2)}) copy-start(bf16[256,6,128]{2,0,1:T(8,128)(2,1)} %param.14) | copy-start | bytes 1179652
  0.7 19.3 %copy-start.14 = (f32[256,12]{0,1:T(8,128)S(1)}, f32[256,12]{0,1:T(8,128)}, u32[]{:S(2)}) copy-start(f32[256,12]{0,1:T(8,128)} %param.17) | copy-start | bytes 36868
  0.7 19.4 %copy-start = (bf16[256,12,128]{2,0,1:T(8,128)(2,1)S(1)}, bf16[256,12,128]{2,0,1:T(8,128)(2,1)}, u32[]{:S(2)}) copy-start(bf16[256,12,128]{2,0,1:T(8,128)(2,1)} %param.16) | copy-start | bytes 2359300
  0.7 19.4 %copy-start.4 = (bf16[256,128]{1,0:T(8,128)(2,1)S(1)}, bf16[256,128]{1,0:T(8,128)(2,1)}, u32[]{:S(2)}) copy-start(bf16[256,128]{1,0:T(8,128)(2,1)} %bc_ref.3) | copy-start | bytes 196612
  0.7 19.4 %copy-start.6 = (f32[12]{0:T(128)S(1)}, f32[12]{0:T(128)}, u32[]{:S(2)}) copy-start(f32[12]{0:T(128)} %rates_ref.3) | copy-start | bytes 148
  2.1 13.1 %collective-permute-start.2 = (bf16[2,3,256,128]{3,2,1,0:T(8,128)(2,1)S(1)}, bf16[2,3,256,128]{3,2,1,0:T(8,128)(2,1)}, u32[]{:S(2)}, u32[]{:S(2)}) collective-permute-start(bf16[2,3,256,128]{3,2,1,0:T(8,128)(2,1)S(1)} %get-tuple-element.62), channel_id=1, source_target_pairs={{0,4},{4,0},{8,12},{12,8},{16,20},{20,16},{24,28},{28,24},{1,5},{5... | collective-permute-start | bytes 1179656 | tf_op jit(solution)/shard_map/ppermute | solution.py:40
  5.9 18.3 %collective-permute-start.5 = (bf16[2,3,256,128]{3,2,1,0:T(8,128)(2,1)}, bf16[2,3,256,128]{3,2,1,0:T(8,128)(2,1)S(1)}, u32[]{:S(2)}, u32[]{:S(2)}) collective-permute-start(bf16[2,3,256,128]{3,2,1,0:T(8,128)(2,1)} %get-tuple-element.60), channel_id=1, source_target_pairs={{0,4},{4,0},{8,12},{12,8},{16,20},{20,16},{24,28},{28,24},{1,5},{5... | collective-permute-start | bytes 1179656 | tf_op jit(solution)/shard_map/ppermute | solution.py:40
  6.0 19.6 %collective-permute-start = (bf16[2,3,256,128]{3,2,1,0:T(8,128)(2,1)S(1)}, bf16[2,3,256,128]{3,2,1,0:T(8,128)(2,1)S(1)}, u32[]{:S(2)}, u32[]{:S(2)}) collective-permute-start(bf16[2,3,256,128]{3,2,1,0:T(8,128)(2,1)S(1)} %get-tuple-element.63.refs_3_.refs_5_.refs_1_), channel_id=1, source_target_pairs={{0,8},{4,12},{8,16},{12,20},{16,24},{20,28},{1,9},{5,13},{9,17},{1... | collective-permute-start | bytes 1179656 | tf_op jit(solution)/shard_map/ppermute | solution.py:35
  10.0 15.6 %collective-permute-start.7 = (bf16[2,3,256,128]{3,2,1,0:T(8,128)(2,1)S(1)}, bf16[2,3,256,128]{3,2,1,0:T(8,128)(2,1)}, u32[]{:S(2)}, u32[]{:S(2)}) collective-permute-start(bf16[2,3,256,128]{3,2,1,0:T(8,128)(2,1)S(1)} %get-tuple-element.61.refs_5_.refs_3_.refs_7_), channel_id=1, source_target_pairs={{8,0},{12,4},{16,8},{20,12},{24,16},{28,20},{9,1},{13,5},{17,9},{2... | collective-permute-start | bytes 1179656 | tf_op jit(solution)/shard_map/ppermute | solution.py:35
  15.2 22.7 %collective-permute-start.3 = (bf16[2,3,256,128]{3,2,1,0:T(8,128)(2,1)}, bf16[2,3,256,128]{3,2,1,0:T(8,128)(2,1)}, u32[]{:S(2)}, u32[]{:S(2)}) collective-permute-start(bf16[2,3,256,128]{3,2,1,0:T(8,128)(2,1)} %collective-permute-done.2.refs_4_.refs_6_.refs_2_), channel_id=1, source_target_pairs={{0,8},{4,12},{8,16},{12,20},{16,24},{20,28},{1,9},{5,13},{9,17},{1... | collective-permute-start | bytes 1179656 | tf_op jit(solution)/shard_map/ppermute | solution.py:35
  22.3 0.7 copy-start.9
  23.0 7.6 %collective-permute-start.14 = (bf16[784,128]{1,0:T(8,128)(2,1)S(1)}, bf16[784,128]{1,0:T(8,128)(2,1)S(1)}, u32[]{:S(2)}, u32[]{:S(2)}) collective-permute-start(bf16[784,128]{1,0:T(8,128)(2,1)S(1)} %get-tuple-element.42), channel_id=1, source_target_pairs={{4,0},{8,4},{12,8},{16,12},{20,16},{24,20},{28,24},{5,1},{9,5},{13... | collective-permute-start | bytes 602120 | tf_op jit(solution)/shard_map/ppermute | solution.py:35
  24.3 25.8 %collective-permute-start.8 = (bf16[2,3,256,128]{3,2,1,0:T(8,128)(2,1)S(1)}, bf16[2,3,256,128]{3,2,1,0:T(8,128)(2,1)}, u32[]{:S(2)}, u32[]{:S(2)}) collective-permute-start(bf16[2,3,256,128]{3,2,1,0:T(8,128)(2,1)S(1)} %collective-permute-done.5.refs_6_.refs_4_.refs_8_), channel_id=1, source_target_pairs={{8,0},{12,4},{16,8},{20,12},{24,16},{28,20},{9,1},{13,5},{17,9},{2... | collective-permute-start | bytes 1179656 | tf_op jit(solution)/shard_map/ppermute | solution.py:35
  25.6 0.7 copy-start.1
  31.3 11.6 %collective-permute-start.15 = (bf16[784,128]{1,0:T(8,128)(2,1)}, bf16[784,128]{1,0:T(8,128)(2,1)S(1)}, u32[]{:S(2)}, u32[]{:S(2)}) collective-permute-start(bf16[784,128]{1,0:T(8,128)(2,1)} %get-tuple-element.44), channel_id=1, source_target_pairs={{8,0},{12,4},{16,8},{20,12},{24,16},{28,20},{9,1},{13,5},{17,9},{2... | collective-permute-start | bytes 602120 | tf_op jit(solution)/shard_map/ppermute | solution.py:35
  32.6 23.0 %collective-permute-start.1 = (bf16[2,3,256,128]{3,2,1,0:T(8,128)(2,1)}, bf16[2,3,256,128]{3,2,1,0:T(8,128)(2,1)S(1)}, u32[]{:S(2)}, u32[]{:S(2)}) collective-permute-start(bf16[2,3,256,128]{3,2,1,0:T(8,128)(2,1)} %copy-done.1), channel_id=1, source_target_pairs={{0,8},{4,12},{8,16},{12,20},{16,24},{20,28},{1,9},{5,13},{9,17},{1... | collective-permute-start | bytes 1179656 | tf_op jit(solution)/shard_map/ppermute | solution.py:35
  37.9 17.7 %collective-permute-start.4 = (bf16[2,3,256,128]{3,2,1,0:T(8,128)(2,1)}, bf16[2,3,256,128]{3,2,1,0:T(8,128)(2,1)}, u32[]{:S(2)}, u32[]{:S(2)}) collective-permute-start(bf16[2,3,256,128]{3,2,1,0:T(8,128)(2,1)} %collective-permute-done.3.refs_2_.refs_4_), channel_id=1, source_target_pairs={{0,8},{4,12},{8,16},{12,20},{16,24},{20,28},{1,9},{5,13},{9,17},{1... | collective-permute-start | bytes 1179656 | tf_op jit(solution)/shard_map/ppermute | solution.py:35
  43.1 11.8 %collective-permute-start.16 = (bf16[784,128]{1,0:T(8,128)(2,1)S(1)}, bf16[784,128]{1,0:T(8,128)(2,1)S(1)}, u32[]{:S(2)}, u32[]{:S(2)}) collective-permute-start(bf16[784,128]{1,0:T(8,128)(2,1)S(1)} %get-tuple-element.46), channel_id=1, source_target_pairs={{16,0},{20,4},{24,8},{28,12},{17,1},{21,5},{25,9},{29,13},{18,2},{... | collective-permute-start | bytes 602120 | tf_op jit(solution)/shard_map/ppermute | solution.py:35
  44.4 1.0 copy-start.2
  48.6 12.1 %copy-start.5 = (bf16[256,128]{1,0:T(8,128)(2,1)S(1)}, bf16[256,128]{1,0:T(8,128)(2,1)}, u32[]{:S(2)}) copy-start(bf16[256,128]{1,0:T(8,128)(2,1)} %bc_ref.3) | copy-start | bytes 196612
  48.6 12.1 %copy-start.7 = (bf16[256,12,128]{2,0,1:T(8,128)(2,1)S(1)}, bf16[256,12,128]{2,0,1:T(8,128)(2,1)}, u32[]{:S(2)}) copy-start(bf16[256,12,128]{2,0,1:T(8,128)(2,1)} %param.15) | copy-start | bytes 2359300
  48.6 12.1 %copy-start.8 = (f32[1,12,64,128]{3,2,1,0:T(8,128)S(1)}, f32[1,12,64,128]{3,2,1,0:T(8,128)}, u32[]{:S(2)}) copy-start(f32[1,12,64,128]{3,2,1,0:T(8,128)} %param.21) | copy-start | bytes 1179652
  48.6 12.0 %copy-start.10 = (f32[256,128]{1,0:T(8,128)S(1)}, f32[256,128]{1,0:T(8,128)}, u32[]{:S(2)}) copy-start(f32[256,128]{1,0:T(8,128)} %copy-done.9) | copy-start | bytes 393220
  48.6 12.0 %copy-start.11 = (f32[12]{0:T(128)S(1)}, f32[12]{0:T(128)}, u32[]{:S(2)}) copy-start(f32[12]{0:T(128)} %skips_ref.1) | copy-start | bytes 148
  48.6 27.6 %collective-permute-start.9 = (bf16[2,3,256,128]{3,2,1,0:T(8,128)(2,1)}, bf16[2,3,256,128]{3,2,1,0:T(8,128)(2,1)S(1)}, u32[]{:S(2)}, u32[]{:S(2)}) collective-permute-start(bf16[2,3,256,128]{3,2,1,0:T(8,128)(2,1)} %collective-permute-done.7.refs_3_), channel_id=1, source_target_pairs={{8,0},{12,4},{16,8},{20,12},{24,16},{28,20},{9,1},{13,5},{17,9},{2... | collective-permute-start | bytes 1179656 | tf_op jit(solution)/shard_map/ppermute | solution.py:35
  50.1 26.2 %collective-permute-start.10 = (bf16[2,3,256,128]{3,2,1,0:T(8,128)(2,1)}, bf16[2,3,256,128]{3,2,1,0:T(8,128)(2,1)S(1)}, u32[]{:S(2)}, u32[]{:S(2)}) collective-permute-start(bf16[2,3,256,128]{3,2,1,0:T(8,128)(2,1)} %collective-permute-done.8.refs_4_), channel_id=1, source_target_pairs={{8,0},{12,4},{16,8},{20,12},{24,16},{28,20},{9,1},{13,5},{17,9},{2... | collective-permute-start | bytes 1179656 | tf_op jit(solution)/shard_map/ppermute | solution.py:35
  57.7 11.9 %copy-start.3 = (bf16[2,3,256,128]{3,2,1,0:T(8,128)(2,1)S(1)}, bf16[2,3,256,128]{3,2,1,0:T(8,128)(2,1)}, u32[]{:S(2)}) copy-start(bf16[2,3,256,128]{3,2,1,0:T(8,128)(2,1)} %copy-done.1) | copy-start | bytes 1179652
  57.7 18.5 %collective-permute-start.11 = (f32[2,6,256]{2,1,0:T(8,128)S(1)}, f32[2,6,256]{2,1,0:T(8,128)S(1)}, u32[]{:S(2)}, u32[]{:S(2)}) collective-permute-start(f32[2,6,256]{2,1,0:T(8,128)S(1)} %late.1.refs_9_), channel_id=1, source_target_pairs={{8,0},{12,4},{16,8},{20,12},{24,16},{28,20},{9,1},{13,5},{17,9},{2... | collective-permute-start | bytes 36872 | tf_op jit(solution)/shard_map/ppermute | solution.py:35
  59.1 17.1 %collective-permute-start.12 = (f32[2,6,256]{2,1,0:T(8,128)S(1)}, f32[2,6,256]{2,1,0:T(8,128)S(1)}, u32[]{:S(2)}, u32[]{:S(2)}) collective-permute-start(f32[2,6,256]{2,1,0:T(8,128)S(1)} %late.1.refs_9_), channel_id=1, source_target_pairs={{16,0},{20,4},{24,8},{28,12},{17,1},{21,5},{25,9},{29,13},{18,2},{... | collective-permute-start | bytes 36872 | tf_op jit(solution)/shard_map/ppermute | solution.py:35
  66.3 9.9 %collective-permute-start.17 = (f32[8,128]{1,0:T(8,128)S(1)}, f32[8,128]{1,0:T(8,128)S(1)}, u32[]{:S(2)}, u32[]{:S(2)}) collective-permute-start(f32[8,128]{1,0:T(8,128)S(1)} %get-tuple-element.54), channel_id=1, source_target_pairs={{0,4},{4,0},{8,12},{12,8},{16,20},{20,16},{24,28},{28,24},{1,5},{5... | collective-permute-start | bytes 12296 | tf_op jit(solution)/shard_map/ppermute | solution.py:40
  81.5 12.5 %all-to-all-start.1 = ((f32[4,8,128]{2,1,0:T(8,128)}), f32[4,8,128]{2,1,0:T(8,128)S(1)}, u32[]{:S(2)}, u32[]{:S(2)}) async-start(f32[4,8,128]{2,1,0:T(8,128)} %broadcast_in_dim.2), calls=%async_computation.1 | async-start | bytes 32768 | tf_op jit(solution)/shard_map/all_to_all | solution.py:549
  88.4 13.6 %collective-permute-start.6 = (bf16[3,256,128]{2,1,0:T(8,128)(2,1)S(1)}, bf16[3,256,128]{2,1,0:T(8,128)(2,1)S(1)}, u32[]{:S(2)}, u32[]{:S(2)}) collective-permute-start(bf16[3,256,128]{2,1,0:T(8,128)(2,1)S(1)} %get-tuple-element.33), channel_id=1, source_target_pairs={{0,4},{4,0},{8,12},{12,8},{16,20},{20,16},{24,28},{28,24},{1,5},{5... | collective-permute-start | bytes 589832 | tf_op jit(solution)/shard_map/ppermute | solution.py:40
  88.4 14.4 %collective-permute-start.13 = (bf16[2,3,256,128]{3,2,1,0:T(8,128)(2,1)S(1)}, bf16[2,3,256,128]{3,2,1,0:T(8,128)(2,1)S(1)}, u32[]{:S(2)}, u32[]{:S(2)}) collective-permute-start(bf16[2,3,256,128]{3,2,1,0:T(8,128)(2,1)S(1)} %get-tuple-element.38), channel_id=1, source_target_pairs={{0,4},{4,0},{8,12},{12,8},{16,20},{20,16},{24,28},{28,24},{1,5},{5... | collective-permute-start | bytes 1179656 | tf_op jit(solution)/shard_map/ppermute | solution.py:40
  94.0 7.4 %all-to-all-start = ((bf16[4,64,128]{2,1,0:T(8,128)(2,1)}), bf16[4,64,128]{2,1,0:T(8,128)(2,1)S(1)}, u32[]{:S(2)}, u32[]{:S(2)}) async-start(bf16[4,64,128]{2,1,0:T(8,128)(2,1)} %bitcast.22), calls=%async_computation | async-start | bytes 131072 | tf_op jit(solution)/shard_map/all_to_all | solution.py:509
